TPU v7x, 32 devices: a whole 2x2x4 slice. The times are simulated.
32 devices in a mesh: dp: 2 (over core), seq: 16 (over z, y, x).
Axes of the slice: x: 2, y: 2, z: 4, core: 2. Of those that a mesh axis runs over, the one named last changes fastest.
Arguments:
- features: bfloat16 [2, 2048, 512], P('dp', 'seq'), may hold values from -40 to 40
- score_cotangent: float32 [2, 2048], P('dp', 'seq'), may hold values from -24 to 24
- projection_weight: bfloat16 [512, 768], replicated, may hold values from -0.25 to 0.25
- squeeze_weight: bfloat16 [64, 768], replicated, may hold values from -0.21875 to 0.21875
- first_weight: bfloat16 [320, 128], replicated, may hold values from -0.3125 to 0.3125
- second_weight: bfloat16 [640, 256], replicated, may hold values from -0.25 to 0.25
- third_weight: bfloat16 [1280, 256], replicated, may hold values from -0.15625 to 0.15625
- final_weight: bfloat16 [768], replicated, may hold values from -0.875 to 0.875
Outputs:
- scores: float32 [2, 2048], P('dp', 'seq')
- feature_grad: float32 [2, 2048, 512], P('dp', 'seq')
- squeeze_grad: float32 [64, 768], P('seq')
- first_grad: float32 [320, 128], P('seq')
- second_grad: float32 [640, 256], P('seq')
- third_grad: float32 [1280, 256], P('seq')
- final_grad: float32 [768], P('seq')
All inputs are finite; a program needn't handle non-finite values.
Results may differ from a plain program's by a relative error of at most 0.025.
Values may be sent and summed in bfloat16 or wider, within the bound.
No kernel may reach another device: no remote copies, remote signals or barrier semaphores. Data moves between devices by JAX's collectives and lax.ppermute only.
A program may use at most 64 MiB of HBM per device.

v0:
```python
import math

import jax
import jax.numpy as jnp
from jax import lax
from jax.sharding import PartitionSpec as P

C0 = 64
C1 = 128
C2 = 256
HK = 5
PK = 3


EPSILON = 1e-05
SLOPE = 0.1


def padded(block, sides, width):
    for axis, dim in sides:
        count = lax.axis_size(axis)
        forward = [(i, i + 1) for i in range(count - 1)]
        backward = [(target, source) for source, target in forward]
        low = lax.ppermute(
            lax.slice_in_dim(block, block.shape[dim] - width, None, axis=dim), axis, forward
        )
        high = lax.ppermute(lax.slice_in_dim(block, 0, width, axis=dim), axis, backward)
        block = jnp.concatenate([low, block, high], axis=dim)
    return block


def normalize(values):
    average = jnp.mean(values, axis=-1, keepdims=True)
    centred = values - average
    variance = jnp.mean(centred * centred, axis=-1, keepdims=True)
    inverse = lax.rsqrt(variance + EPSILON)
    return (centred * inverse, inverse)


def normalize_back(upstream, normed, inverse):
    first_mean = jnp.mean(upstream, axis=-1, keepdims=True)
    second_mean = jnp.mean(upstream * normed, axis=-1, keepdims=True)
    return (upstream - first_mean - normed * second_mean) * inverse


def gelu_slope(values):
    cumulative = 0.5 * (1.0 + lax.erf(values * math.sqrt(0.5)))
    density = jnp.exp(-0.5 * values * values) / math.sqrt(2.0 * math.pi)
    return cumulative + values * density


def leaky_unit(values):
    return SLOPE * values + (1.0 - SLOPE) * jax.nn.gelu(values, approximate=False)


def leaky_slope(values):
    return SLOPE + (1.0 - SLOPE) * gelu_slope(values)


def convolve(extended, weights):
    return lax.conv_general_dilated(
        extended,
        weights,
        (1,),
        "VALID",
        dimension_numbers=("NWC", "WIO", "NWC"),
        preferred_element_type=jnp.float32,
    )


def flipped_plain(weights):
    return jnp.swapaxes(weights, 1, 2)[::-1]


def tap_gradients(extended, delta):
    length = delta.shape[1]
    pieces = [
        jnp.einsum(
            "utc,ute->ce",
            extended[:, offset : offset + length],
            delta,
            preferred_element_type=jnp.float32,
        )
        for offset in range(HK)
    ]
    return jnp.concatenate(pieces, axis=0)


def shards(
    features,
    score_cotangent,
    projection_weight,
    squeeze_weight,
    first_weight,
    second_weight,
    third_weight,
    final_weight,
):
    frames = features.shape[1]
    head_pad = (HK - 1) // 2
    final_pad = (PK - 1) // 2
    normed_in, inverse_in = normalize(features.astype(jnp.float32))
    rounded_in = normed_in.astype(jnp.bfloat16)
    projected = jnp.einsum(
        "utf,fd->utd", rounded_in, projection_weight, preferred_element_type=jnp.float32
    ).astype(jnp.bfloat16)
    hidden_normed, hidden_inverse = normalize(projected.astype(jnp.float32))
    hidden = hidden_normed.astype(jnp.bfloat16)
    squeezed = jnp.einsum("utd,cd->utc", hidden, squeeze_weight, preferred_element_type=jnp.float32)
    kernel_one = first_weight.reshape(HK, C0, C1)
    kernel_two = second_weight.reshape(HK, C1, C2)
    kernel_three = third_weight.reshape(HK, C2, C2)
    first_ext = padded(leaky_unit(squeezed).astype(jnp.bfloat16), (("seq", 1),), head_pad)
    first_act = convolve(first_ext, kernel_one)
    second_ext = padded(leaky_unit(first_act).astype(jnp.bfloat16), (("seq", 1),), head_pad)
    second_act = convolve(second_ext, kernel_two)
    third_ext = padded(leaky_unit(second_act).astype(jnp.bfloat16), (("seq", 1),), head_pad)
    third_act = convolve(third_ext, kernel_three)
    final_ext = padded(leaky_unit(third_act).astype(jnp.bfloat16), (("seq", 1),), final_pad)
    scores = convolve(final_ext, final_weight.reshape(PK, C2, 1))[:, :, 0]
    cotangent_ext = padded(score_cotangent, (("seq", 1),), final_pad)
    final_taps = final_weight.astype(jnp.float32).reshape(PK, C2)
    upstream = jnp.zeros(third_act.shape, jnp.float32)
    for offset in range(PK):
        upstream = (
            upstream
            + cotangent_ext[:, offset : offset + frames, None] * final_taps[PK - 1 - offset]
        )
    final_grad = jnp.concatenate(
        [
            jnp.einsum(
                "ut,utc->c",
                score_cotangent,
                final_ext[:, offset : offset + frames].astype(jnp.float32),
                precision=lax.Precision.HIGHEST,
            )
            for offset in range(PK)
        ],
        axis=0,
    )
    delta_three = (upstream * leaky_slope(third_act)).astype(jnp.bfloat16)
    third_grad = tap_gradients(third_ext, delta_three)
    delta_three_ext = padded(delta_three, (("seq", 1),), head_pad)
    upstream = convolve(delta_three_ext, flipped_plain(kernel_three))
    delta_two = (upstream * leaky_slope(second_act)).astype(jnp.bfloat16)
    second_grad = tap_gradients(second_ext, delta_two)
    delta_two_ext = padded(delta_two, (("seq", 1),), head_pad)
    upstream = convolve(delta_two_ext, flipped_plain(kernel_two))
    delta_one = (upstream * leaky_slope(first_act)).astype(jnp.bfloat16)
    first_grad = tap_gradients(first_ext, delta_one)
    delta_one_ext = padded(delta_one, (("seq", 1),), head_pad)
    upstream = convolve(delta_one_ext, flipped_plain(kernel_one))
    delta_squeeze = (upstream * leaky_slope(squeezed)).astype(jnp.bfloat16)
    squeeze_grad = jnp.einsum(
        "utc,utd->cd", delta_squeeze, hidden, preferred_element_type=jnp.float32
    )
    hidden_upstream = jnp.einsum(
        "utc,cd->utd", delta_squeeze, squeeze_weight, preferred_element_type=jnp.float32
    )
    projected_grad = normalize_back(hidden_upstream, hidden_normed, hidden_inverse).astype(
        jnp.bfloat16
    )
    normed_grad = jnp.einsum(
        "utd,fd->utf", projected_grad, projection_weight, preferred_element_type=jnp.float32
    )
    feature_grad = normalize_back(normed_grad, normed_in, inverse_in)
    factor = 1.0 / math.sqrt(lax.axis_size("dp") * lax.axis_size("seq") * frames)
    terms = (
        squeeze_grad * factor,
        first_grad * factor,
        second_grad * factor,
        third_grad * factor,
        final_grad * factor,
    )
    partial_value = (
        lax.psum_scatter(terms[0], "seq", scatter_dimension=0, tiled=True),
        lax.psum_scatter(terms[1], "seq", scatter_dimension=0, tiled=True),
        lax.psum_scatter(terms[2], "seq", scatter_dimension=0, tiled=True),
        lax.psum_scatter(terms[3], "seq", scatter_dimension=0, tiled=True),
        lax.psum_scatter(terms[4], "seq", scatter_dimension=0, tiled=True),
    )
    shares = (
        lax.psum(partial_value[0].astype(jnp.bfloat16), "dp").astype(jnp.float32),
        lax.psum(partial_value[1].astype(jnp.bfloat16), "dp").astype(jnp.float32),
        lax.psum(partial_value[2].astype(jnp.bfloat16), "dp").astype(jnp.float32),
        lax.psum(partial_value[3].astype(jnp.bfloat16), "dp").astype(jnp.float32),
        lax.psum(partial_value[4].astype(jnp.bfloat16), "dp").astype(jnp.float32),
    )
    return (scores, feature_grad, shares[0], shares[1], shares[2], shares[3], shares[4])


def solution(mesh):
    placed = (P("dp", "seq", None), P("dp", "seq"), P(), P(), P(), P(), P(), P())
    return jax.shard_map(
        shards,
        mesh=mesh,
        in_specs=placed,
        out_specs=(
            P("dp", "seq"),
            P("dp", "seq", None),
            P("seq", None),
            P("seq", None),
            P("seq", None),
            P("seq", None),
            P("seq"),
        ),
        check_vma=False,
    )
```

profile of v0, /device:TPU:0, one launch (start us, length us, event | category | flops | bytes accessed | tf_op | source)
XLA Modules:
  0.0 259.3 jit_solution(16260300215278702386)
XLA Ops:
  7.2 1.3 fusion.319
  8.6 5.4 %collective-permute-start.8 = (f32[1,1]{1,0:T(1,128)}, f32[1,1]{1,0:T(1,128)}, u32[]{:S(2)}, u32[]{:S(2)}) collective-permute-start(f32[1,1]{1,0:T(1,128)} %get-tuple-element.38), channel_id=1, source_target_pairs={{0,1},{1,2},{2,3},{3,4},{4,5},{5,6},{6,7},{7,8},{8,9},{9,10},{10,1... | collective-permute-start | bytes 20 | tf_op jit(solution)/shard_map/ppermute | solution.py:24
  13.9 1.3 collective-permute-start.9
  15.2 1.0 convert_reduce_fusion
  16.2 1.1 fusion.14
  17.3 1.3 fusion.320
  19.0 0.3 fusion.208
  19.4 4.5 %collective-permute-start = (bf16[1,2,64]{1,2,0:T(8,128)(2,1)S(1)}, bf16[1,2,64]{1,2,0:T(8,128)(2,1)S(1)}, u32[]{:S(2)}, u32[]{:S(2)}) collective-permute-start(bf16[1,2,64]{1,2,0:T(8,128)(2,1)S(1)} %get-tuple-element.31), channel_id=1, source_target_pairs={{0,1},{1,2},{2,3},{3,4},{4,5},{5,6},{6,7},{7,8},{8,9},{9,10},{10,1... | collective-permute-start | bytes 776 | tf_op jit(solution)/shard_map/ppermute | solution.py:24
  23.9 1.3 collective-permute-start.1
  25.4 4.2 %collective-permute-done.1 = bf16[1,2,64]{1,2,0:T(8,128)(2,1)S(1)} collective-permute-done((bf16[1,2,64]{1,2,0:T(8,128)(2,1)S(1)}, bf16[1,2,64]{1,2,0:T(8,128)(2,1)S(1)}, u32[]{:S(2)}, u32[]{:S(2)}) %collective-permute-start.1) | collective-permute-done | bytes 288 | tf_op jit(solution)/shard_map/ppermute | solution.py:27
  29.9 1.0 fusion.116
  30.9 4.7 %collective-permute-start.2 = (bf16[1,2,128]{2,1,0:T(2,128)(2,1)S(1)}, bf16[1,2,128]{2,1,0:T(2,128)(2,1)S(1)}, u32[]{:S(2)}, u32[]{:S(2)}) collective-permute-start(bf16[1,2,128]{2,1,0:T(2,128)(2,1)S(1)} %get-tuple-element.29), channel_id=1, source_target_pairs={{0,1},{1,2},{2,3},{3,4},{4,5},{5,6},{6,7},{7,8},{8,9},{9,10},{10,1... | collective-permute-start | bytes 1544 | tf_op jit(solution)/shard_map/ppermute | solution.py:24
  35.6 1.3 collective-permute-start.3
  36.9 0.6 dynamic-slice
  39.5 1.6 collective-permute-done.3
  41.2 1.1 fusion.34
  42.4 4.7 %collective-permute-start.4 = (bf16[1,2,256]{2,1,0:T(2,128)(2,1)S(1)}, bf16[1,2,256]{2,1,0:T(2,128)(2,1)S(1)}, u32[]{:S(2)}, u32[]{:S(2)}) collective-permute-start(bf16[1,2,256]{2,1,0:T(2,128)(2,1)S(1)} %get-tuple-element.23), channel_id=1, source_target_pairs={{0,1},{1,2},{2,3},{3,4},{4,5},{5,6},{6,7},{7,8},{8,9},{9,10},{10,1... | collective-permute-start | bytes 3080 | tf_op jit(solution)/shard_map/ppermute | solution.py:24
  47.0 1.3 collective-permute-start.5
  48.4 1.4 fusion.256
  49.8 2.7 %collective-permute-done.5 = bf16[1,2,256]{2,1,0:T(2,128)(2,1)S(1)} collective-permute-done((bf16[1,2,256]{2,1,0:T(2,128)(2,1)S(1)}, bf16[1,2,256]{2,1,0:T(2,128)(2,1)S(1)}, u32[]{:S(2)}, u32[]{:S(2)}) %collective-permute-start.5) | collective-permute-done | bytes 1056 | tf_op jit(solution)/shard_map/ppermute | solution.py:27
  52.6 0.6 fusion.40
  53.5 4.8 %collective-permute-start.10 = (bf16[1,2,256]{2,1,0:T(2,128)(2,1)S(1)}, bf16[1,2,256]{2,1,0:T(2,128)(2,1)S(1)}, u32[]{:S(2)}, u32[]{:S(2)}) collective-permute-start(bf16[1,2,256]{2,1,0:T(2,128)(2,1)S(1)} %get-tuple-element.25), channel_id=1, source_target_pairs={{0,1},{1,2},{2,3},{3,4},{4,5},{5,6},{6,7},{7,8},{8,9},{9,10},{10,1... | collective-permute-start | bytes 3080 | tf_op jit(solution)/shard_map/ppermute | solution.py:24
  58.3 1.3 collective-permute-start.11
  59.7 4.5 %collective-permute-start.6 = (bf16[1,1,256]{2,1,0:T(2,128)(2,1)S(1)}, bf16[1,1,256]{2,1,0:T(2,128)(2,1)S(1)}, u32[]{:S(2)}, u32[]{:S(2)}) collective-permute-start(bf16[1,1,256]{2,1,0:T(2,128)(2,1)S(1)} %get-tuple-element.21), channel_id=1, source_target_pairs={{0,1},{1,2},{2,3},{3,4},{4,5},{5,6},{6,7},{7,8},{8,9},{9,10},{10,1... | collective-permute-start | bytes 1544 | tf_op jit(solution)/shard_map/ppermute | solution.py:24
  64.3 1.3 collective-permute-start.7
  65.6 0.2 convolution_dynamic-update-slice_fusion.4
  65.8 0.2 convolution_dynamic-update-slice_fusion.3
  66.2 1.5 fusion.2
  67.7 0.2 convolution_dynamic-update-slice_fusion.9
  68.3 0.2 convolution_dynamic-update-slice_fusion.6
  68.5 0.2 convolution_dynamic-update-slice_fusion.5
  68.7 0.9 broadcast_multiply_fusion.1
  69.7 0.2 convolution_dynamic-update-slice_fusion.2
  69.9 0.2 convolution_dynamic-update-slice_fusion.1
  70.1 0.2 convolution_dynamic-update-slice_fusion
  70.4 1.2 broadcast_multiply_fusion
  71.9 0.3 copy-done.10
  72.6 0.5 slice_bitcast_fusion
  73.5 4.6 %collective-permute-start.12 = (bf16[1,2,256]{2,1,0:T(2,128)(2,1)S(1)}, bf16[1,2,256]{2,1,0:T(2,128)(2,1)S(1)}, u32[]{:S(2)}, u32[]{:S(2)}) collective-permute-start(bf16[1,2,256]{2,1,0:T(2,128)(2,1)S(1)} %get-tuple-element.19), channel_id=1, source_target_pairs={{0,1},{1,2},{2,3},{3,4},{4,5},{5,6},{6,7},{7,8},{8,9},{9,10},{10,1... | collective-permute-start | bytes 3080 | tf_op jit(solution)/shard_map/ppermute | solution.py:24
  78.0 1.3 collective-permute-start.13
  79.4 4.8 %collective-permute-done.13 = bf16[1,2,256]{2,1,0:T(2,128)(2,1)S(1)} collective-permute-done((bf16[1,2,256]{2,1,0:T(2,128)(2,1)S(1)}, bf16[1,2,256]{2,1,0:T(2,128)(2,1)S(1)}, u32[]{:S(2)}, u32[]{:S(2)}) %collective-permute-start.13) | collective-permute-done | bytes 1056 | tf_op jit(solution)/shard_map/ppermute | solution.py:27
  84.3 0.3 fusion.4
  84.7 4.8 %collective-permute-start.14 = (bf16[1,2,128]{2,1,0:T(2,128)(2,1)S(1)}, bf16[1,2,128]{2,1,0:T(2,128)(2,1)S(1)}, u32[]{:S(2)}, u32[]{:S(2)}) collective-permute-start(bf16[1,2,128]{2,1,0:T(2,128)(2,1)S(1)} %get-tuple-element.27), channel_id=1, source_target_pairs={{0,1},{1,2},{2,3},{3,4},{4,5},{5,6},{6,7},{7,8},{8,9},{9,10},{10,1... | collective-permute-start | bytes 1544 | tf_op jit(solution)/shard_map/ppermute | solution.py:24
  89.5 1.3 collective-permute-start.15
  91.3 0.2 convolution_dynamic-update-slice_fusion.11
  91.5 0.2 convolution_dynamic-update-slice_fusion.10
  91.8 3.2 %collective-permute-done.15 = bf16[1,2,128]{2,1,0:T(2,128)(2,1)S(1)} collective-permute-done((bf16[1,2,128]{2,1,0:T(2,128)(2,1)S(1)}, bf16[1,2,128]{2,1,0:T(2,128)(2,1)S(1)}, u32[]{:S(2)}, u32[]{:S(2)}) %collective-permute-start.15) | collective-permute-done | bytes 544 | tf_op jit(solution)/shard_map/ppermute | solution.py:27
  95.0 0.2 convolution_select_fusion.3
  95.6 79.7 %all-reduce.9 = (bf16[64,768]{1,0:T(8,128)(2,1)S(1)}, bf16[320,128]{1,0:T(8,128)(2,1)S(1)}, bf16[768]{0:T(1024)(128)(2,1)S(1)}) all-reduce(f32[64,768]{1,0:T(8,128)S(1)} %convolution_multiply_fusion, f32[320,128]{1,0:T(8,128)S(1)} %broadcast_multiply_fusion.2, ...), channel_id=2, replica_groups=mesh['dp'=2,'seq'=16] {'seq'}, use_global_device_ids=true, to_apply=%region_8.0.clone | all-reduce | flops 90880 | bytes 545280
  175.3 0.6 dynamic-slice.9
  175.9 0.3 fusion.310
  176.3 0.5 fusion.11
  176.9 0.6 dynamic-slice_convert_fusion.1
  177.5 0.6 dynamic-slice_convert_fusion
  178.1 1.4 convert_element_type.105
  179.5 48.4 %reduce-scatter.5.cloned.1.call-done = f32[80,256]{1,0:T(8,128)} async-done(((f32[1280,256]{1,0:T(8,128)}), f32[80,256]{1,0:T(8,128)}) %reduce-scatter.5.cloned.1.call-update) | async-done | bytes 81936 | tf_op jit(solution)/shard_map/reduce_scatter | solution.py:179
  227.9 1.5 convert_element_type.107
  229.5 0.8 fusion.13
  230.3 15.9 %all-reduce.8.cloned.1.call-done = (bf16[4,768]{1,0:T(4,128)(2,1)}, bf16[20,128]{1,0:T(8,128)(2,1)}, bf16[40,256]{1,0:T(8,128)(2,1)}, bf16[80,256]{1,0:T(8,128)(2,1)}, bf16[48]{0:T(256)(128)(2,1)}) async-done(((bf16[4,768]{1,0:T(4,128)(2,1)}, bf16[20,128]{1,0:T(8,128)(2,1)}, bf16[40,256]{1,0:T(8,128)(2,1)}, bf16[80,256]{1,0:T(8,128)(2,1)}, bf16[48]{0:T(256)(128)(2,1)}), (bf16[4,768]{1,0:T(4,128)(2,1)}, ...) | async-done | bytes 72816 | tf_op jit(solution)/shard_map/psum | solution.py:183
  246.3 1.2 convert_element_type.110
  247.5 1.3 convert_element_type.102
  248.7 1.3 convert_element_type.104
  250.0 1.3 convert_element_type.106
  251.4 1.4 convert_element_type.108
  (130 shorter events, 4.2 us)
Async XLA Ops:
  7.2 10.2 %copy-start = (bf16[512,768]{1,0:T(8,128)(2,1)S(1)}, bf16[512,768]{1,0:T(8,128)(2,1)}, u32[]{:S(2)}) copy-start(bf16[512,768]{1,0:T(8,128)(2,1)} %param.10) | copy-start | bytes 2359300
  7.2 11.8 %copy-start.2 = (bf16[64,768]{1,0:T(8,128)(2,1)S(1)}, bf16[64,768]{1,0:T(8,128)(2,1)}, u32[]{:S(2)}) copy-start(bf16[64,768]{1,0:T(8,128)(2,1)} %param.11) | copy-start | bytes 294916
  7.2 170.9 %reduce-scatter.3.cloned.1.call-start = ((), (), s32[]{:S(2)}) async-start(), calls=%async_computation.2 | async-start | bytes 696320 | tf_op jit(solution)/shard_map/reduce_scatter | solution.py:178
  8.6 39.8 %collective-permute-start.8 = (f32[1,1]{1,0:T(1,128)}, f32[1,1]{1,0:T(1,128)}, u32[]{:S(2)}, u32[]{:S(2)}) collective-permute-start(f32[1,1]{1,0:T(1,128)} %get-tuple-element.38), channel_id=1, source_target_pairs={{0,1},{1,2},{2,3},{3,4},{4,5},{5,6},{6,7},{7,8},{8,9},{9,10},{10,1... | collective-permute-start | bytes 20 | tf_op jit(solution)/shard_map/ppermute | solution.py:24
  13.9 34.4 %collective-permute-start.9 = (f32[1,1]{1,0:T(1,128)}, f32[1,1]{1,0:T(1,128)}, u32[]{:S(2)}, u32[]{:S(2)}) collective-permute-start(f32[1,1]{1,0:T(1,128)} %get-tuple-element.39), channel_id=1, source_target_pairs={{1,0},{2,1},{3,2},{4,3},{5,4},{6,5},{7,6},{8,7},{9,8},{10,9},{11,1... | collective-permute-start | bytes 20 | tf_op jit(solution)/shard_map/ppermute | solution.py:27
  18.6 6.6 %copy-start.4 = (bf16[768]{0:T(1024)(128)(2,1)S(1)}, bf16[768]{0:T(1024)(128)(2,1)}, u32[]{:S(2)}) copy-start(bf16[768]{0:T(1024)(128)(2,1)} %param.15) | copy-start | bytes 4612
  18.6 11.2 %copy-start.8 = (bf16[320,128]{1,0:T(8,128)(2,1)S(1)}, bf16[320,128]{1,0:T(8,128)(2,1)}, u32[]{:S(2)}) copy-start(bf16[320,128]{1,0:T(8,128)(2,1)} %param.12) | copy-start | bytes 245764
  18.7 11.2 %copy-start.12 = (pred[8,17]{0,1:T(8,128)(4,1)S(1)}, pred[8,17]{0,1:T(8,128)(4,1)}, u32[]{:S(2)}) copy-start(pred[8,17]{0,1:T(8,128)(4,1)} %constant.81) | copy-start | bytes 412
  19.3 17.6 %copy-start.11 = (u32[32]{0:T(128)S(1)}, u32[32]{0:T(128)}, u32[]{:S(2)}) copy-start(u32[32]{0:T(128)} %constant.90) | copy-start | bytes 388
  19.4 6.0 %collective-permute-start = (bf16[1,2,64]{1,2,0:T(8,128)(2,1)S(1)}, bf16[1,2,64]{1,2,0:T(8,128)(2,1)S(1)}, u32[]{:S(2)}, u32[]{:S(2)}) collective-permute-start(bf16[1,2,64]{1,2,0:T(8,128)(2,1)S(1)} %get-tuple-element.31), channel_id=1, source_target_pairs={{0,1},{1,2},{2,3},{3,4},{4,5},{5,6},{6,7},{7,8},{8,9},{9,10},{10,1... | collective-permute-start | bytes 776 | tf_op jit(solution)/shard_map/ppermute | solution.py:24
  23.9 5.6 %collective-permute-start.1 = (bf16[1,2,64]{1,2,0:T(8,128)(2,1)S(1)}, bf16[1,2,64]{1,2,0:T(8,128)(2,1)S(1)}, u32[]{:S(2)}, u32[]{:S(2)}) collective-permute-start(bf16[1,2,64]{1,2,0:T(8,128)(2,1)S(1)} %get-tuple-element.32), channel_id=1, source_target_pairs={{1,0},{2,1},{3,2},{4,3},{5,4},{6,5},{7,6},{8,7},{9,8},{10,9},{11,1... | collective-permute-start | bytes 776 | tf_op jit(solution)/shard_map/ppermute | solution.py:27
  29.8 11.3 %copy-start.6 = (bf16[640,256]{1,0:T(8,128)(2,1)S(1)}, bf16[640,256]{1,0:T(8,128)(2,1)}, u32[]{:S(2)}) copy-start(bf16[640,256]{1,0:T(8,128)(2,1)} %param.13) | copy-start | bytes 983044
  30.9 8.6 %collective-permute-start.2 = (bf16[1,2,128]{2,1,0:T(2,128)(2,1)S(1)}, bf16[1,2,128]{2,1,0:T(2,128)(2,1)S(1)}, u32[]{:S(2)}, u32[]{:S(2)}) collective-permute-start(bf16[1,2,128]{2,1,0:T(2,128)(2,1)S(1)} %get-tuple-element.29), channel_id=1, source_target_pairs={{0,1},{1,2},{2,3},{3,4},{4,5},{5,6},{6,7},{7,8},{8,9},{9,10},{10,1... | collective-permute-start | bytes 1544 | tf_op jit(solution)/shard_map/ppermute | solution.py:24
  35.6 5.4 %collective-permute-start.3 = (bf16[1,2,128]{2,1,0:T(2,128)(2,1)S(1)}, bf16[1,2,128]{2,1,0:T(2,128)(2,1)S(1)}, u32[]{:S(2)}, u32[]{:S(2)}) collective-permute-start(bf16[1,2,128]{2,1,0:T(2,128)(2,1)S(1)} %get-tuple-element.30), channel_id=1, source_target_pairs={{1,0},{2,1},{3,2},{4,3},{5,4},{6,5},{7,6},{8,7},{9,8},{10,9},{11,1... | collective-permute-start | bytes 1544 | tf_op jit(solution)/shard_map/ppermute | solution.py:27
  41.1 7.2 %copy-start.3 = (f32[1,128]{1,0:T(1,128)S(1)}, f32[1,128]{1,0:T(1,128)}, u32[]{:S(2)}) copy-start(f32[1,128]{1,0:T(1,128)} %param.9) | copy-start | bytes 1540
  41.1 11.5 %copy-start.5 = (bf16[1280,256]{1,0:T(8,128)(2,1)S(1)}, bf16[1280,256]{1,0:T(8,128)(2,1)}, u32[]{:S(2)}) copy-start(bf16[1280,256]{1,0:T(8,128)(2,1)} %param.14) | copy-start | bytes 1966084
  42.4 7.4 %collective-permute-start.4 = (bf16[1,2,256]{2,1,0:T(2,128)(2,1)S(1)}, bf16[1,2,256]{2,1,0:T(2,128)(2,1)S(1)}, u32[]{:S(2)}, u32[]{:S(2)}) collective-permute-start(bf16[1,2,256]{2,1,0:T(2,128)(2,1)S(1)} %get-tuple-element.23), channel_id=1, source_target_pairs={{0,1},{1,2},{2,3},{3,4},{4,5},{5,6},{6,7},{7,8},{8,9},{9,10},{10,1... | collective-permute-start | bytes 3080 | tf_op jit(solution)/shard_map/ppermute | solution.py:24
  47.0 5.5 %collective-permute-start.5 = (bf16[1,2,256]{2,1,0:T(2,128)(2,1)S(1)}, bf16[1,2,256]{2,1,0:T(2,128)(2,1)S(1)}, u32[]{:S(2)}, u32[]{:S(2)}) collective-permute-start(bf16[1,2,256]{2,1,0:T(2,128)(2,1)S(1)} %get-tuple-element.24), channel_id=1, source_target_pairs={{1,0},{2,1},{3,2},{4,3},{5,4},{6,5},{7,6},{8,7},{9,8},{10,9},{11,1... | collective-permute-start | bytes 3080 | tf_op jit(solution)/shard_map/ppermute | solution.py:27
  53.5 12.5 %collective-permute-start.10 = (bf16[1,2,256]{2,1,0:T(2,128)(2,1)S(1)}, bf16[1,2,256]{2,1,0:T(2,128)(2,1)S(1)}, u32[]{:S(2)}, u32[]{:S(2)}) collective-permute-start(bf16[1,2,256]{2,1,0:T(2,128)(2,1)S(1)} %get-tuple-element.25), channel_id=1, source_target_pairs={{0,1},{1,2},{2,3},{3,4},{4,5},{5,6},{6,7},{7,8},{8,9},{9,10},{10,1... | collective-permute-start | bytes 3080 | tf_op jit(solution)/shard_map/ppermute | solution.py:24
  58.3 7.7 %collective-permute-start.11 = (bf16[1,2,256]{2,1,0:T(2,128)(2,1)S(1)}, bf16[1,2,256]{2,1,0:T(2,128)(2,1)S(1)}, u32[]{:S(2)}, u32[]{:S(2)}) collective-permute-start(bf16[1,2,256]{2,1,0:T(2,128)(2,1)S(1)} %get-tuple-element.26), channel_id=1, source_target_pairs={{1,0},{2,1},{3,2},{4,3},{5,4},{6,5},{7,6},{8,7},{9,8},{10,9},{11,1... | collective-permute-start | bytes 3080 | tf_op jit(solution)/shard_map/ppermute | solution.py:27
  59.7 12.0 %collective-permute-start.6 = (bf16[1,1,256]{2,1,0:T(2,128)(2,1)S(1)}, bf16[1,1,256]{2,1,0:T(2,128)(2,1)S(1)}, u32[]{:S(2)}, u32[]{:S(2)}) collective-permute-start(bf16[1,1,256]{2,1,0:T(2,128)(2,1)S(1)} %get-tuple-element.21), channel_id=1, source_target_pairs={{0,1},{1,2},{2,3},{3,4},{4,5},{5,6},{6,7},{7,8},{8,9},{9,10},{10,1... | collective-permute-start | bytes 1544 | tf_op jit(solution)/shard_map/ppermute | solution.py:24
  64.3 7.5 %collective-permute-start.7 = (bf16[1,1,256]{2,1,0:T(2,128)(2,1)S(1)}, bf16[1,1,256]{2,1,0:T(2,128)(2,1)S(1)}, u32[]{:S(2)}, u32[]{:S(2)}) collective-permute-start(bf16[1,1,256]{2,1,0:T(2,128)(2,1)S(1)} %get-tuple-element.22), channel_id=1, source_target_pairs={{1,0},{2,1},{3,2},{4,3},{5,4},{6,5},{7,6},{8,7},{9,8},{10,9},{11,1... | collective-permute-start | bytes 1544 | tf_op jit(solution)/shard_map/ppermute | solution.py:27
  69.7 158.3 %reduce-scatter.5.cloned.1.call-start = ((), (), s32[]{:S(2)}) async-start(), calls=%async_computation.3 | async-start | bytes 1392640 | tf_op jit(solution)/shard_map/reduce_scatter | solution.py:179
  71.5 0.7 copy-start.10
  71.7 12.7 %copy-start.7 = (bf16[640,256]{1,0:T(8,128)(2,1)S(1)}, bf16[640,256]{1,0:T(8,128)(2,1)}, u32[]{:S(2)}) copy-start(bf16[640,256]{1,0:T(8,128)(2,1)} %param.13) | copy-start | bytes 983044
  71.7 12.7 %copy-start.13 = (f32[8,17,128]{2,0,1:T(8,128)S(1)}, f32[8,17,128]{2,0,1:T(8,128)}, u32[]{:S(2)}) copy-start(f32[8,17,128]{2,0,1:T(8,128)} %get-tuple-element.45) | copy-start | bytes 208900
  71.7 174.5 %all-reduce.8.cloned.1.call-start = ((), (), s32[]{:S(2)}) async-start(), calls=%async_computation.4 | async-start | bytes 148480 | tf_op jit(solution)/shard_map/psum | solution.py:183
  73.5 5.9 %collective-permute-start.12 = (bf16[1,2,256]{2,1,0:T(2,128)(2,1)S(1)}, bf16[1,2,256]{2,1,0:T(2,128)(2,1)S(1)}, u32[]{:S(2)}, u32[]{:S(2)}) collective-permute-start(bf16[1,2,256]{2,1,0:T(2,128)(2,1)S(1)} %get-tuple-element.19), channel_id=1, source_target_pairs={{0,1},{1,2},{2,3},{3,4},{4,5},{5,6},{6,7},{7,8},{8,9},{9,10},{10,1... | collective-permute-start | bytes 3080 | tf_op jit(solution)/shard_map/ppermute | solution.py:24
  78.0 6.2 %collective-permute-start.13 = (bf16[1,2,256]{2,1,0:T(2,128)(2,1)S(1)}, bf16[1,2,256]{2,1,0:T(2,128)(2,1)S(1)}, u32[]{:S(2)}, u32[]{:S(2)}) collective-permute-start(bf16[1,2,256]{2,1,0:T(2,128)(2,1)S(1)} %get-tuple-element.20), channel_id=1, source_target_pairs={{1,0},{2,1},{3,2},{4,3},{5,4},{6,5},{7,6},{8,7},{9,8},{10,9},{11,1... | collective-permute-start | bytes 3080 | tf_op jit(solution)/shard_map/ppermute | solution.py:27
  79.4 15.7 %copy-start.9 = (bf16[320,128]{1,0:T(8,128)(2,1)S(1)}, bf16[320,128]{1,0:T(8,128)(2,1)}, u32[]{:S(2)}) copy-start(bf16[320,128]{1,0:T(8,128)(2,1)} %param.12) | copy-start | bytes 245764
  84.7 7.1 %collective-permute-start.14 = (bf16[1,2,128]{2,1,0:T(2,128)(2,1)S(1)}, bf16[1,2,128]{2,1,0:T(2,128)(2,1)S(1)}, u32[]{:S(2)}, u32[]{:S(2)}) collective-permute-start(bf16[1,2,128]{2,1,0:T(2,128)(2,1)S(1)} %get-tuple-element.27), channel_id=1, source_target_pairs={{0,1},{1,2},{2,3},{3,4},{4,5},{5,6},{6,7},{7,8},{8,9},{9,10},{10,1... | collective-permute-start | bytes 1544 | tf_op jit(solution)/shard_map/ppermute | solution.py:24
  89.5 5.4 %collective-permute-start.15 = (bf16[1,2,128]{2,1,0:T(2,128)(2,1)S(1)}, bf16[1,2,128]{2,1,0:T(2,128)(2,1)S(1)}, u32[]{:S(2)}, u32[]{:S(2)}) collective-permute-start(bf16[1,2,128]{2,1,0:T(2,128)(2,1)S(1)} %get-tuple-element.28), channel_id=1, source_target_pairs={{1,0},{2,1},{3,2},{4,3},{5,4},{6,5},{7,6},{8,7},{9,8},{10,9},{11,1... | collective-permute-start | bytes 1544 | tf_op jit(solution)/shard_map/ppermute | solution.py:27
  95.0 81.2 %copy-start.1 = (bf16[1,128,512]{2,1,0:T(8,128)(2,1)S(1)}, bf16[1,128,512]{2,1,0:T(8,128)(2,1)}, u32[]{:S(2)}) copy-start(bf16[1,128,512]{2,1,0:T(8,128)(2,1)} %param.8) | copy-start | bytes 393220
Sparse Core Ops, SparseCore 0:
  69.8 80.7 reduce-scatter.2
  153.0 74.9 reduce-scatter.4
  231.3 14.8 all-reduce.7
where the time goes:
time: 260 us; the launch traced here: 259 us
  waiting for transfers between devices  81 us (31%)
  blocking collectives  79.7 us (31%)
  starting transfers between devices  48.4 us (19%)
  other arithmetic  16.7 us (6%)
  between operations  16.7 us (6%)
  matrix products  10.8 us (4%)
  local copies, waits for them, and re-layouts  5.96 us (2%)
    unnamed x1, blocking collectives  79.7 us
    reduce_scatter x1, waiting for transfers between devices, shards(): lax.psum_scatter(terms[3], 'seq', scatter_dimension=0, tiled=True)  48.4 us
    ppermute x8, starting transfers between devices, padded(): lax.ppermute(lax.slice_in_dim(block, block.shape[dim] - width, None, axis...  38 us
    ppermute x8, waiting for transfers between devices, padded(): lax.ppermute(lax.slice_in_dim(block, 0, width, axis=dim), axis, backward)  16.5 us
    psum x1, waiting for transfers between devices, shards(): lax.psum(partial_value[0].astype(jnp.bfloat16), 'dp').astype(jnp.float32)  15.9 us
    ppermute x8, starting transfers between devices, padded(): lax.ppermute(lax.slice_in_dim(block, 0, width, axis=dim), axis, backward)  10.3 us
  transfers between devices with their start and end apart: 19, of which 8 were waited for; matrix products, arithmetic and copies ran while one was open for 9% of the time, Pallas kernels for 0%

commit v1 on v0

v1 whole, which is shorter than its diff:
```python
import functools
import math

import jax
import jax.numpy as jnp
from jax import lax
from jax.experimental import pallas as pl
from jax.experimental.pallas import tpu as pltpu
from jax.sharding import PartitionSpec as P

C0 = 64
C1 = 128
C2 = 256
HK = 5
PK = 3
EDGE = 16
LANES = 128

EPSILON = 1e-05
SLOPE = 0.1
BF16 = jnp.bfloat16
F32 = jnp.float32
NT = (((1,), (1,)), ((), ()))
TN = (((0,), (0,)), ((), ()))


def normalize(values):
    average = jnp.mean(values, axis=-1, keepdims=True)
    centred = values - average
    variance = jnp.mean(centred * centred, axis=-1, keepdims=True)
    inverse = lax.rsqrt(variance + EPSILON)
    return (centred * inverse, inverse)


def normalize_back(upstream, normed, inverse):
    first_mean = jnp.mean(upstream, axis=-1, keepdims=True)
    second_mean = jnp.mean(upstream * normed, axis=-1, keepdims=True)
    return (upstream - first_mean - normed * second_mean) * inverse


def leaky_pair(values):
    cumulative = 0.5 * (1.0 + lax.erf(values * math.sqrt(0.5)))
    density = jnp.exp(-0.5 * values * values) * (1.0 / math.sqrt(2.0 * math.pi))
    unit = SLOPE * values + (1.0 - SLOPE) * (values * cumulative)
    slope = SLOPE + (1.0 - SLOPE) * (cumulative + values * density)
    return unit, slope


def dot(a, b, dims=(((1,), (0,)), ((), ()))):
    return lax.dot_general(a, b, dims, preferred_element_type=F32)


def forward_rows(rows, projection, squeeze):
    normed, _ = normalize(rows.astype(F32))
    projected = dot(normed.astype(BF16), projection).astype(BF16)
    hidden_normed, _ = normalize(projected.astype(F32))
    hidden = hidden_normed.astype(BF16)
    return projected, hidden, dot(hidden, squeeze, NT)


def edges_kernel(first_ref, last_ref, cot_ref, up_ref, down_ref):
    cot = cot_ref[...]
    high = cot.astype(BF16).astype(F32)
    middle = (cot - high).astype(BF16).astype(F32)
    low = cot - high - middle
    stack = jnp.concatenate([high, middle, low, jnp.zeros((EDGE - 3, cot.shape[1]), F32)], axis=0).astype(BF16)
    rest = jnp.zeros((EDGE, first_ref.shape[1] - cot.shape[1]), BF16)
    extra = jnp.concatenate([stack, rest], axis=1)
    up_ref[:EDGE, :] = last_ref[...]
    up_ref[EDGE:, :] = extra
    down_ref[:EDGE, :] = first_ref[...]
    down_ref[EDGE:, :] = extra


def project_kernel(rows_ref, projection_ref, squeeze_ref, projected_ref, hidden_ref, squeezed_ref):
    projected, hidden, squeezed = forward_rows(rows_ref[...], projection_ref[...], squeeze_ref[...])
    projected_ref[...] = projected
    hidden_ref[...] = hidden
    squeezed_ref[...] = squeezed


def shifted(values, taps, sign):
    count = values.shape[0]
    pieces = []
    for k in range(taps):
        amount = (-sign * (k - (taps - 1) // 2)) % count
        moved = values if amount == 0 else pltpu.roll(values, amount, 0)
        pieces.append(moved.astype(BF16))
    return pieces


def pieces_of(n, count, rows):
    found = []
    for s in range(n):
        at = s * count
        while at < (s + 1) * count:
            tap, row = divmod(at, rows)
            length = min(rows - row, (s + 1) * count - at)
            found.append((s, tap, row, at - s * count, length))
            at += length
    return found


def head_kernel(
    n,
    packed,
    place_ref,
    squeezed_ref,
    low_ref,
    high_ref,
    cot_ref,
    hidden_ref,
    projection_ref,
    squeeze_ref,
    first_ref,
    second_ref,
    third_ref,
    final_ref,
    scores_ref,
    delta_ref,
    *outs,
):
    frames = squeezed_ref.shape[0]
    total = frames + 2 * EDGE
    own = slice(EDGE, EDGE + frames)
    seq, core = place_ref[0], place_ref[1]
    row = lax.broadcasted_iota(jnp.int32, (total, LANES), 0)
    inside = ((row >= EDGE) | (seq > 0)) & ((row < EDGE + frames) | (seq < n - 1))

    def mask(values):
        width = values.shape[1]
        if width <= LANES:
            return jnp.where(inside[:, :width], values, 0.0)
        return jnp.concatenate(
            [jnp.where(inside, values[:, i : i + LANES], 0.0) for i in range(0, width, LANES)], axis=1
        )

    edge = jnp.concatenate([low_ref[:EDGE, :], high_ref[:EDGE, :]], axis=0)
    _, _, edge_squeezed = forward_rows(edge, projection_ref[...], squeeze_ref[...])
    squeezed = jnp.concatenate([edge_squeezed[:EDGE], squeezed_ref[...], edge_squeezed[EDGE:]], axis=0)

    def joined(ref):
        parts = ref[EDGE:, :LANES].astype(F32)
        return parts[0:1] + parts[1:2] + parts[2:3]

    rows = [cot_ref[...], joined(low_ref), joined(high_ref), jnp.zeros((5, LANES), F32)]
    columns = jnp.concatenate(rows, axis=0).T
    cot = jnp.concatenate(
        [
            jnp.broadcast_to(columns[frames - EDGE :, 1:2], (EDGE, LANES)),
            jnp.broadcast_to(columns[:, 0:1], (frames, LANES)),
            jnp.broadcast_to(columns[:EDGE, 2:3], (EDGE, LANES)),
        ],
        axis=0,
    )

    weights = (first_ref, second_ref, third_ref)
    act = squeezed
    inputs, slopes = [], []
    for ref in weights:
        unit, slope = leaky_pair(act)
        unit = mask(unit)
        slopes.append(slope)
        inputs.append(unit[own].astype(BF16))
        width = unit.shape[1]
        act = jnp.zeros((total, ref.shape[1]), F32)
        for k, piece in enumerate(shifted(unit, HK, 1)):
            act = act + dot(piece, ref[k * width : (k + 1) * width, :])
    unit, slope = leaky_pair(act)
    final_in = mask(unit).astype(BF16).astype(F32)
    taps = shifted(final_in, PK, 1)
    scores = jnp.zeros((1, frames), F32)
    for k in range(PK):
        scores = scores + dot(final_ref[:, k * C2 : (k + 1) * C2], taps[k][own], NT)
    scores_ref[...] = scores

    upstream = [jnp.zeros((total, LANES), F32)] * (C2 // LANES)
    final_grad = []
    for k in range(PK):
        amount = (k - 1) % total
        moved = cot if amount == 0 else pltpu.roll(cot, amount, 0)
        for h in range(C2 // LANES):
            lanes = slice(k * C2 + h * LANES, k * C2 + (h + 1) * LANES)
            upstream[h] = upstream[h] + moved * final_ref[:, lanes].astype(F32)
            final_grad.append(
                jnp.sum(moved[own] * final_in[own, h * LANES : (h + 1) * LANES], axis=0, keepdims=True)
            )
    upstream = jnp.concatenate(upstream, axis=1)
    slopes.append(slope)
    grads = []
    for layer in (2, 1, 0):
        delta = mask(upstream * slopes[layer + 1])
        pieces = shifted(delta, HK, -1)
        near = jnp.concatenate([p[own] for p in pieces], axis=1)
        grads.append(dot(inputs[layer], near, TN))
        ref = weights[layer]
        width = ref.shape[0] // HK
        upstream = jnp.zeros((total, width), F32)
        for k, piece in enumerate(pieces):
            upstream = upstream + dot(piece, ref[k * width : (k + 1) * width, :], NT)
    third, second, first = grads
    delta = (upstream[own] * slopes[0][own]).astype(BF16)
    delta_ref[...] = delta
    squeeze_grad = dot(delta, hidden_ref[...], TN)

    if not packed:
        squeeze_out, first_out, second_out, third_out, final_out = outs
        squeeze_out[...] = squeeze_grad
        for out, grad in ((first_out, first), (second_out, second), (third_out, third)):
            width, cols = grad.shape[0], out.shape[1]
            for k in range(HK):
                out[k * width : (k + 1) * width, :] = grad[:, k * cols : (k + 1) * cols]
        for i, part in enumerate(final_grad):
            final_out[:, i * LANES : (i + 1) * LANES] = part
        return

    (payload_ref, scratch) = outs
    half = payload_ref.shape[3]
    mine = [(seq ^ s) for s in range(n)]

    def put(s, at, rows):
        slot = mine[s]
        while rows.shape[0]:
            side, start = divmod(at, half)
            length = min(rows.shape[0], half - start)
            payload_ref[side ^ core, slot & 3, slot >> 2, start : start + length, :] = rows[:length]
            rows = rows[length:]
            at += length

    base = 0
    for grad, channels, cols in ((third, C2, C2), (second, C1, C2)):
        count = HK * channels // n
        for s, tap, start, offset, length in pieces_of(n, count, channels):
            for h in range(cols // LANES):
                lanes = slice(tap * cols + h * LANES, tap * cols + (h + 1) * LANES)
                scratch[s, base + h * count + offset : base + h * count + offset + length, :] = grad[
                    start : start + length, lanes
                ]
        base += count * (cols // LANES)
    count = C0 // n
    for s in range(n):
        for h in range(squeeze_grad.shape[1] // LANES):
            scratch[s, base + h * count : base + (h + 1) * count, :] = squeeze_grad[
                s * count : (s + 1) * count, h * LANES : (h + 1) * LANES
            ]
    base += count * (squeeze_grad.shape[1] // LANES)
    count = HK * C0 // n
    for s, tap, start, offset, length in pieces_of(n, count, C0):
        scratch[s, base + offset : base + offset + length, :] = first[
            start : start + length, tap * C1 : (tap + 1) * C1
        ]
    base += count
    final_row = jnp.concatenate(final_grad, axis=1)
    count = final_row.shape[1] // n
    for s in range(n):
        first_half = s * count // LANES * LANES
        piece = final_row[:, first_half : first_half + 2 * LANES]
        if piece.shape[1] < 2 * LANES:
            piece = jnp.concatenate([piece, piece[:, :LANES]], axis=1)
        amount = (first_half - s * count) % (2 * LANES)
        piece = piece if amount == 0 else pltpu.roll(jnp.broadcast_to(piece, (8, 2 * LANES)), amount, 1)
        scratch[s, base : base + 1, :] = piece[0:1, :LANES]
        scratch[s, base + 1 :, :] = jnp.zeros((scratch.shape[1] - base - 1, LANES), F32)
    for s in range(n):
        put(s, 0, scratch[s].astype(BF16))


def feature_kernel(rows_ref, projected_ref, delta_ref, squeeze_ref, projection_ref, out_ref):
    hidden_upstream = dot(delta_ref[...], squeeze_ref[...])
    hidden_normed, hidden_inverse = normalize(projected_ref[...].astype(F32))
    projected_grad = normalize_back(hidden_upstream, hidden_normed, hidden_inverse).astype(BF16)
    normed_grad = dot(projected_grad, projection_ref[...], NT)
    normed, inverse = normalize(rows_ref[...].astype(F32))
    out_ref[...] = normalize_back(normed_grad, normed, inverse)


def unpack_kernel(factor, mine_ref, other_ref, place_ref, squeeze_ref, first_ref, second_ref, third_ref, final_ref, both):
    half = mine_ref.shape[0]
    core = place_ref[1]
    both[pl.ds(pl.multiple_of(core * half, 16), half), :] = mine_ref[...].astype(F32) * factor
    both[pl.ds(pl.multiple_of((1 - core) * half, 16), half), :] = other_ref[...].astype(F32) * factor
    base = 0
    for ref in (third_ref, second_ref, squeeze_ref, first_ref):
        count = ref.shape[0]
        for h in range(ref.shape[1] // LANES):
            ref[:, h * LANES : (h + 1) * LANES] = both[base : base + count, :]
            base += count
    final_ref[...] = both[base : base + 1, :]


def sds(shape, dtype):
    return jax.ShapeDtypeStruct(shape, dtype)


VMEM = pl.BlockSpec(memory_space=pltpu.VMEM)
SMEM = pl.BlockSpec(memory_space=pltpu.SMEM)


def params(mib):
    return pltpu.CompilerParams(vmem_limit_bytes=mib * 1024 * 1024)


def cost(flops, nbytes):
    return pl.CostEstimate(flops=flops, bytes_accessed=nbytes, transcendentals=0)


def shards(
    features,
    score_cotangent,
    projection_weight,
    squeeze_weight,
    first_weight,
    second_weight,
    third_weight,
    final_weight,
):
    n, cores = lax.axis_size("seq"), lax.axis_size("dp")
    frames, feat = features.shape[1:]
    width = projection_weight.shape[1]
    seq, core = lax.axis_index("seq"), lax.axis_index("dp")
    packed = n == 16 and cores == 2
    rows = features.reshape(frames, feat)
    place = jnp.stack([seq, core]).astype(jnp.int32)

    up, down = pl.pallas_call(
        edges_kernel,
        grid=(1,),
        in_specs=[
            pl.BlockSpec((EDGE, feat), lambda i: (0, 0)),
            pl.BlockSpec((EDGE, feat), lambda i: (frames // EDGE - 1, 0)),
            pl.BlockSpec((1, frames), lambda i: (0, 0)),
        ],
        out_specs=[pl.BlockSpec((2 * EDGE, feat), lambda i: (0, 0))] * 2,
        out_shape=[sds((2 * EDGE, feat), BF16)] * 2,
        name="edges",
    )(rows, rows, score_cotangent)
    low = lax.ppermute(up, "seq", [(i, i + 1) for i in range(n - 1)])
    high = lax.ppermute(down, "seq", [(i + 1, i) for i in range(n - 1)])

    projected, hidden, squeezed = pl.pallas_call(
        project_kernel,
        in_specs=[VMEM] * 3,
        out_specs=[VMEM] * 3,
        out_shape=[sds((frames, width), BF16), sds((frames, width), BF16), sds((frames, C0), F32)],
        compiler_params=params(16),
        cost_estimate=cost(2 * frames * width * (feat + C0), 2 * feat * width),
        name="project",
    )(rows, projection_weight, squeeze_weight)

    if packed:
        half = 144
        grad_shapes = [sds((2, 4, 4, half, LANES), BF16)]
        scratch = [pltpu.VMEM((n, 2 * half, LANES), F32)]
    else:
        grad_shapes = [
            sds((C0, width), F32),
            sds(first_weight.shape, F32),
            sds(second_weight.shape, F32),
            sds(third_weight.shape, F32),
            sds((1, PK * C2), F32),
        ]
        scratch = []
    scores, delta, *grads = pl.pallas_call(
        functools.partial(head_kernel, n, packed),
        in_specs=[SMEM] + [VMEM] * 11,
        out_specs=[VMEM] * (2 + len(grad_shapes)),
        out_shape=[sds((1, frames), F32), sds((frames, C0), BF16), *grad_shapes],
        scratch_shapes=scratch,
        compiler_params=params(32),
        cost_estimate=cost(10**9, 4 * 10**6),
        name="head",
    )(
        place,
        squeezed,
        low,
        high,
        score_cotangent,
        hidden,
        projection_weight,
        squeeze_weight,
        first_weight,
        second_weight,
        third_weight,
        final_weight.reshape(1, PK * C2),
    )

    feature_grad = pl.pallas_call(
        feature_kernel,
        in_specs=[VMEM] * 5,
        out_specs=VMEM,
        out_shape=sds((frames, feat), F32),
        compiler_params=params(16),
        cost_estimate=cost(2 * frames * width * (feat + C0), 2 * feat * width),
        name="feature",
    )(rows, projected, delta, squeeze_weight, projection_weight)

    factor = 1.0 / math.sqrt(cores * n * frames)
    if not packed:
        shares = []
        for term in grads[:4] + [grads[4].reshape(PK * C2)]:
            part = lax.psum_scatter(term * factor, "seq", scatter_dimension=0, tiled=True)
            shares.append(lax.psum(part.astype(BF16), "dp").astype(F32))
        return (scores, feature_grad[None], *shares)

    def added(*terms):
        total = terms[0].astype(F32)
        for term in terms[1:]:
            total = total + term.astype(F32)
        return total.astype(BF16)

    swap = [(0, 1), (1, 0)]
    (payload,) = grads
    held = added(payload[0], lax.ppermute(payload[1], "dp", swap))
    for stride in (1, 4):
        moved = [
            lax.ppermute(held[j], "seq", [(i, i ^ (j * stride)) for i in range(n)]) for j in (3, 1, 2)
        ]
        held = added(held[0], *moved)
    other = lax.ppermute(held, "dp", swap)
    shapes = [
        (C0 // n, width),
        (HK * C0 // n, C1),
        (HK * C1 // n, C2),
        (HK * C2 // n, C2),
        (1, LANES),
    ]
    *shares, final = pl.pallas_call(
        functools.partial(unpack_kernel, factor),
        in_specs=[VMEM, VMEM, SMEM],
        out_specs=[VMEM] * 5,
        out_shape=[sds(shape, F32) for shape in shapes],
        scratch_shapes=[pltpu.VMEM((2 * half, LANES), F32)],
        name="unpack",
    )(held, other, place)
    return (scores, feature_grad[None], *shares, final[0, : PK * C2 // n])


def solution(mesh):
    placed = (P("dp", "seq", None), P("dp", "seq"), P(), P(), P(), P(), P(), P())
    return jax.shard_map(
        shards,
        mesh=mesh,
        in_specs=placed,
        out_specs=(
            P("dp", "seq"),
            P("dp", "seq", None),
            P("seq", None),
            P("seq", None),
            P("seq", None),
            P("seq", None),
            P("seq"),
        ),
        check_vma=False,
    )
```

time: 260 us -> 49.8 us (0.19)
  blocking collectives: 79.7 us -> 0 us
  waiting for transfers between devices: 81 us -> 13.8 us
  starting transfers between devices: 48.4 us -> 16.4 us
  other arithmetic: 16.7 us -> 0.35 us
  between operations: 16.7 us -> 0.79 us
  matrix products: 10.8 us -> 0 us
  Pallas kernels: 0 us -> 9.38 us
  local copies, waits for them, and re-layouts: 5.96 us -> 8.67 us
    unnamed x1 -> x0, blocking collectives: 79.7 us -> none
    reduce_scatter x2 -> x0, waiting for transfers between devices: 48.4 us -> none  [the longest x1 48.4 us: shards(): lax.psum_scatter(terms[3], 'seq', scatter_dimension=0, tiled=True)]
    ppermute x16 -> x10, starting transfers between devices: 48.3 us -> 16.4 us  [the longest x6 10.1 us: shards(): lax.ppermute(held[j], 'seq', [(i, i ^ j * stride) for i in range(n)])]
    psum x1 -> x0, waiting for transfers between devices: 15.9 us -> none  [shards(): lax.psum(partial_value[0].astype(jnp.bfloat16), 'dp').astype(jnp.float32)]
    convert_element_type x9 -> x3, other arithmetic: 9.69 us -> 0.27 us  [added(): return total.astype(BF16)]
    pallas_call x0 -> x5, Pallas kernels: none -> 9.38 us  [the longest x1 4.21 us: shards(): pl.pallas_call(functools.partial(head_kernel, n, packed), in_specs=[SMEM]...]
    dot_general x23 -> x0, matrix products: 5.99 us -> none  [the longest x15 2.97 us: tap_gradients(): jnp.einsum('utc,ute->ce', extended[:, offset:offset + length], delta, pre...]
    unnamed x32 -> x26, local copies, waits for them, and re-layouts: 1.77 us -> 6.76 us
  transfers between devices with their start and end apart: 19 -> 10, of which waited for: 8 -> 7; matrix products, arithmetic and copies ran while one was open for 9% -> 2% of each run, Pallas kernels for 0% -> 5%
where the time goes in v1:
time: 49.8 us; the launch traced here: 49.3 us
  starting transfers between devices  16.4 us (33%)
  waiting for transfers between devices  13.8 us (28%)
  Pallas kernels  9.38 us (19%)
  local copies, waits for them, and re-layouts  8.67 us (17%)
  between operations  0.79 us (2%)
    ppermute x6, waiting for transfers between devices, shards(): lax.ppermute(held[j], 'seq', [(i, i ^ j * stride) for i in range(n)])  11.6 us
    ppermute x6, starting transfers between devices, shards(): lax.ppermute(held[j], 'seq', [(i, i ^ j * stride) for i in range(n)])  10.1 us
    unnamed x26, local copies, waits for them, and re-layouts  6.76 us
    ppermute x1, starting transfers between devices, shards(): low = lax.ppermute(up, 'seq', [(i, i + 1) for i in range(n - 1)])  4.83 us
    pallas_call x1, Pallas kernels, shards(): pl.pallas_call(functools.partial(head_kernel, n, packed), in_specs=[SMEM]...  4.21 us
    ppermute x1, waiting for transfers between devices, shards(): held = added(payload[0], lax.ppermute(payload[1], 'dp', swap))  1.99 us
    pallas_call x1, Pallas kernels, shards(): pl.pallas_call(functools.partial(unpack_kernel, factor), in_specs=[VMEM,...  1.47 us
    pallas_call x1, Pallas kernels, shards(): pl.pallas_call(feature_kernel, in_specs=[VMEM] * 5, out_specs=VMEM, out_s...  1.46 us
  transfers between devices with their start and end apart: 10, of which 7 were waited for; matrix products, arithmetic and copies ran while one was open for 2% of the time, Pallas kernels for 5%

profile of v1, /device:TPU:0, one launch (start us, length us, event | category | flops | bytes accessed | tf_op | source)
XLA Modules:
  0.0 49.3 jit_solution(5012916966900879362)
XLA Ops:
  0.6 0.0 copy-start.6
  0.6 0.0 copy-start.5
  0.7 0.0 copy-start.10
  0.7 1.4 %edges.1 = (bf16[32,512]{1,0:T(8,128)(2,1)}, bf16[32,512]{1,0:T(8,128)(2,1)}) custom-call(bf16[128,512]{1,0:T(8,128)(2,1)} %bitcast.33, bf16[128,512]{1,0:T(8,128)(2,1)} %bitcast.34, f32[1,128]{1,0:T(1,128)} %cot_ref.3), custom_call_target="tpu_custom_call" | custom-call | tf_op jit(solution)/shard_map/edges/pallas_call | solution.py:325
  2.1 4.8 %collective-permute-start = (bf16[32,512]{1,0:T(8,128)(2,1)}, bf16[32,512]{1,0:T(8,128)(2,1)S(1)}, u32[]{:S(2)}, u32[]{:S(2)}) collective-permute-start(bf16[32,512]{1,0:T(8,128)(2,1)} %get-tuple-element.21), channel_id=1, source_target_pairs={{0,1},{1,2},{2,3},{3,4},{4,5},{5,6},{6,7},{7,8},{8,9},{9,10},{10,1... | collective-permute-start | bytes 98312 | tf_op jit(solution)/shard_map/ppermute | solution.py:337
  6.9 1.3 %collective-permute-start.1 = (bf16[32,512]{1,0:T(8,128)(2,1)}, bf16[32,512]{1,0:T(8,128)(2,1)S(1)}, u32[]{:S(2)}, u32[]{:S(2)}) collective-permute-start(bf16[32,512]{1,0:T(8,128)(2,1)} %get-tuple-element.22), channel_id=1, source_target_pairs={{1,0},{2,1},{3,2},{4,3},{5,4},{6,5},{7,6},{8,7},{9,8},{10,9},{11,1... | collective-permute-start | bytes 98312 | tf_op jit(solution)/shard_map/ppermute | solution.py:338
  8.2 0.1 pad_add_fusion.place_ref
  8.3 0.0 copy-start.7
  8.3 0.7 %reshape.27.final_ref = bf16[1,768]{1,0:T(2,128)(2,1)S(1)} reshape(bf16[768]{0:T(1024)(128)(2,1)} %param.15) | data formatting | bytes 3072 | tf_op jit(solution)/shard_map/reshape | solution.py:384
  9.0 0.0 copy-start
  9.0 1.1 %copy-done = bf16[512,768]{1,0:T(8,128)(2,1)S(1)} copy-done((bf16[512,768]{1,0:T(8,128)(2,1)S(1)}, bf16[512,768]{1,0:T(8,128)(2,1)}, u32[]{:S(2)}) %copy-start) | copy-done | bytes 786456
  10.1 0.0 copy-start.2
  10.1 0.9 %copy-done.2 = bf16[1,128,512]{2,1,0:T(8,128)(2,1)S(1)} copy-done((bf16[1,128,512]{2,1,0:T(8,128)(2,1)S(1)}, bf16[1,128,512]{2,1,0:T(8,128)(2,1)}, u32[]{:S(2)}) %copy-start.2) | copy-done | bytes 131096
  11.0 0.0 copy-start.4
  11.0 0.9 %copy-done.4 = bf16[64,768]{1,0:T(8,128)(2,1)S(1)} copy-done((bf16[64,768]{1,0:T(8,128)(2,1)S(1)}, bf16[64,768]{1,0:T(8,128)(2,1)}, u32[]{:S(2)}) %copy-start.4) | copy-done | bytes 98328
  11.9 0.8 %project.1 = (bf16[128,768]{1,0:T(8,128)(2,1)S(1)}, bf16[128,768]{1,0:T(8,128)(2,1)S(1)}, f32[128,64]{1,0:T(8,128)S(1)}) custom-call(bf16[128,512]{1,0:T(8,128)(2,1)S(1)} %bitcast.35, bf16[512,768]{1,0:T(8,128)(2,1)S(1)} %copy-done, bf16[64,768]{1,0:T(8,128)(2,1)S(1)} %copy-done.4), custom_call_target="tpu_custom_call" | custom-call | flops 113246208 | bytes 786432 | tf_op jit(solution)/shard_map/project/pallas_call | solution.py:340
  12.7 0.0 collective-permute-done.low_ref
  12.8 0.2 collective-permute-done.1.high_ref
  12.9 0.0 copy-done.6
  12.9 0.0 copy-done.5
  12.9 0.0 copy-done.10
  13.0 0.0 copy-start.1
  13.0 1.1 %copy-done.1 = bf16[512,768]{1,0:T(8,128)(2,1)S(1)} copy-done((bf16[512,768]{1,0:T(8,128)(2,1)S(1)}, bf16[512,768]{1,0:T(8,128)(2,1)}, u32[]{:S(2)}) %copy-start.1) | copy-done | bytes 786456
  14.1 0.0 copy-start.8
  14.1 1.1 %copy-done.8 = bf16[1280,256]{1,0:T(8,128)(2,1)S(1)} copy-done((bf16[1280,256]{1,0:T(8,128)(2,1)S(1)}, bf16[1280,256]{1,0:T(8,128)(2,1)}, u32[]{:S(2)}) %copy-start.8) | copy-done | bytes 655384
  15.2 0.0 copy-start.9
  15.2 1.0 %copy-done.9 = bf16[640,256]{1,0:T(8,128)(2,1)S(1)} copy-done((bf16[640,256]{1,0:T(8,128)(2,1)S(1)}, bf16[640,256]{1,0:T(8,128)(2,1)}, u32[]{:S(2)}) %copy-start.9) | copy-done | bytes 327704
  16.2 4.2 %head.1 = (f32[1,128]{1,0:T(1,128)}, bf16[128,64]{1,0:T(8,128)(2,1)S(1)}, bf16[2,4,4,144,128]{4,3,2,1,0:T(8,128)(2,1)S(1)}) custom-call(s32[2]{0:T(128)S(1)} %pad_add_fusion.place_ref, f32[128,64]{1,0:T(8,128)S(1)} %get-tuple-element.20.squeezed_ref, bf16[32,512]{1,0:T(8,128)(2,1)S(1)} %collective-permute-done.low_ref, ...), custom_call_target="tpu_custom_call" | custom-call | flops 1000000000 | bytes 4000000 | tf_op jit(solution)/shard_map/head/pallas_call | solution.py:363
  20.4 0.0 copy-done.7
  20.4 0.1 collective-permute-start.2
  20.5 2.0 %collective-permute-done.2 = bf16[4,4,144,128]{3,2,1,0:T(8,128)(2,1)S(1)} collective-permute-done((bf16[4,4,144,128]{3,2,1,0:T(8,128)(2,1)S(1)}, bf16[4,4,144,128]{3,2,1,0:T(8,128)(2,1)S(1)}, u32[]{:S(2)}, u32[]{:S(2)}) %collective-permute-start.2) | collective-permute-done | bytes 589856 | tf_op jit(solution)/shard_map/ppermute | solution.py:413
  22.5 0.2 fusion
  22.6 0.0 copy-start.3
  22.7 4.4 %collective-permute-start.3 = (bf16[4,144,128]{2,1,0:T(8,128)(2,1)S(1)}, bf16[4,144,128]{2,1,0:T(8,128)(2,1)S(1)}, u32[]{:S(2)}, u32[]{:S(2)}) collective-permute-start(bf16[4,144,128]{2,1,0:T(8,128)(2,1)S(1)} %get-tuple-element.33), channel_id=1, source_target_pairs={{0,3},{1,2},{2,1},{3,0},{4,7},{5,6},{6,5},{7,4},{8,11},{9,10},{10,... | collective-permute-start | bytes 442376 | tf_op jit(solution)/shard_map/ppermute | solution.py:416
  27.1 0.6 %collective-permute-start.4 = (bf16[4,144,128]{2,1,0:T(8,128)(2,1)S(1)}, bf16[4,144,128]{2,1,0:T(8,128)(2,1)S(1)}, u32[]{:S(2)}, u32[]{:S(2)}) collective-permute-start(bf16[4,144,128]{2,1,0:T(8,128)(2,1)S(1)} %get-tuple-element.35), channel_id=1, source_target_pairs={{0,1},{1,0},{2,3},{3,2},{4,5},{5,4},{6,7},{7,6},{8,9},{9,8},{10,11... | collective-permute-start | bytes 442376 | tf_op jit(solution)/shard_map/ppermute | solution.py:416
  27.7 0.1 collective-permute-start.5
  27.7 4.0 %collective-permute-done.3 = bf16[4,144,128]{2,1,0:T(8,128)(2,1)S(1)} collective-permute-done((bf16[4,144,128]{2,1,0:T(8,128)(2,1)S(1)}, bf16[4,144,128]{2,1,0:T(8,128)(2,1)S(1)}, u32[]{:S(2)}, u32[]{:S(2)}) %collective-permute-start.3) | collective-permute-done | bytes 147488 | tf_op jit(solution)/shard_map/ppermute | solution.py:416
  31.7 3.0 %collective-permute-done.4 = bf16[4,144,128]{2,1,0:T(8,128)(2,1)S(1)} collective-permute-done((bf16[4,144,128]{2,1,0:T(8,128)(2,1)S(1)}, bf16[4,144,128]{2,1,0:T(8,128)(2,1)S(1)}, u32[]{:S(2)}, u32[]{:S(2)}) %collective-permute-start.4) | collective-permute-done | bytes 147488 | tf_op jit(solution)/shard_map/ppermute | solution.py:416
  34.7 0.0 collective-permute-done.5
  34.7 0.1 fusion.3
  34.8 4.5 %collective-permute-start.6 = (bf16[144,128]{1,0:T(8,128)(2,1)S(1)}, bf16[144,128]{1,0:T(8,128)(2,1)S(1)}, u32[]{:S(2)}, u32[]{:S(2)}) collective-permute-start(bf16[144,128]{1,0:T(8,128)(2,1)S(1)} %get-tuple-element.36), channel_id=1, source_target_pairs={{0,12},{1,13},{2,14},{3,15},{4,8},{5,9},{6,10},{7,11},{8,4},{9,5},... | collective-permute-start | bytes 110600 | tf_op jit(solution)/shard_map/ppermute | solution.py:416
  39.3 0.0 collective-permute-start.7
  39.3 0.6 %collective-permute-start.8 = (bf16[144,128]{1,0:T(8,128)(2,1)S(1)}, bf16[144,128]{1,0:T(8,128)(2,1)S(1)}, u32[]{:S(2)}, u32[]{:S(2)}) collective-permute-start(bf16[144,128]{1,0:T(8,128)(2,1)S(1)} %get-tuple-element.37), channel_id=1, source_target_pairs={{0,8},{1,9},{2,10},{3,11},{4,12},{5,13},{6,14},{7,15},{8,0},{9,1},... | collective-permute-start | bytes 110600 | tf_op jit(solution)/shard_map/ppermute | solution.py:416
  39.9 1.4 %collective-permute-done.6 = bf16[144,128]{1,0:T(8,128)(2,1)S(1)} collective-permute-done((bf16[144,128]{1,0:T(8,128)(2,1)S(1)}, bf16[144,128]{1,0:T(8,128)(2,1)S(1)}, u32[]{:S(2)}, u32[]{:S(2)}) %collective-permute-start.6) | collective-permute-done | bytes 36896 | tf_op jit(solution)/shard_map/ppermute | solution.py:416
  41.3 2.0 %collective-permute-done.7 = bf16[144,128]{1,0:T(8,128)(2,1)S(1)} collective-permute-done((bf16[144,128]{1,0:T(8,128)(2,1)S(1)}, bf16[144,128]{1,0:T(8,128)(2,1)S(1)}, u32[]{:S(2)}, u32[]{:S(2)}) %collective-permute-start.7) | collective-permute-done | bytes 36896 | tf_op jit(solution)/shard_map/ppermute | solution.py:416
  43.3 1.2 %collective-permute-done.8 = bf16[144,128]{1,0:T(8,128)(2,1)S(1)} collective-permute-done((bf16[144,128]{1,0:T(8,128)(2,1)S(1)}, bf16[144,128]{1,0:T(8,128)(2,1)S(1)}, u32[]{:S(2)}, u32[]{:S(2)}) %collective-permute-start.8) | collective-permute-done | bytes 36896 | tf_op jit(solution)/shard_map/ppermute | solution.py:416
  44.5 0.0 copy-start.11
  44.5 0.1 collective-permute-start.9
  44.6 0.0 copy-done.3
  44.6 1.5 %feature.1 = f32[128,512]{1,0:T(8,128)} custom-call(bf16[128,512]{1,0:T(8,128)(2,1)S(1)} %bitcast.36, bf16[128,768]{1,0:T(8,128)(2,1)S(1)} %get-tuple-element.25.projected_ref, bf16[128,64]{1,0:T(8,128)(2,1)S(1)} %get-tuple-element.26.delta_ref, bf16[64,768]{1,0:T(8,128)(2,1)S(1)} %copy-done.5, bf16[512,768]{1,0:T(8,128)(2,1)S(1)} %copy-done.1), custom_call_target="tpu_custom_call" | custom-call | flops 113246208 | bytes 786432 | tf_op jit(solution)/shard_map/feature/pallas_call | solution.py:387
  46.1 0.0 collective-permute-done.9.other_ref
  46.1 0.0 copy-done.11
  46.1 0.0 copy-start.12
  46.1 0.6 %copy-done.12 = bf16[144,128]{1,0:T(8,128)(2,1)} copy-done((bf16[144,128]{1,0:T(8,128)(2,1)}, bf16[144,128]{1,0:T(8,128)(2,1)S(1)}, u32[]{:S(2)}) %copy-start.12) | copy-done | bytes 36888
  46.7 1.5 %unpack.1 = (f32[4,768]{1,0:T(4,128)}, f32[20,128]{1,0:T(8,128)}, f32[40,256]{1,0:T(8,128)}, f32[80,256]{1,0:T(8,128)}, f32[1,128]{1,0:T(1,128)}) custom-call(bf16[144,128]{1,0:T(8,128)(2,1)} %copy-done.11, bf16[144,128]{1,0:T(8,128)(2,1)} %copy-done.12, s32[2]{0:T(128)} %copy-done.7), custom_call_target="tpu_custom_call" | custom-call | tf_op jit(solution)/shard_map/unpack/pallas_call | solution.py:427
  48.2 1.1 %slice_bitcast_fusion.9 = f32[48]{0:T(128)} fusion(f32[1,128]{1,0:T(1,128)} %get-tuple-element.32), kind=kLoop, calls=%fused_computation.20 | loop fusion | bytes 384 | tf_op jit(solution)/shard_map/squeeze | solution.py:435
  (4 shorter events, 0.1 us)
Async XLA Ops:
  0.6 12.3 %copy-start.6 = (f32[1,128]{1,0:T(1,128)S(1)}, f32[1,128]{1,0:T(1,128)}, u32[]{:S(2)}) copy-start(f32[1,128]{1,0:T(1,128)} %cot_ref.3) | copy-start | bytes 1540
  0.6 12.3 %copy-start.5 = (bf16[64,768]{1,0:T(8,128)(2,1)S(1)}, bf16[64,768]{1,0:T(8,128)(2,1)}, u32[]{:S(2)}) copy-start(bf16[64,768]{1,0:T(8,128)(2,1)} %squeeze_ref.5) | copy-start | bytes 294916
  0.7 12.3 %copy-start.10 = (bf16[320,128]{1,0:T(8,128)(2,1)S(1)}, bf16[320,128]{1,0:T(8,128)(2,1)}, u32[]{:S(2)}) copy-start(bf16[320,128]{1,0:T(8,128)(2,1)} %first_ref.1) | copy-start | bytes 245764
  2.1 10.7 %collective-permute-start = (bf16[32,512]{1,0:T(8,128)(2,1)}, bf16[32,512]{1,0:T(8,128)(2,1)S(1)}, u32[]{:S(2)}, u32[]{:S(2)}) collective-permute-start(bf16[32,512]{1,0:T(8,128)(2,1)} %get-tuple-element.21), channel_id=1, source_target_pairs={{0,1},{1,2},{2,3},{3,4},{4,5},{5,6},{6,7},{7,8},{8,9},{9,10},{10,1... | collective-permute-start | bytes 98312 | tf_op jit(solution)/shard_map/ppermute | solution.py:337
  6.9 6.0 %collective-permute-start.1 = (bf16[32,512]{1,0:T(8,128)(2,1)}, bf16[32,512]{1,0:T(8,128)(2,1)S(1)}, u32[]{:S(2)}, u32[]{:S(2)}) collective-permute-start(bf16[32,512]{1,0:T(8,128)(2,1)} %get-tuple-element.22), channel_id=1, source_target_pairs={{1,0},{2,1},{3,2},{4,3},{5,4},{6,5},{7,6},{8,7},{9,8},{10,9},{11,1... | collective-permute-start | bytes 98312 | tf_op jit(solution)/shard_map/ppermute | solution.py:338
  8.3 12.1 %copy-start.7 = (s32[2]{0:T(128)}, s32[2]{0:T(128)S(1)}, u32[]{:S(2)}) copy-start(s32[2]{0:T(128)S(1)} %pad_add_fusion.place_ref) | copy-start | bytes 28
  9.0 1.1 %copy-start = (bf16[512,768]{1,0:T(8,128)(2,1)S(1)}, bf16[512,768]{1,0:T(8,128)(2,1)}, u32[]{:S(2)}) copy-start(bf16[512,768]{1,0:T(8,128)(2,1)} %projection_ref.5) | copy-start | bytes 2359300
  10.1 0.9 %copy-start.2 = (bf16[1,128,512]{2,1,0:T(8,128)(2,1)S(1)}, bf16[1,128,512]{2,1,0:T(8,128)(2,1)}, u32[]{:S(2)}) copy-start(bf16[1,128,512]{2,1,0:T(8,128)(2,1)} %param.8) | copy-start | bytes 393220
  11.0 0.9 %copy-start.4 = (bf16[64,768]{1,0:T(8,128)(2,1)S(1)}, bf16[64,768]{1,0:T(8,128)(2,1)}, u32[]{:S(2)}) copy-start(bf16[64,768]{1,0:T(8,128)(2,1)} %squeeze_ref.5) | copy-start | bytes 294916
  13.0 1.1 %copy-start.1 = (bf16[512,768]{1,0:T(8,128)(2,1)S(1)}, bf16[512,768]{1,0:T(8,128)(2,1)}, u32[]{:S(2)}) copy-start(bf16[512,768]{1,0:T(8,128)(2,1)} %projection_ref.5) | copy-start | bytes 2359300
  14.1 1.1 %copy-start.8 = (bf16[1280,256]{1,0:T(8,128)(2,1)S(1)}, bf16[1280,256]{1,0:T(8,128)(2,1)}, u32[]{:S(2)}) copy-start(bf16[1280,256]{1,0:T(8,128)(2,1)} %third_ref.1) | copy-start | bytes 1966084
  15.2 1.0 %copy-start.9 = (bf16[640,256]{1,0:T(8,128)(2,1)S(1)}, bf16[640,256]{1,0:T(8,128)(2,1)}, u32[]{:S(2)}) copy-start(bf16[640,256]{1,0:T(8,128)(2,1)} %second_ref.1) | copy-start | bytes 983044
  20.4 2.1 %collective-permute-start.2 = (bf16[4,4,144,128]{3,2,1,0:T(8,128)(2,1)S(1)}, bf16[4,4,144,128]{3,2,1,0:T(8,128)(2,1)S(1)}, u32[]{:S(2)}, u32[]{:S(2)}) collective-permute-start(bf16[4,4,144,128]{3,2,1,0:T(8,128)(2,1)S(1)} %slice_bitcast_fusion), channel_id=1, source_target_pairs={{0,16},{16,0},{1,17},{17,1},{2,18},{18,2},{3,19},{19,3},{4,20},{20... | collective-permute-start | bytes 1769480 | tf_op jit(solution)/shard_map/ppermute | solution.py:413
  22.6 22.0 %copy-start.3 = (bf16[1,128,512]{2,1,0:T(8,128)(2,1)S(1)}, bf16[1,128,512]{2,1,0:T(8,128)(2,1)}, u32[]{:S(2)}) copy-start(bf16[1,128,512]{2,1,0:T(8,128)(2,1)} %param.8) | copy-start | bytes 393220
  22.7 9.0 %collective-permute-start.3 = (bf16[4,144,128]{2,1,0:T(8,128)(2,1)S(1)}, bf16[4,144,128]{2,1,0:T(8,128)(2,1)S(1)}, u32[]{:S(2)}, u32[]{:S(2)}) collective-permute-start(bf16[4,144,128]{2,1,0:T(8,128)(2,1)S(1)} %get-tuple-element.33), channel_id=1, source_target_pairs={{0,3},{1,2},{2,1},{3,0},{4,7},{5,6},{6,5},{7,4},{8,11},{9,10},{10,... | collective-permute-start | bytes 442376 | tf_op jit(solution)/shard_map/ppermute | solution.py:416
  27.1 7.7 %collective-permute-start.4 = (bf16[4,144,128]{2,1,0:T(8,128)(2,1)S(1)}, bf16[4,144,128]{2,1,0:T(8,128)(2,1)S(1)}, u32[]{:S(2)}, u32[]{:S(2)}) collective-permute-start(bf16[4,144,128]{2,1,0:T(8,128)(2,1)S(1)} %get-tuple-element.35), channel_id=1, source_target_pairs={{0,1},{1,0},{2,3},{3,2},{4,5},{5,4},{6,7},{7,6},{8,9},{9,8},{10,11... | collective-permute-start | bytes 442376 | tf_op jit(solution)/shard_map/ppermute | solution.py:416
  27.7 7.1 %collective-permute-start.5 = (bf16[4,144,128]{2,1,0:T(8,128)(2,1)S(1)}, bf16[4,144,128]{2,1,0:T(8,128)(2,1)S(1)}, u32[]{:S(2)}, u32[]{:S(2)}) collective-permute-start(bf16[4,144,128]{2,1,0:T(8,128)(2,1)S(1)} %get-tuple-element.34), channel_id=1, source_target_pairs={{0,2},{1,3},{2,0},{3,1},{4,6},{5,7},{6,4},{7,5},{8,10},{9,11},{10,... | collective-permute-start | bytes 442376 | tf_op jit(solution)/shard_map/ppermute | solution.py:416
  34.8 6.5 %collective-permute-start.6 = (bf16[144,128]{1,0:T(8,128)(2,1)S(1)}, bf16[144,128]{1,0:T(8,128)(2,1)S(1)}, u32[]{:S(2)}, u32[]{:S(2)}) collective-permute-start(bf16[144,128]{1,0:T(8,128)(2,1)S(1)} %get-tuple-element.36), channel_id=1, source_target_pairs={{0,12},{1,13},{2,14},{3,15},{4,8},{5,9},{6,10},{7,11},{8,4},{9,5},... | collective-permute-start | bytes 110600 | tf_op jit(solution)/shard_map/ppermute | solution.py:416
  39.3 4.0 %collective-permute-start.7 = (bf16[144,128]{1,0:T(8,128)(2,1)S(1)}, bf16[144,128]{1,0:T(8,128)(2,1)S(1)}, u32[]{:S(2)}, u32[]{:S(2)}) collective-permute-start(bf16[144,128]{1,0:T(8,128)(2,1)S(1)} %get-tuple-element.38), channel_id=1, source_target_pairs={{0,4},{1,5},{2,6},{3,7},{4,0},{5,1},{6,2},{7,3},{8,12},{9,13},{10,... | collective-permute-start | bytes 110600 | tf_op jit(solution)/shard_map/ppermute | solution.py:416
  39.3 5.2 %collective-permute-start.8 = (bf16[144,128]{1,0:T(8,128)(2,1)S(1)}, bf16[144,128]{1,0:T(8,128)(2,1)S(1)}, u32[]{:S(2)}, u32[]{:S(2)}) collective-permute-start(bf16[144,128]{1,0:T(8,128)(2,1)S(1)} %get-tuple-element.37), channel_id=1, source_target_pairs={{0,8},{1,9},{2,10},{3,11},{4,12},{5,13},{6,14},{7,15},{8,0},{9,1},... | collective-permute-start | bytes 110600 | tf_op jit(solution)/shard_map/ppermute | solution.py:416
  44.5 1.6 %copy-start.11 = (bf16[144,128]{1,0:T(8,128)(2,1)}, bf16[144,128]{1,0:T(8,128)(2,1)S(1)}, u32[]{:S(2)}) copy-start(bf16[144,128]{1,0:T(8,128)(2,1)S(1)} %fusion.6.mine_ref) | copy-start | bytes 110596
  44.5 1.5 %collective-permute-start.9 = (bf16[144,128]{1,0:T(8,128)(2,1)S(1)}, bf16[144,128]{1,0:T(8,128)(2,1)S(1)}, u32[]{:S(2)}, u32[]{:S(2)}) collective-permute-start(bf16[144,128]{1,0:T(8,128)(2,1)S(1)} %fusion.6.mine_ref), channel_id=1, source_target_pairs={{0,16},{16,0},{1,17},{17,1},{2,18},{18,2},{3,19},{19,3},{4,20},{20... | collective-permute-start | bytes 110600 | tf_op jit(solution)/shard_map/ppermute | solution.py:419
  46.1 0.6 %copy-start.12 = (bf16[144,128]{1,0:T(8,128)(2,1)}, bf16[144,128]{1,0:T(8,128)(2,1)S(1)}, u32[]{:S(2)}) copy-start(bf16[144,128]{1,0:T(8,128)(2,1)S(1)} %collective-permute-done.9.other_ref) | copy-start | bytes 110596

commit v2 on v1

--- a/solution.py
+++ b/solution.py
@@ -13,7 +13,10 @@
 C2 = 256
 HK = 5
 PK = 3
-EDGE = 16
+EDGE = 32
+REACH = 12
+MORE = 16
+BACK = 16
 LANES = 128
 
 EPSILON = 1e-05
@@ -58,25 +61,39 @@
     return projected, hidden, dot(hidden, squeeze, NT)
 
 
-def edges_kernel(first_ref, last_ref, cot_ref, up_ref, down_ref):
-    cot = cot_ref[...]
+def edge_kernel(rows_ref, cot_ref, out_ref, cot_held, sems):
+    frames = rows_ref.shape[0]
+    copies = [
+        pltpu.make_async_copy(cot_ref, cot_held, sems.at[0]),
+        pltpu.make_async_copy(rows_ref.at[frames - EDGE :], out_ref.at[:EDGE], sems.at[1]),
+    ]
+    for copy in copies:
+        copy.start()
+    copies[0].wait()
+    cot = cot_held[...]
     high = cot.astype(BF16).astype(F32)
     middle = (cot - high).astype(BF16).astype(F32)
     low = cot - high - middle
-    stack = jnp.concatenate([high, middle, low, jnp.zeros((EDGE - 3, cot.shape[1]), F32)], axis=0).astype(BF16)
-    rest = jnp.zeros((EDGE, first_ref.shape[1] - cot.shape[1]), BF16)
-    extra = jnp.concatenate([stack, rest], axis=1)
-    up_ref[:EDGE, :] = last_ref[...]
-    up_ref[EDGE:, :] = extra
-    down_ref[:EDGE, :] = first_ref[...]
-    down_ref[EDGE:, :] = extra
-
-
-def project_kernel(rows_ref, projection_ref, squeeze_ref, projected_ref, hidden_ref, squeezed_ref):
-    projected, hidden, squeezed = forward_rows(rows_ref[...], projection_ref[...], squeeze_ref[...])
+    stack = jnp.concatenate([high, middle, low, jnp.zeros((MORE - 3, frames), F32)], axis=0)
+    out_ref[EDGE:, :frames] = stack.astype(BF16)
+    out_ref[EDGE:, frames:] = jnp.zeros((MORE, out_ref.shape[1] - frames), BF16)
+    copies[1].wait()
+
+
+def project_kernel(count, *refs):
+    sources, held = refs[:count], refs[count : 2 * count]
+    projected_ref, hidden_ref, squeezed_ref, sems = refs[2 * count :]
+    copies = [pltpu.make_async_copy(a, b, sems.at[i]) for i, (a, b) in enumerate(zip(sources, held))]
+    for copy in copies:
+        copy.start()
+    for copy in copies[:3]:
+        copy.wait()
+    projected, hidden, squeezed = forward_rows(held[0][...], held[1][...], held[2][...])
     projected_ref[...] = projected
     hidden_ref[...] = hidden
     squeezed_ref[...] = squeezed
+    for copy in copies[3:]:
+        copy.wait()
 
 
 def shifted(values, taps, sign):
@@ -106,8 +123,7 @@
     packed,
     place_ref,
     squeezed_ref,
-    low_ref,
-    high_ref,
+    edge_ref,
     cot_ref,
     hidden_ref,
     projection_ref,
@@ -117,65 +133,68 @@
     third_ref,
     final_ref,
     scores_ref,
+    before_ref,
     delta_ref,
+    edge_projected_ref,
     *outs,
 ):
     frames = squeezed_ref.shape[0]
-    total = frames + 2 * EDGE
-    own = slice(EDGE, EDGE + frames)
+    total = EDGE + frames
     seq, core = place_ref[0], place_ref[1]
     row = lax.broadcasted_iota(jnp.int32, (total, LANES), 0)
-    inside = ((row >= EDGE) | (seq > 0)) & ((row < EDGE + frames) | (seq < n - 1))
-
-    def mask(values):
+    inside = (row >= EDGE - 2 * REACH) & ((row >= EDGE) | (seq > 0))
+    window = inside & (row >= EDGE - REACH) & ((row < total - REACH) | (seq == n - 1))
+
+    def mask(values, where):
         width = values.shape[1]
         if width <= LANES:
-            return jnp.where(inside[:, :width], values, 0.0)
+            return jnp.where(where[:, :width], values, 0.0)
         return jnp.concatenate(
-            [jnp.where(inside, values[:, i : i + LANES], 0.0) for i in range(0, width, LANES)], axis=1
+            [jnp.where(where, values[:, i : i + LANES], 0.0) for i in range(0, width, LANES)], axis=1
         )
 
-    edge = jnp.concatenate([low_ref[:EDGE, :], high_ref[:EDGE, :]], axis=0)
-    _, _, edge_squeezed = forward_rows(edge, projection_ref[...], squeeze_ref[...])
-    squeezed = jnp.concatenate([edge_squeezed[:EDGE], squeezed_ref[...], edge_squeezed[EDGE:]], axis=0)
-
-    def joined(ref):
-        parts = ref[EDGE:, :LANES].astype(F32)
-        return parts[0:1] + parts[1:2] + parts[2:3]
-
-    rows = [cot_ref[...], joined(low_ref), joined(high_ref), jnp.zeros((5, LANES), F32)]
-    columns = jnp.concatenate(rows, axis=0).T
+    edge_projected, edge_hidden, edge_squeezed = forward_rows(
+        edge_ref[:EDGE, :], projection_ref[...], squeeze_ref[...]
+    )
+    edge_projected_ref[...] = edge_projected[EDGE - BACK :]
+    squeezed = jnp.concatenate([edge_squeezed, squeezed_ref[...]], axis=0)
+
+    parts = edge_ref[EDGE:, :LANES].astype(F32)
+    parts = parts[0:1] + parts[1:2] + parts[2:3]
+    columns = jnp.concatenate([cot_ref[...], parts, jnp.zeros((6, LANES), F32)], axis=0).T
     cot = jnp.concatenate(
         [
             jnp.broadcast_to(columns[frames - EDGE :, 1:2], (EDGE, LANES)),
             jnp.broadcast_to(columns[:, 0:1], (frames, LANES)),
-            jnp.broadcast_to(columns[:EDGE, 2:3], (EDGE, LANES)),
         ],
         axis=0,
     )
+    cot = mask(cot, inside)
 
     weights = (first_ref, second_ref, third_ref)
     act = squeezed
     inputs, slopes = [], []
     for ref in weights:
         unit, slope = leaky_pair(act)
-        unit = mask(unit)
+        unit = mask(unit, inside)
         slopes.append(slope)
-        inputs.append(unit[own].astype(BF16))
+        inputs.append(mask(unit, window).astype(BF16))
         width = unit.shape[1]
         act = jnp.zeros((total, ref.shape[1]), F32)
         for k, piece in enumerate(shifted(unit, HK, 1)):
             act = act + dot(piece, ref[k * width : (k + 1) * width, :])
     unit, slope = leaky_pair(act)
-    final_in = mask(unit).astype(BF16).astype(F32)
+    final_in = mask(unit, inside).astype(BF16).astype(F32)
     taps = shifted(final_in, PK, 1)
-    scores = jnp.zeros((1, frames), F32)
-    for k in range(PK):
-        scores = scores + dot(final_ref[:, k * C2 : (k + 1) * C2], taps[k][own], NT)
-    scores_ref[...] = scores
+    for ref, rows in ((scores_ref, slice(EDGE, total)), (before_ref, slice(0, LANES))):
+        scores = jnp.zeros((1, rows.stop - rows.start), F32)
+        for k in range(PK):
+            scores = scores + dot(final_ref[:, k * C2 : (k + 1) * C2], taps[k][rows], NT)
+        ref[...] = scores
 
     upstream = [jnp.zeros((total, LANES), F32)] * (C2 // LANES)
     final_grad = []
+    final_in = mask(final_in, window)
     for k in range(PK):
         amount = (k - 1) % total
         moved = cot if amount == 0 else pltpu.roll(cot, amount, 0)
@@ -183,25 +202,25 @@
             lanes = slice(k * C2 + h * LANES, k * C2 + (h + 1) * LANES)
             upstream[h] = upstream[h] + moved * final_ref[:, lanes].astype(F32)
             final_grad.append(
-                jnp.sum(moved[own] * final_in[own, h * LANES : (h + 1) * LANES], axis=0, keepdims=True)
+                jnp.sum(moved * final_in[:, h * LANES : (h + 1) * LANES], axis=0, keepdims=True)
             )
     upstream = jnp.concatenate(upstream, axis=1)
     slopes.append(slope)
     grads = []
     for layer in (2, 1, 0):
-        delta = mask(upstream * slopes[layer + 1])
+        delta = mask(upstream * slopes[layer + 1], inside)
         pieces = shifted(delta, HK, -1)
-        near = jnp.concatenate([p[own] for p in pieces], axis=1)
-        grads.append(dot(inputs[layer], near, TN))
+        grads.append(dot(inputs[layer], jnp.concatenate(pieces, axis=1), TN))
         ref = weights[layer]
         width = ref.shape[0] // HK
         upstream = jnp.zeros((total, width), F32)
         for k, piece in enumerate(pieces):
             upstream = upstream + dot(piece, ref[k * width : (k + 1) * width, :], NT)
     third, second, first = grads
-    delta = (upstream[own] * slopes[0][own]).astype(BF16)
-    delta_ref[...] = delta
-    squeeze_grad = dot(delta, hidden_ref[...], TN)
+    delta = mask(upstream * slopes[0], inside)
+    delta_ref[...] = delta[EDGE - BACK :].astype(BF16)
+    hidden = jnp.concatenate([edge_hidden, hidden_ref[...]], axis=0)
+    squeeze_grad = dot(mask(delta, window).astype(BF16), hidden, TN)
 
     if not packed:
         squeeze_out, first_out, second_out, third_out, final_out = outs
@@ -265,13 +284,33 @@
         put(s, 0, scratch[s].astype(BF16))
 
 
-def feature_kernel(rows_ref, projected_ref, delta_ref, squeeze_ref, projection_ref, out_ref):
+def feature_kernel(
+    rows_ref, edge_ref, projected_ref, edge_projected_ref, delta_ref, before_ref, squeeze_ref, projection_ref, out_ref, back_ref
+):
     hidden_upstream = dot(delta_ref[...], squeeze_ref[...])
-    hidden_normed, hidden_inverse = normalize(projected_ref[...].astype(F32))
+    projected = jnp.concatenate([edge_projected_ref[...], projected_ref[...]], axis=0)
+    hidden_normed, hidden_inverse = normalize(projected.astype(F32))
     projected_grad = normalize_back(hidden_upstream, hidden_normed, hidden_inverse).astype(BF16)
     normed_grad = dot(projected_grad, projection_ref[...], NT)
-    normed, inverse = normalize(rows_ref[...].astype(F32))
-    out_ref[...] = normalize_back(normed_grad, normed, inverse)
+    rows = jnp.concatenate([edge_ref[EDGE - BACK : EDGE, :], rows_ref[...]], axis=0)
+    normed, inverse = normalize(rows.astype(F32))
+    grad = normalize_back(normed_grad, normed, inverse)
+    out_ref[...] = grad[BACK:]
+    back_ref[:BACK, :] = grad[:BACK]
+    back_ref[BACK:, :LANES] = jnp.broadcast_to(before_ref[...], (8, LANES))
+    back_ref[BACK:, LANES:] = jnp.zeros((8, back_ref.shape[1] - LANES), F32)
+
+
+def assemble_kernel(n, place_ref, own_ref, scores_ref, back_ref, grad_ref, final_scores_ref):
+    frames = own_ref.shape[0]
+    last = place_ref[0] == n - 1
+    grad_ref[: frames - BACK, :] = own_ref[: frames - BACK, :]
+    row = lax.broadcasted_iota(jnp.int32, (BACK, own_ref.shape[1]), 0)
+    keep = last | (row < BACK - REACH)
+    grad_ref[frames - BACK :, :] = jnp.where(keep, own_ref[frames - BACK :, :], back_ref[:BACK, :])
+    moved = pltpu.roll(back_ref[BACK:, :LANES], frames - EDGE, 1)
+    lane = lax.broadcasted_iota(jnp.int32, (1, frames), 1)
+    final_scores_ref[...] = jnp.where(last | (lane < frames - REACH), scores_ref[...], moved[0:1])
 
 
 def unpack_kernel(factor, mine_ref, other_ref, place_ref, squeeze_ref, first_ref, second_ref, third_ref, final_ref, both):
@@ -285,14 +324,23 @@
         for h in range(ref.shape[1] // LANES):
             ref[:, h * LANES : (h + 1) * LANES] = both[base : base + count, :]
             base += count
-    final_ref[...] = both[base : base + 1, :]
+    final_ref[...] = both[base : base + 1, : final_ref.shape[1]]
 
 
 def sds(shape, dtype):
     return jax.ShapeDtypeStruct(shape, dtype)
 
 
+def hbm(array):
+    return pltpu.with_memory_space_constraint(array, pltpu.HBM)
+
+
+def vmem(shape, dtype):
+    return pltpu.VMEM(shape, dtype)
+
+
 VMEM = pl.BlockSpec(memory_space=pltpu.VMEM)
+HBM = pl.BlockSpec(memory_space=pltpu.HBM)
 SMEM = pl.BlockSpec(memory_space=pltpu.SMEM)
 
 
@@ -322,30 +370,40 @@
     rows = features.reshape(frames, feat)
     place = jnp.stack([seq, core]).astype(jnp.int32)
 
-    up, down = pl.pallas_call(
-        edges_kernel,
-        grid=(1,),
-        in_specs=[
-            pl.BlockSpec((EDGE, feat), lambda i: (0, 0)),
-            pl.BlockSpec((EDGE, feat), lambda i: (frames // EDGE - 1, 0)),
-            pl.BlockSpec((1, frames), lambda i: (0, 0)),
+    edge = pl.pallas_call(
+        edge_kernel,
+        in_specs=[HBM, HBM],
+        out_specs=VMEM,
+        out_shape=vmem((EDGE + MORE, feat), BF16),
+        scratch_shapes=[pltpu.VMEM((1, frames), F32), pltpu.SemaphoreType.DMA((2,))],
+        name="edge",
+    )(hbm(rows), hbm(score_cotangent))
+    edge = lax.ppermute(edge, "seq", [(i, i + 1) for i in range(n - 1)])
+
+    sources = (
+        rows,
+        projection_weight,
+        squeeze_weight,
+        score_cotangent,
+        first_weight,
+        second_weight,
+        third_weight,
+    )
+    rows, projection, squeeze, cot, first, second, third, projected, hidden, squeezed = pl.pallas_call(
+        functools.partial(project_kernel, len(sources)),
+        in_specs=[HBM] * len(sources),
+        out_specs=[VMEM] * (len(sources) + 3),
+        out_shape=[
+            *[vmem(a.shape, a.dtype) for a in sources],
+            vmem((frames, width), BF16),
+            vmem((frames, width), BF16),
+            vmem((frames, C0), F32),
         ],
-        out_specs=[pl.BlockSpec((2 * EDGE, feat), lambda i: (0, 0))] * 2,
-        out_shape=[sds((2 * EDGE, feat), BF16)] * 2,
-        name="edges",
-    )(rows, rows, score_cotangent)
-    low = lax.ppermute(up, "seq", [(i, i + 1) for i in range(n - 1)])
-    high = lax.ppermute(down, "seq", [(i + 1, i) for i in range(n - 1)])
-
-    projected, hidden, squeezed = pl.pallas_call(
-        project_kernel,
-        in_specs=[VMEM] * 3,
-        out_specs=[VMEM] * 3,
-        out_shape=[sds((frames, width), BF16), sds((frames, width), BF16), sds((frames, C0), F32)],
-        compiler_params=params(16),
+        scratch_shapes=[pltpu.SemaphoreType.DMA((len(sources),))],
+        compiler_params=params(8),
         cost_estimate=cost(2 * frames * width * (feat + C0), 2 * feat * width),
         name="project",
-    )(rows, projection_weight, squeeze_weight)
+    )(*[hbm(a) for a in sources])
 
     if packed:
         half = 144
@@ -360,39 +418,56 @@
             sds((1, PK * C2), F32),
         ]
         scratch = []
-    scores, delta, *grads = pl.pallas_call(
+    own_scores, before, delta, edge_projected, *grads = pl.pallas_call(
         functools.partial(head_kernel, n, packed),
-        in_specs=[SMEM] + [VMEM] * 11,
-        out_specs=[VMEM] * (2 + len(grad_shapes)),
-        out_shape=[sds((1, frames), F32), sds((frames, C0), BF16), *grad_shapes],
+        in_specs=[SMEM] + [VMEM] * 10,
+        out_specs=[VMEM] * (4 + len(grad_shapes)),
+        out_shape=[
+            sds((1, frames), F32),
+            sds((1, LANES), F32),
+            sds((BACK + frames, C0), BF16),
+            sds((BACK, width), BF16),
+            *grad_shapes,
+        ],
         scratch_shapes=scratch,
-        compiler_params=params(32),
+        compiler_params=params(20),
         cost_estimate=cost(10**9, 4 * 10**6),
         name="head",
     )(
         place,
         squeezed,
-        low,
-        high,
-        score_cotangent,
+        edge,
+        cot,
         hidden,
-        projection_weight,
-        squeeze_weight,
-        first_weight,
-        second_weight,
-        third_weight,
+        projection,
+        squeeze,
+        first,
+        second,
+        third,
         final_weight.reshape(1, PK * C2),
     )
 
-    feature_grad = pl.pallas_call(
-        feature_kernel,
-        in_specs=[VMEM] * 5,
-        out_specs=VMEM,
-        out_shape=sds((frames, feat), F32),
-        compiler_params=params(16),
-        cost_estimate=cost(2 * frames * width * (feat + C0), 2 * feat * width),
-        name="feature",
-    )(rows, projected, delta, squeeze_weight, projection_weight)
+    def features_back():
+        own_grad, back = pl.pallas_call(
+            feature_kernel,
+            in_specs=[VMEM] * 8,
+            out_specs=[VMEM] * 2,
+            out_shape=[sds((frames, feat), F32), sds((BACK + 8, feat), F32)],
+            compiler_params=params(8),
+            cost_estimate=cost(2 * frames * width * (feat + C0), 2 * feat * width),
+            name="feature",
+        )(rows, edge, projected, edge_projected, delta, before, squeeze, projection)
+        back = lax.ppermute(back, "seq", [(i + 1, i) for i in range(n - 1)])
+        feature_grad, scores = pl.pallas_call(
+            functools.partial(assemble_kernel, n),
+            in_specs=[SMEM] + [VMEM] * 3,
+            out_specs=[VMEM] * 2,
+            out_shape=[sds((frames, feat), F32), sds((1, frames), F32)],
+            compiler_params=params(4),
+            cost_estimate=cost(frames * feat, 8 * frames * feat),
+            name="assemble",
+        )(place, own_grad, own_scores, back)
+        return feature_grad[None], scores
 
     factor = 1.0 / math.sqrt(cores * n * frames)
     if not packed:
@@ -400,7 +475,8 @@
         for term in grads[:4] + [grads[4].reshape(PK * C2)]:
             part = lax.psum_scatter(term * factor, "seq", scatter_dimension=0, tiled=True)
             shares.append(lax.psum(part.astype(BF16), "dp").astype(F32))
-        return (scores, feature_grad[None], *shares)
+        feature_grad, scores = features_back()
+        return (scores, feature_grad, *shares)
 
     def added(*terms):
         total = terms[0].astype(F32)
@@ -416,13 +492,16 @@
             lax.ppermute(held[j], "seq", [(i, i ^ (j * stride)) for i in range(n)]) for j in (3, 1, 2)
         ]
         held = added(held[0], *moved)
+        if stride == 1:
+            feature_grad, scores = features_back()
+            held, feature_grad, scores = lax.optimization_barrier((held, feature_grad, scores))
     other = lax.ppermute(held, "dp", swap)
     shapes = [
         (C0 // n, width),
         (HK * C0 // n, C1),
         (HK * C1 // n, C2),
         (HK * C2 // n, C2),
-        (1, LANES),
+        (1, PK * C2 // n),
     ]
     *shares, final = pl.pallas_call(
         functools.partial(unpack_kernel, factor),
@@ -430,9 +509,10 @@
         out_specs=[VMEM] * 5,
         out_shape=[sds(shape, F32) for shape in shapes],
         scratch_shapes=[pltpu.VMEM((2 * half, LANES), F32)],
+        compiler_params=params(4),
         name="unpack",
     )(held, other, place)
-    return (scores, feature_grad[None], *shares, final[0, : PK * C2 // n])
+    return (scores, feature_grad, *shares, final.reshape(PK * C2 // n))
 
 
 def solution(mesh):

time: 49.8 us -> 40.2 us (0.81)
  local copies, waits for them, and re-layouts: 8.67 us -> 0.77 us
  starting transfers between devices: 16.4 us -> 14.4 us
  Pallas kernels: 9.38 us -> 10.4 us
    ppermute x6, waiting for transfers between devices: 11.6 us -> 4.13 us  [shards(): lax.ppermute(held[j], 'seq', [(i, i ^ j * stride) for i in range(n)])]
    unnamed x26 -> x0, local copies, waits for them, and re-layouts: 6.76 us -> none
    ppermute x2, waiting for transfers between devices: 0.19 us -> 6.04 us  [the longest x1 6.04 us: features_back(): back = lax.ppermute(back, 'seq', [(i + 1, i) for i in range(n - 1)])]
    ppermute x6, starting transfers between devices: 10.1 us -> 8.08 us  [shards(): lax.ppermute(held[j], 'seq', [(i, i ^ j * stride) for i in range(n)])]
    pallas_call x3 -> x4, Pallas kernels: 3.69 us -> 4.94 us  [the longest x1 2.11 us: shards(): pl.pallas_call(functools.partial(project_kernel, len(sources)), in_specs=...]
    ppermute x1, waiting for transfers between devices: 0.01 us -> 1.2 us  [shards(): other = lax.ppermute(held, 'dp', swap)]
    squeeze x1 -> x0, local copies, waits for them, and re-layouts: 1.14 us -> none  [shards(): return (scores, feature_grad[None], *shares, final[0, :PK * C2 // n])]
  transfers between devices with their start and end apart: 10 -> 10, of which waited for: 7 -> 5; matrix products, arithmetic and copies ran while one was open for 2% -> 2% of each run, Pallas kernels for 5% -> 10%
where the time goes in v2:
time: 40.2 us; the launch traced here: 40 us
  starting transfers between devices  14.4 us (36%)
  waiting for transfers between devices  13.4 us (33%)
  Pallas kernels  10.4 us (26%)
  local copies, waits for them, and re-layouts  0.77 us (2%)
  between operations  0.76 us (2%)
    ppermute x6, starting transfers between devices, shards(): lax.ppermute(held[j], 'seq', [(i, i ^ j * stride) for i in range(n)])  8.08 us
    ppermute x1, waiting for transfers between devices, features_back(): back = lax.ppermute(back, 'seq', [(i + 1, i) for i in range(n - 1)])  6.04 us
    ppermute x1, starting transfers between devices, shards(): edge = lax.ppermute(edge, 'seq', [(i, i + 1) for i in range(n - 1)])  4.84 us
    pallas_call x1, Pallas kernels, shards(): pl.pallas_call(functools.partial(head_kernel, n, packed), in_specs=[SMEM]...  4.21 us
    ppermute x6, waiting for transfers between devices, shards(): lax.ppermute(held[j], 'seq', [(i, i ^ j * stride) for i in range(n)])  4.13 us
    pallas_call x1, Pallas kernels, shards(): pl.pallas_call(functools.partial(project_kernel, len(sources)), in_specs=...  2.11 us
    ppermute x1, waiting for transfers between devices, shards(): held = added(payload[0], lax.ppermute(payload[1], 'dp', swap))  1.99 us
    ppermute x1, starting transfers between devices, features_back(): back = lax.ppermute(back, 'seq', [(i + 1, i) for i in range(n - 1)])  1.29 us
  transfers between devices with their start and end apart: 10, of which 5 were waited for; matrix products, arithmetic and copies ran while one was open for 2% of the time, Pallas kernels for 10%

profile of v2, /device:TPU:0, one launch (start us, length us, event | category | flops | bytes accessed | tf_op | source)
XLA Modules:
  0.0 40.0 jit_solution(13518077917454681946)
XLA Ops:
  0.6 0.8 %edge.1 = bf16[48,512]{1,0:T(8,128)(2,1)S(1)} custom-call(bf16[128,512]{1,0:T(8,128)(2,1)} %bitcast.30, f32[1,128]{1,0:T(1,128)} %cot_ref.1), custom_call_target="tpu_custom_call" | custom-call | tf_op jit(solution)/shard_map/edge/pallas_call | solution.py:373
  1.4 4.8 %collective-permute-start = (bf16[48,512]{1,0:T(8,128)(2,1)S(1)}, bf16[48,512]{1,0:T(8,128)(2,1)S(1)}, u32[]{:S(2)}, u32[]{:S(2)}) collective-permute-start(bf16[48,512]{1,0:T(8,128)(2,1)S(1)} %edge.1), channel_id=1, source_target_pairs={{0,1},{1,2},{2,3},{3,4},{4,5},{5,6},{6,7},{7,8},{8,9},{9,10},{10,1... | collective-permute-start | bytes 147464 | tf_op jit(solution)/shard_map/ppermute | solution.py:381
  6.3 0.1 pad_add_fusion.place_ref
  6.4 0.7 %reshape.30.final_ref = bf16[1,768]{1,0:T(2,128)(2,1)S(1)} reshape(bf16[768]{0:T(1024)(128)(2,1)} %param.15) | data formatting | bytes 3072 | tf_op jit(solution)/shard_map/reshape | solution.py:447
  7.1 2.1 %project.1 = (bf16[128,512]{1,0:T(8,128)(2,1)S(1)}, bf16[512,768]{1,0:T(8,128)(2,1)S(1)}, bf16[64,768]{1,0:T(8,128)(2,1)S(1)}, f32[1,128]{1,0:T(1,128)S(1)}, bf1...) custom-call(bf16[128,512]{1,0:T(8,128)(2,1)} %bitcast.31, ...), custom_call_target="tpu_custom_call" | custom-call | flops 113246208 | bytes 786432 | tf_op jit(solution)/shard_map/project/pallas_call | solution.py:392
  9.2 0.0 collective-permute-done.edge_ref
  9.2 4.2 %head.1 = (f32[1,128]{1,0:T(1,128)S(1)}, f32[1,128]{1,0:T(1,128)S(1)}, bf16[144,64]{1,0:T(8,128)(2,1)S(1)}, bf16[16,768]{1,0:T(8,128)(2,1)S(1)}, bf16[2,4,4,144,128]{4,3,2,1,0:T(8,128)(2,1)S(1)}) custom-call(s32[2]{0:T(128)S(1)} %pad_add_fusion.place_ref, f32[128,64]{1,0:T(8,128)S(1)} %get-tuple-element.34.squeezed_ref, ...), custom_call_target="tpu_custom_call" | custom-call | flops 1000000000 | bytes 4000000 | tf_op jit(solution)/shard_map/head/pallas_call | solution.py:421
  13.4 0.1 collective-permute-start.1
  13.5 2.0 %collective-permute-done.1 = bf16[4,4,144,128]{3,2,1,0:T(8,128)(2,1)S(1)} collective-permute-done((bf16[4,4,144,128]{3,2,1,0:T(8,128)(2,1)S(1)}, bf16[4,4,144,128]{3,2,1,0:T(8,128)(2,1)S(1)}, u32[]{:S(2)}, u32[]{:S(2)}) %collective-permute-start.1) | collective-permute-done | bytes 589856 | tf_op jit(solution)/shard_map/ppermute | solution.py:489
  15.5 0.2 fusion
  15.7 2.5 %collective-permute-start.2 = (bf16[4,144,128]{2,1,0:T(8,128)(2,1)S(1)}, bf16[4,144,128]{2,1,0:T(8,128)(2,1)S(1)}, u32[]{:S(2)}, u32[]{:S(2)}) collective-permute-start(bf16[4,144,128]{2,1,0:T(8,128)(2,1)S(1)} %get-tuple-element.61), channel_id=1, source_target_pairs={{0,3},{1,2},{2,1},{3,0},{4,7},{5,6},{6,5},{7,4},{8,11},{9,10},{10,... | collective-permute-start | bytes 442376 | tf_op jit(solution)/shard_map/ppermute | solution.py:492
  18.2 0.5 %collective-permute-start.4 = (bf16[4,144,128]{2,1,0:T(8,128)(2,1)S(1)}, bf16[4,144,128]{2,1,0:T(8,128)(2,1)S(1)}, u32[]{:S(2)}, u32[]{:S(2)}) collective-permute-start(bf16[4,144,128]{2,1,0:T(8,128)(2,1)S(1)} %get-tuple-element.62), channel_id=1, source_target_pairs={{0,2},{1,3},{2,0},{3,1},{4,6},{5,7},{6,4},{7,5},{8,10},{9,11},{10,... | collective-permute-start | bytes 442376 | tf_op jit(solution)/shard_map/ppermute | solution.py:492
  18.7 0.6 %collective-permute-start.3 = (bf16[4,144,128]{2,1,0:T(8,128)(2,1)S(1)}, bf16[4,144,128]{2,1,0:T(8,128)(2,1)S(1)}, u32[]{:S(2)}, u32[]{:S(2)}) collective-permute-start(bf16[4,144,128]{2,1,0:T(8,128)(2,1)S(1)} %get-tuple-element.63), channel_id=1, source_target_pairs={{0,1},{1,0},{2,3},{3,2},{4,5},{5,4},{6,7},{7,6},{8,9},{9,8},{10,11... | collective-permute-start | bytes 442376 | tf_op jit(solution)/shard_map/ppermute | solution.py:492
  19.3 0.8 %feature.1 = (f32[128,512]{1,0:T(8,128)S(1)}, f32[24,512]{1,0:T(8,128)S(1)}) custom-call(bf16[128,512]{1,0:T(8,128)(2,1)S(1)} %get-tuple-element.43.rows_ref, bf16[48,512]{1,0:T(8,128)(2,1)S(1)} %collective-permute-done.edge_ref, bf16[128,768]{1,0:T(8,128)(2,1)S(1)} %get-tuple-element.44.projected_ref, ...), custom_call_target="tpu_custom_call" | custom-call | flops 113246208 | bytes 786432 | tf_op jit(solution)/shard_map/feature/pallas_call | solution.py:451
  20.1 1.3 %collective-permute-start.5 = (f32[24,512]{1,0:T(8,128)S(1)}, f32[24,512]{1,0:T(8,128)S(1)}, u32[]{:S(2)}, u32[]{:S(2)}) collective-permute-start(f32[24,512]{1,0:T(8,128)S(1)} %get-tuple-element.50), channel_id=1, source_target_pairs={{1,0},{2,1},{3,2},{4,3},{5,4},{6,5},{7,6},{8,7},{9,8},{10,9},{11,1... | collective-permute-start | bytes 147464 | tf_op jit(solution)/shard_map/ppermute | solution.py:460
  21.4 6.0 %collective-permute-done.5.back_ref = f32[24,512]{1,0:T(8,128)S(1)} collective-permute-done((f32[24,512]{1,0:T(8,128)S(1)}, f32[24,512]{1,0:T(8,128)S(1)}, u32[]{:S(2)}, u32[]{:S(2)}) %collective-permute-start.5) | collective-permute-done | bytes 49184 | tf_op jit(solution)/shard_map/ppermute | solution.py:460
  27.5 1.3 %assemble.1 = (f32[128,512]{1,0:T(8,128)}, f32[1,128]{1,0:T(1,128)}) custom-call(s32[2]{0:T(128)S(1)} %pad_add_fusion.place_ref, f32[128,512]{1,0:T(8,128)S(1)} %get-tuple-element.48.own_ref, f32[1,128]{1,0:T(1,128)S(1)} %get-tuple-element.49.scores_ref, f32[24,512]{1,0:T(8,128)S(1)} %collective-permute-done.5.back_ref), custom_call_target="tpu_custom_call" | custom-call | flops 65536 | bytes 524288 | tf_op jit(solution)/shard_map/assemble/pallas_call | solution.py:461
  28.7 0.0 collective-permute-done.2
  28.7 0.0 collective-permute-done.4
  28.7 0.0 collective-permute-done.3
  28.7 0.1 fusion.3
  28.9 3.7 %collective-permute-start.6 = (bf16[144,128]{1,0:T(8,128)(2,1)S(1)}, bf16[144,128]{1,0:T(8,128)(2,1)S(1)}, u32[]{:S(2)}, u32[]{:S(2)}) collective-permute-start(bf16[144,128]{1,0:T(8,128)(2,1)S(1)} %get-tuple-element.64), channel_id=1, source_target_pairs={{0,12},{1,13},{2,14},{3,15},{4,8},{5,9},{6,10},{7,11},{8,4},{9,5},... | collective-permute-start | bytes 110600 | tf_op jit(solution)/shard_map/ppermute | solution.py:492
  32.6 0.0 collective-permute-start.8
  32.6 0.7 %collective-permute-start.7 = (bf16[144,128]{1,0:T(8,128)(2,1)S(1)}, bf16[144,128]{1,0:T(8,128)(2,1)S(1)}, u32[]{:S(2)}, u32[]{:S(2)}) collective-permute-start(bf16[144,128]{1,0:T(8,128)(2,1)S(1)} %get-tuple-element.66), channel_id=1, source_target_pairs={{0,4},{1,5},{2,6},{3,7},{4,0},{5,1},{6,2},{7,3},{8,12},{9,13},{10,... | collective-permute-start | bytes 110600 | tf_op jit(solution)/shard_map/ppermute | solution.py:492
  33.3 1.6 %collective-permute-done.6 = bf16[144,128]{1,0:T(8,128)(2,1)S(1)} collective-permute-done((bf16[144,128]{1,0:T(8,128)(2,1)S(1)}, bf16[144,128]{1,0:T(8,128)(2,1)S(1)}, u32[]{:S(2)}, u32[]{:S(2)}) %collective-permute-start.6) | collective-permute-done | bytes 36896 | tf_op jit(solution)/shard_map/ppermute | solution.py:492
  34.9 2.5 %collective-permute-done.8 = bf16[144,128]{1,0:T(8,128)(2,1)S(1)} collective-permute-done((bf16[144,128]{1,0:T(8,128)(2,1)S(1)}, bf16[144,128]{1,0:T(8,128)(2,1)S(1)}, u32[]{:S(2)}, u32[]{:S(2)}) %collective-permute-start.8) | collective-permute-done | bytes 36896 | tf_op jit(solution)/shard_map/ppermute | solution.py:492
  37.4 0.0 collective-permute-done.7
  37.5 0.1 collective-permute-start.9
  37.5 1.2 %collective-permute-done.9.other_ref = bf16[144,128]{1,0:T(8,128)(2,1)S(1)} collective-permute-done((bf16[144,128]{1,0:T(8,128)(2,1)S(1)}, bf16[144,128]{1,0:T(8,128)(2,1)S(1)}, u32[]{:S(2)}, u32[]{:S(2)}) %collective-permute-start.9) | collective-permute-done | bytes 36896 | tf_op jit(solution)/shard_map/ppermute | solution.py:498
  38.7 1.2 %unpack.1 = (f32[4,768]{1,0:T(4,128)}, f32[20,128]{1,0:T(8,128)}, f32[40,256]{1,0:T(8,128)}, f32[80,256]{1,0:T(8,128)}, f32[1,48]{1,0:T(1,128)}) custom-call(bf16[144,128]{1,0:T(8,128)(2,1)S(1)} %fusion.6.mine_ref, bf16[144,128]{1,0:T(8,128)(2,1)S(1)} %collective-permute-done.9.other_ref, s32[2]{0:T(128)S(1)} %pad_add_fusion.place_ref), custom_call_target="tpu_custom_call" | custom-call | tf_op jit(solution)/shard_map/unpack/pallas_call | solution.py:506
  (4 shorter events, 0.1 us)
Async XLA Ops:
  1.4 7.7 %collective-permute-start = (bf16[48,512]{1,0:T(8,128)(2,1)S(1)}, bf16[48,512]{1,0:T(8,128)(2,1)S(1)}, u32[]{:S(2)}, u32[]{:S(2)}) collective-permute-start(bf16[48,512]{1,0:T(8,128)(2,1)S(1)} %edge.1), channel_id=1, source_target_pairs={{0,1},{1,2},{2,3},{3,4},{4,5},{5,6},{6,7},{7,8},{8,9},{9,10},{10,1... | collective-permute-start | bytes 147464 | tf_op jit(solution)/shard_map/ppermute | solution.py:381
  13.4 2.1 %collective-permute-start.1 = (bf16[4,4,144,128]{3,2,1,0:T(8,128)(2,1)S(1)}, bf16[4,4,144,128]{3,2,1,0:T(8,128)(2,1)S(1)}, u32[]{:S(2)}, u32[]{:S(2)}) collective-permute-start(bf16[4,4,144,128]{3,2,1,0:T(8,128)(2,1)S(1)} %slice_bitcast_fusion), channel_id=1, source_target_pairs={{0,16},{16,0},{1,17},{17,1},{2,18},{18,2},{3,19},{19,3},{4,20},{20... | collective-permute-start | bytes 1769480 | tf_op jit(solution)/shard_map/ppermute | solution.py:489
  15.7 13.0 %collective-permute-start.2 = (bf16[4,144,128]{2,1,0:T(8,128)(2,1)S(1)}, bf16[4,144,128]{2,1,0:T(8,128)(2,1)S(1)}, u32[]{:S(2)}, u32[]{:S(2)}) collective-permute-start(bf16[4,144,128]{2,1,0:T(8,128)(2,1)S(1)} %get-tuple-element.61), channel_id=1, source_target_pairs={{0,3},{1,2},{2,1},{3,0},{4,7},{5,6},{6,5},{7,4},{8,11},{9,10},{10,... | collective-permute-start | bytes 442376 | tf_op jit(solution)/shard_map/ppermute | solution.py:492
  18.2 10.5 %collective-permute-start.4 = (bf16[4,144,128]{2,1,0:T(8,128)(2,1)S(1)}, bf16[4,144,128]{2,1,0:T(8,128)(2,1)S(1)}, u32[]{:S(2)}, u32[]{:S(2)}) collective-permute-start(bf16[4,144,128]{2,1,0:T(8,128)(2,1)S(1)} %get-tuple-element.62), channel_id=1, source_target_pairs={{0,2},{1,3},{2,0},{3,1},{4,6},{5,7},{6,4},{7,5},{8,10},{9,11},{10,... | collective-permute-start | bytes 442376 | tf_op jit(solution)/shard_map/ppermute | solution.py:492
  18.7 10.0 %collective-permute-start.3 = (bf16[4,144,128]{2,1,0:T(8,128)(2,1)S(1)}, bf16[4,144,128]{2,1,0:T(8,128)(2,1)S(1)}, u32[]{:S(2)}, u32[]{:S(2)}) collective-permute-start(bf16[4,144,128]{2,1,0:T(8,128)(2,1)S(1)} %get-tuple-element.63), channel_id=1, source_target_pairs={{0,1},{1,0},{2,3},{3,2},{4,5},{5,4},{6,7},{7,6},{8,9},{9,8},{10,11... | collective-permute-start | bytes 442376 | tf_op jit(solution)/shard_map/ppermute | solution.py:492
  20.1 7.3 %collective-permute-start.5 = (f32[24,512]{1,0:T(8,128)S(1)}, f32[24,512]{1,0:T(8,128)S(1)}, u32[]{:S(2)}, u32[]{:S(2)}) collective-permute-start(f32[24,512]{1,0:T(8,128)S(1)} %get-tuple-element.50), channel_id=1, source_target_pairs={{1,0},{2,1},{3,2},{4,3},{5,4},{6,5},{7,6},{8,7},{9,8},{10,9},{11,1... | collective-permute-start | bytes 147464 | tf_op jit(solution)/shard_map/ppermute | solution.py:460
  28.9 6.1 %collective-permute-start.6 = (bf16[144,128]{1,0:T(8,128)(2,1)S(1)}, bf16[144,128]{1,0:T(8,128)(2,1)S(1)}, u32[]{:S(2)}, u32[]{:S(2)}) collective-permute-start(bf16[144,128]{1,0:T(8,128)(2,1)S(1)} %get-tuple-element.64), channel_id=1, source_target_pairs={{0,12},{1,13},{2,14},{3,15},{4,8},{5,9},{6,10},{7,11},{8,4},{9,5},... | collective-permute-start | bytes 110600 | tf_op jit(solution)/shard_map/ppermute | solution.py:492
  32.6 4.9 %collective-permute-start.8 = (bf16[144,128]{1,0:T(8,128)(2,1)S(1)}, bf16[144,128]{1,0:T(8,128)(2,1)S(1)}, u32[]{:S(2)}, u32[]{:S(2)}) collective-permute-start(bf16[144,128]{1,0:T(8,128)(2,1)S(1)} %get-tuple-element.65), channel_id=1, source_target_pairs={{0,8},{1,9},{2,10},{3,11},{4,12},{5,13},{6,14},{7,15},{8,0},{9,1},... | collective-permute-start | bytes 110600 | tf_op jit(solution)/shard_map/ppermute | solution.py:492
  32.6 4.9 %collective-permute-start.7 = (bf16[144,128]{1,0:T(8,128)(2,1)S(1)}, bf16[144,128]{1,0:T(8,128)(2,1)S(1)}, u32[]{:S(2)}, u32[]{:S(2)}) collective-permute-start(bf16[144,128]{1,0:T(8,128)(2,1)S(1)} %get-tuple-element.66), channel_id=1, source_target_pairs={{0,4},{1,5},{2,6},{3,7},{4,0},{5,1},{6,2},{7,3},{8,12},{9,13},{10,... | collective-permute-start | bytes 110600 | tf_op jit(solution)/shard_map/ppermute | solution.py:492
  37.5 1.3 %collective-permute-start.9 = (bf16[144,128]{1,0:T(8,128)(2,1)S(1)}, bf16[144,128]{1,0:T(8,128)(2,1)S(1)}, u32[]{:S(2)}, u32[]{:S(2)}) collective-permute-start(bf16[144,128]{1,0:T(8,128)(2,1)S(1)} %fusion.6.mine_ref), channel_id=1, source_target_pairs={{0,16},{16,0},{1,17},{17,1},{2,18},{18,2},{3,19},{19,3},{4,20},{20... | collective-permute-start | bytes 110600 | tf_op jit(solution)/shard_map/ppermute | solution.py:498

commit v3 on v2

--- a/solution.py
+++ b/solution.py
@@ -15,7 +15,7 @@
 PK = 3
 EDGE = 32
 REACH = 12
-MORE = 16
+MORE = 8
 BACK = 16
 LANES = 128
 
@@ -61,11 +61,17 @@
     return projected, hidden, dot(hidden, squeeze, NT)
 
 
-def edge_kernel(rows_ref, cot_ref, out_ref, cot_held, sems):
-    frames = rows_ref.shape[0]
+def here():
+    return lax.axis_index("seq"), lax.rem(lax.axis_index("dp"), 2)
+
+
+def edge_kernel(rows_ref, cot_ref, out_ref, held, cot_held, sems):
+    frames, feat = rows_ref.shape
+    _, odd = here()
+    start = pl.multiple_of(odd * (frames - EDGE), 16)
     copies = [
         pltpu.make_async_copy(cot_ref, cot_held, sems.at[0]),
-        pltpu.make_async_copy(rows_ref.at[frames - EDGE :], out_ref.at[:EDGE], sems.at[1]),
+        pltpu.make_async_copy(rows_ref.at[pl.ds(start, EDGE)], held, sems.at[1]),
     ]
     for copy in copies:
         copy.start()
@@ -75,9 +81,12 @@
     middle = (cot - high).astype(BF16).astype(F32)
     low = cot - high - middle
     stack = jnp.concatenate([high, middle, low, jnp.zeros((MORE - 3, frames), F32)], axis=0)
-    out_ref[EDGE:, :frames] = stack.astype(BF16)
-    out_ref[EDGE:, frames:] = jnp.zeros((MORE, out_ref.shape[1] - frames), BF16)
+    stack = jnp.concatenate([stack] * (EDGE // MORE), axis=0)
+    row = lax.broadcasted_iota(jnp.int32, (EDGE, frames), 0)
+    carries = (row < MORE) & (odd == 1) | (row >= EDGE - MORE) & (odd == 0)
     copies[1].wait()
+    out_ref[:, frames:] = held[:, frames:]
+    out_ref[:, :frames] = jnp.where(carries, stack, held[:, :frames].astype(F32)).astype(BF16)
 
 
 def project_kernel(count, *refs):
@@ -121,7 +130,6 @@
 def head_kernel(
     n,
     packed,
-    place_ref,
     squeezed_ref,
     edge_ref,
     cot_ref,
@@ -133,17 +141,22 @@
     third_ref,
     final_ref,
     scores_ref,
-    before_ref,
+    edge_scores_ref,
     delta_ref,
     edge_projected_ref,
     *outs,
 ):
     frames = squeezed_ref.shape[0]
     total = EDGE + frames
-    seq, core = place_ref[0], place_ref[1]
+    seq, odd = here()
     row = lax.broadcasted_iota(jnp.int32, (total, LANES), 0)
-    inside = (row >= EDGE - 2 * REACH) & ((row >= EDGE) | (seq > 0))
-    window = inside & (row >= EDGE - REACH) & ((row < total - REACH) | (seq == n - 1))
+    frame = row - jnp.where(row >= frames, odd * total, 0)
+    before = jnp.where((odd == 1) & (seq > 0), REACH, 0)
+    after = jnp.where((odd == 0) & (seq < n - 1), REACH, 0)
+    inside = (frame >= -2 * before) & (frame < frames + 2 * after)
+    first = jnp.where((odd == 0) & (seq > 0), REACH, -before)
+    last = jnp.where((odd == 1) & (seq < n - 1), -REACH, after)
+    window = (frame >= first) & (frame < frames + last)
 
     def mask(values, where):
         width = values.shape[1]
@@ -154,18 +167,21 @@
         )
 
     edge_projected, edge_hidden, edge_squeezed = forward_rows(
-        edge_ref[:EDGE, :], projection_ref[...], squeeze_ref[...]
+        edge_ref[...], projection_ref[...], squeeze_ref[...]
     )
-    edge_projected_ref[...] = edge_projected[EDGE - BACK :]
-    squeezed = jnp.concatenate([edge_squeezed, squeezed_ref[...]], axis=0)
-
-    parts = edge_ref[EDGE:, :LANES].astype(F32)
+    edge_projected_ref[...] = edge_projected
+    squeezed = jnp.concatenate([squeezed_ref[...], edge_squeezed], axis=0)
+
+    parts = edge_ref[:, :LANES].astype(F32)
+    parts = jnp.where(odd == 0, parts[EDGE - MORE :], parts[:MORE])
     parts = parts[0:1] + parts[1:2] + parts[2:3]
     columns = jnp.concatenate([cot_ref[...], parts, jnp.zeros((6, LANES), F32)], axis=0).T
     cot = jnp.concatenate(
         [
-            jnp.broadcast_to(columns[frames - EDGE :, 1:2], (EDGE, LANES)),
             jnp.broadcast_to(columns[:, 0:1], (frames, LANES)),
+            jnp.broadcast_to(
+                jnp.where(odd == 0, columns[:EDGE, 1:2], columns[frames - EDGE :, 1:2]), (EDGE, LANES)
+            ),
         ],
         axis=0,
     )
@@ -186,7 +202,7 @@
     unit, slope = leaky_pair(act)
     final_in = mask(unit, inside).astype(BF16).astype(F32)
     taps = shifted(final_in, PK, 1)
-    for ref, rows in ((scores_ref, slice(EDGE, total)), (before_ref, slice(0, LANES))):
+    for ref, rows in ((scores_ref, slice(0, frames)), (edge_scores_ref, slice(total - LANES, total))):
         scores = jnp.zeros((1, rows.stop - rows.start), F32)
         for k in range(PK):
             scores = scores + dot(final_ref[:, k * C2 : (k + 1) * C2], taps[k][rows], NT)
@@ -218,8 +234,8 @@
             upstream = upstream + dot(piece, ref[k * width : (k + 1) * width, :], NT)
     third, second, first = grads
     delta = mask(upstream * slopes[0], inside)
-    delta_ref[...] = delta[EDGE - BACK :].astype(BF16)
-    hidden = jnp.concatenate([edge_hidden, hidden_ref[...]], axis=0)
+    delta_ref[...] = delta.astype(BF16)
+    hidden = jnp.concatenate([hidden_ref[...], edge_hidden], axis=0)
     squeeze_grad = dot(mask(delta, window).astype(BF16), hidden, TN)
 
     if not packed:
@@ -242,7 +258,7 @@
         while rows.shape[0]:
             side, start = divmod(at, half)
             length = min(rows.shape[0], half - start)
-            payload_ref[side ^ core, slot & 3, slot >> 2, start : start + length, :] = rows[:length]
+            payload_ref[side ^ odd, slot & 3, slot >> 2, start : start + length, :] = rows[:length]
             rows = rows[length:]
             at += length
 
@@ -285,37 +301,41 @@
 
 
 def feature_kernel(
-    rows_ref, edge_ref, projected_ref, edge_projected_ref, delta_ref, before_ref, squeeze_ref, projection_ref, out_ref, back_ref
+    rows_ref, edge_ref, projected_ref, edge_projected_ref, delta_ref, after_ref, squeeze_ref, projection_ref, out_ref, back_ref
 ):
     hidden_upstream = dot(delta_ref[...], squeeze_ref[...])
-    projected = jnp.concatenate([edge_projected_ref[...], projected_ref[...]], axis=0)
+    projected = jnp.concatenate([projected_ref[...], edge_projected_ref[...]], axis=0)
     hidden_normed, hidden_inverse = normalize(projected.astype(F32))
     projected_grad = normalize_back(hidden_upstream, hidden_normed, hidden_inverse).astype(BF16)
     normed_grad = dot(projected_grad, projection_ref[...], NT)
-    rows = jnp.concatenate([edge_ref[EDGE - BACK : EDGE, :], rows_ref[...]], axis=0)
+    rows = jnp.concatenate([rows_ref[...], edge_ref[...]], axis=0)
     normed, inverse = normalize(rows.astype(F32))
     grad = normalize_back(normed_grad, normed, inverse)
-    out_ref[...] = grad[BACK:]
-    back_ref[:BACK, :] = grad[:BACK]
-    back_ref[BACK:, :LANES] = jnp.broadcast_to(before_ref[...], (8, LANES))
+    out_ref[...] = grad[:-EDGE]
+    back_ref[:BACK, :] = jnp.where(here()[1] == 0, grad[-EDGE : BACK - EDGE], grad[-BACK:])
+    back_ref[BACK:, :LANES] = jnp.broadcast_to(after_ref[...], (8, LANES))
     back_ref[BACK:, LANES:] = jnp.zeros((8, back_ref.shape[1] - LANES), F32)
 
 
-def assemble_kernel(n, place_ref, own_ref, scores_ref, back_ref, grad_ref, final_scores_ref):
+def assemble_kernel(n, own_ref, scores_ref, back_ref, grad_ref, final_scores_ref):
     frames = own_ref.shape[0]
-    last = place_ref[0] == n - 1
-    grad_ref[: frames - BACK, :] = own_ref[: frames - BACK, :]
+    seq, odd = here()
+    low, high = (odd == 0) & (seq > 0), (odd == 1) & (seq < n - 1)
+    grad_ref[BACK : frames - BACK, :] = own_ref[BACK : frames - BACK, :]
     row = lax.broadcasted_iota(jnp.int32, (BACK, own_ref.shape[1]), 0)
-    keep = last | (row < BACK - REACH)
-    grad_ref[frames - BACK :, :] = jnp.where(keep, own_ref[frames - BACK :, :], back_ref[:BACK, :])
-    moved = pltpu.roll(back_ref[BACK:, :LANES], frames - EDGE, 1)
+    came = back_ref[:BACK, :]
+    grad_ref[:BACK, :] = jnp.where(low & (row < REACH), came, own_ref[:BACK, :])
+    grad_ref[frames - BACK :, :] = jnp.where(high & (row >= BACK - REACH), came, own_ref[frames - BACK :, :])
+    scores = back_ref[BACK:, :LANES]
+    moved = pltpu.roll(scores, EDGE, 1)
     lane = lax.broadcasted_iota(jnp.int32, (1, frames), 1)
-    final_scores_ref[...] = jnp.where(last | (lane < frames - REACH), scores_ref[...], moved[0:1])
-
-
-def unpack_kernel(factor, mine_ref, other_ref, place_ref, squeeze_ref, first_ref, second_ref, third_ref, final_ref, both):
+    kept = jnp.where(high & (lane >= frames - REACH), scores[0:1], scores_ref[...])
+    final_scores_ref[...] = jnp.where(low & (lane < REACH), moved[0:1], kept)
+
+
+def unpack_kernel(factor, mine_ref, other_ref, squeeze_ref, first_ref, second_ref, third_ref, final_ref, both):
     half = mine_ref.shape[0]
-    core = place_ref[1]
+    _, core = here()
     both[pl.ds(pl.multiple_of(core * half, 16), half), :] = mine_ref[...].astype(F32) * factor
     both[pl.ds(pl.multiple_of((1 - core) * half, 16), half), :] = other_ref[...].astype(F32) * factor
     base = 0
@@ -341,7 +361,6 @@
 
 VMEM = pl.BlockSpec(memory_space=pltpu.VMEM)
 HBM = pl.BlockSpec(memory_space=pltpu.HBM)
-SMEM = pl.BlockSpec(memory_space=pltpu.SMEM)
 
 
 def params(mib):
@@ -365,20 +384,26 @@
     n, cores = lax.axis_size("seq"), lax.axis_size("dp")
     frames, feat = features.shape[1:]
     width = projection_weight.shape[1]
-    seq, core = lax.axis_index("seq"), lax.axis_index("dp")
     packed = n == 16 and cores == 2
     rows = features.reshape(frames, feat)
-    place = jnp.stack([seq, core]).astype(jnp.int32)
+    along = []
+    for i in range(0, cores * n, n):
+        down = [(i + j + 1, i + j) for j in range(n - 1)]
+        along += down if i // n % 2 == 0 else [(target, source) for source, target in down]
+    for i in range(0, (cores // 2) * 2 * n, 2 * n):
+        along += [(i, i + n), (i + 2 * n - 1, i + n - 1)]
+    along = sorted(along)
+    returning = sorted((target, source) for source, target in along)
 
     edge = pl.pallas_call(
         edge_kernel,
         in_specs=[HBM, HBM],
         out_specs=VMEM,
-        out_shape=vmem((EDGE + MORE, feat), BF16),
-        scratch_shapes=[pltpu.VMEM((1, frames), F32), pltpu.SemaphoreType.DMA((2,))],
+        out_shape=vmem((EDGE, feat), BF16),
+        scratch_shapes=[pltpu.VMEM((EDGE, feat), BF16), pltpu.VMEM((1, frames), F32), pltpu.SemaphoreType.DMA((2,))],
         name="edge",
     )(hbm(rows), hbm(score_cotangent))
-    edge = lax.ppermute(edge, "seq", [(i, i + 1) for i in range(n - 1)])
+    edge = lax.ppermute(edge, ("dp", "seq"), along)
 
     sources = (
         rows,
@@ -418,15 +443,15 @@
             sds((1, PK * C2), F32),
         ]
         scratch = []
-    own_scores, before, delta, edge_projected, *grads = pl.pallas_call(
+    own_scores, after, delta, edge_projected, *grads = pl.pallas_call(
         functools.partial(head_kernel, n, packed),
-        in_specs=[SMEM] + [VMEM] * 10,
+        in_specs=[VMEM] * 10,
         out_specs=[VMEM] * (4 + len(grad_shapes)),
         out_shape=[
             sds((1, frames), F32),
             sds((1, LANES), F32),
-            sds((BACK + frames, C0), BF16),
-            sds((BACK, width), BF16),
+            sds((frames + EDGE, C0), BF16),
+            sds((EDGE, width), BF16),
             *grad_shapes,
         ],
         scratch_shapes=scratch,
@@ -434,7 +459,6 @@
         cost_estimate=cost(10**9, 4 * 10**6),
         name="head",
     )(
-        place,
         squeezed,
         edge,
         cot,
@@ -456,17 +480,20 @@
             compiler_params=params(8),
             cost_estimate=cost(2 * frames * width * (feat + C0), 2 * feat * width),
             name="feature",
-        )(rows, edge, projected, edge_projected, delta, before, squeeze, projection)
-        back = lax.ppermute(back, "seq", [(i + 1, i) for i in range(n - 1)])
+        )(rows, edge, projected, edge_projected, delta, after, squeeze, projection)
+        back = lax.ppermute(back, ("dp", "seq"), returning)
+        return own_grad, back
+
+    def assembled(own_grad, back):
         feature_grad, scores = pl.pallas_call(
             functools.partial(assemble_kernel, n),
-            in_specs=[SMEM] + [VMEM] * 3,
+            in_specs=[VMEM] * 3,
             out_specs=[VMEM] * 2,
             out_shape=[sds((frames, feat), F32), sds((1, frames), F32)],
             compiler_params=params(4),
             cost_estimate=cost(frames * feat, 8 * frames * feat),
             name="assemble",
-        )(place, own_grad, own_scores, back)
+        )(own_grad, own_scores, back)
         return feature_grad[None], scores
 
     factor = 1.0 / math.sqrt(cores * n * frames)
@@ -475,7 +502,7 @@
         for term in grads[:4] + [grads[4].reshape(PK * C2)]:
             part = lax.psum_scatter(term * factor, "seq", scatter_dimension=0, tiled=True)
             shares.append(lax.psum(part.astype(BF16), "dp").astype(F32))
-        feature_grad, scores = features_back()
+        feature_grad, scores = assembled(*features_back())
         return (scores, feature_grad, *shares)
 
     def added(*terms):
@@ -493,7 +520,10 @@
         ]
         held = added(held[0], *moved)
         if stride == 1:
-            feature_grad, scores = features_back()
+            own_grad, back = features_back()
+            held, own_grad = lax.optimization_barrier((held, own_grad))
+        else:
+            feature_grad, scores = assembled(own_grad, back)
             held, feature_grad, scores = lax.optimization_barrier((held, feature_grad, scores))
     other = lax.ppermute(held, "dp", swap)
     shapes = [
@@ -505,13 +535,13 @@
     ]
     *shares, final = pl.pallas_call(
         functools.partial(unpack_kernel, factor),
-        in_specs=[VMEM, VMEM, SMEM],
+        in_specs=[VMEM, VMEM],
         out_specs=[VMEM] * 5,
         out_shape=[sds(shape, F32) for shape in shapes],
         scratch_shapes=[pltpu.VMEM((2 * half, LANES), F32)],
         compiler_params=params(4),
         name="unpack",
-    )(held, other, place)
+    )(held, other)
     return (scores, feature_grad, *shares, final.reshape(PK * C2 // n))
 
 

time: 40.2 us -> 35.1 us (0.87)
  starting transfers between devices: 14.4 us -> 12.4 us
  Pallas kernels: 10.4 us -> 8.84 us
  waiting for transfers between devices: 13.4 us -> 11.9 us
    ppermute x2, waiting for transfers between devices: 6.04 us -> 1.58 us  [the longest x1 1.58 us: shards(): edge = lax.ppermute(edge, ('dp', 'seq'), along)]
    ppermute x2, starting transfers between devices: 6.14 us -> 1.95 us  [the longest x1 1.44 us: features_back(): back = lax.ppermute(back, ('dp', 'seq'), returning)]
    ppermute x6, waiting for transfers between devices: 4.13 us -> 7.48 us  [shards(): lax.ppermute(held[j], 'seq', [(i, i ^ j * stride) for i in range(n)])]
    ppermute x6, starting transfers between devices: 8.08 us -> 9.83 us  [shards(): lax.ppermute(held[j], 'seq', [(i, i ^ j * stride) for i in range(n)])]
    pallas_call x2, Pallas kernels: 5.48 us -> 4.46 us  [the longest x1 3.74 us: shards(): pl.pallas_call(functools.partial(head_kernel, n, packed), in_specs=[VMEM]...]
    pallas_call x1, Pallas kernels: 1.22 us -> 0.68 us  [shards(): pl.pallas_call(functools.partial(unpack_kernel, factor), in_specs=[VMEM,...]
    ppermute x1, starting transfers between devices: 0.07 us -> 0.54 us  [shards(): held = added(payload[0], lax.ppermute(payload[1], 'dp', swap))]
  transfers between devices with their start and end apart: 10 -> 10, of which waited for: 5 -> 7; matrix products, arithmetic and copies ran while one was open for 2% -> 2% of each run, Pallas kernels for 10% -> 10%
where the time goes in v3:
time: 35.1 us; the launch traced here: 34.9 us
  starting transfers between devices  12.4 us (35%)
  waiting for transfers between devices  11.9 us (34%)
  Pallas kernels  8.84 us (25%)
  local copies, waits for them, and re-layouts  0.77 us (2%)
  between operations  0.71 us (2%)
    ppermute x6, starting transfers between devices, shards(): lax.ppermute(held[j], 'seq', [(i, i ^ j * stride) for i in range(n)])  9.83 us
    ppermute x6, waiting for transfers between devices, shards(): lax.ppermute(held[j], 'seq', [(i, i ^ j * stride) for i in range(n)])  7.48 us
    pallas_call x1, Pallas kernels, shards(): pl.pallas_call(functools.partial(head_kernel, n, packed), in_specs=[VMEM]...  3.74 us
    pallas_call x1, Pallas kernels, shards(): pl.pallas_call(functools.partial(project_kernel, len(sources)), in_specs=...  2.11 us
    ppermute x1, waiting for transfers between devices, shards(): held = added(payload[0], lax.ppermute(payload[1], 'dp', swap))  1.63 us
    ppermute x1, waiting for transfers between devices, shards(): edge = lax.ppermute(edge, ('dp', 'seq'), along)  1.58 us
    ppermute x1, starting transfers between devices, features_back(): back = lax.ppermute(back, ('dp', 'seq'), returning)  1.44 us
    ppermute x1, waiting for transfers between devices, shards(): other = lax.ppermute(held, 'dp', swap)  1.2 us
  transfers between devices with their start and end apart: 10, of which 7 were waited for; matrix products, arithmetic and copies ran while one was open for 2% of the time, Pallas kernels for 10%

profile of v3, /device:TPU:0, one launch (start us, length us, event | category | flops | bytes accessed | tf_op | source)
XLA Modules:
  0.0 34.9 jit_solution(2659252693911945757)
XLA Ops:
  0.6 0.8 %edge.1 = bf16[32,512]{1,0:T(8,128)(2,1)S(1)} custom-call(bf16[128,512]{1,0:T(8,128)(2,1)} %bitcast.28, f32[1,128]{1,0:T(1,128)} %cot_ref.1), custom_call_target="tpu_custom_call" | custom-call | tf_op jit(solution)/shard_map/edge/pallas_call | solution.py:398
  1.4 0.5 %collective-permute-start = (bf16[32,512]{1,0:T(8,128)(2,1)S(1)}, bf16[32,512]{1,0:T(8,128)(2,1)S(1)}, u32[]{:S(2)}, u32[]{:S(2)}) collective-permute-start(bf16[32,512]{1,0:T(8,128)(2,1)S(1)} %edge.1), channel_id=1, source_target_pairs={{0,16},{1,0},{2,1},{3,2},{4,3},{5,4},{6,5},{7,6},{8,7},{9,8},{10,9... | collective-permute-start | bytes 98312 | tf_op jit(solution)/shard_map/ppermute | solution.py:406
  1.9 0.7 %reshape.30.final_ref = bf16[1,768]{1,0:T(2,128)(2,1)S(1)} reshape(bf16[768]{0:T(1024)(128)(2,1)} %param.15) | data formatting | bytes 3072 | tf_op jit(solution)/shard_map/reshape | solution.py:471
  2.6 2.1 %project.1 = (bf16[128,512]{1,0:T(8,128)(2,1)S(1)}, bf16[512,768]{1,0:T(8,128)(2,1)S(1)}, bf16[64,768]{1,0:T(8,128)(2,1)S(1)}, f32[1,128]{1,0:T(1,128)S(1)}, bf1...) custom-call(bf16[128,512]{1,0:T(8,128)(2,1)} %bitcast.29, ...), custom_call_target="tpu_custom_call" | custom-call | flops 113246208 | bytes 786432 | tf_op jit(solution)/shard_map/project/pallas_call | solution.py:417
  4.8 1.6 %collective-permute-done.edge_ref = bf16[32,512]{1,0:T(8,128)(2,1)S(1)} collective-permute-done((bf16[32,512]{1,0:T(8,128)(2,1)S(1)}, bf16[32,512]{1,0:T(8,128)(2,1)S(1)}, u32[]{:S(2)}, u32[]{:S(2)}) %collective-permute-start) | collective-permute-done | bytes 32800 | tf_op jit(solution)/shard_map/ppermute | solution.py:406
  6.3 3.7 %head.1 = (f32[1,128]{1,0:T(1,128)S(1)}, f32[1,128]{1,0:T(1,128)S(1)}, bf16[160,64]{1,0:T(8,128)(2,1)S(1)}, bf16[32,768]{1,0:T(8,128)(2,1)S(1)}, bf16[2,4,4,144,128]{4,3,2,1,0:T(8,128)(2,1)S(1)}) custom-call(f32[128,64]{1,0:T(8,128)S(1)} %get-tuple-element.36.squeezed_ref, bf16[32,512]{1,0:T(8,128)(2,1)S(1)} %collective-permute-done.edge_ref, ...), custom_call_target="tpu_custom_call" | custom-call | flops 1000000000 | bytes 4000000 | tf_op jit(solution)/shard_map/head/pallas_call | solution.py:446
  10.1 0.5 %collective-permute-start.1 = (bf16[4,4,144,128]{3,2,1,0:T(8,128)(2,1)S(1)}, bf16[4,4,144,128]{3,2,1,0:T(8,128)(2,1)S(1)}, u32[]{:S(2)}, u32[]{:S(2)}) collective-permute-start(bf16[4,4,144,128]{3,2,1,0:T(8,128)(2,1)S(1)} %slice_bitcast_fusion), channel_id=1, source_target_pairs={{0,16},{16,0},{1,17},{17,1},{2,18},{18,2},{3,19},{19,3},{4,20},{20... | collective-permute-start | bytes 1769480 | tf_op jit(solution)/shard_map/ppermute | solution.py:516
  10.7 1.6 %collective-permute-done.1 = bf16[4,4,144,128]{3,2,1,0:T(8,128)(2,1)S(1)} collective-permute-done((bf16[4,4,144,128]{3,2,1,0:T(8,128)(2,1)S(1)}, bf16[4,4,144,128]{3,2,1,0:T(8,128)(2,1)S(1)}, u32[]{:S(2)}, u32[]{:S(2)}) %collective-permute-start.1) | collective-permute-done | bytes 589856 | tf_op jit(solution)/shard_map/ppermute | solution.py:516
  12.3 0.2 fusion
  12.5 4.7 %collective-permute-start.2 = (bf16[4,144,128]{2,1,0:T(8,128)(2,1)S(1)}, bf16[4,144,128]{2,1,0:T(8,128)(2,1)S(1)}, u32[]{:S(2)}, u32[]{:S(2)}) collective-permute-start(bf16[4,144,128]{2,1,0:T(8,128)(2,1)S(1)} %get-tuple-element.65), channel_id=1, source_target_pairs={{0,3},{1,2},{2,1},{3,0},{4,7},{5,6},{6,5},{7,4},{8,11},{9,10},{10,... | collective-permute-start | bytes 442376 | tf_op jit(solution)/shard_map/ppermute | solution.py:519
  17.2 0.0 collective-permute-start.4
  17.2 0.6 %collective-permute-start.3 = (bf16[4,144,128]{2,1,0:T(8,128)(2,1)S(1)}, bf16[4,144,128]{2,1,0:T(8,128)(2,1)S(1)}, u32[]{:S(2)}, u32[]{:S(2)}) collective-permute-start(bf16[4,144,128]{2,1,0:T(8,128)(2,1)S(1)} %get-tuple-element.67), channel_id=1, source_target_pairs={{0,1},{1,0},{2,3},{3,2},{4,5},{5,4},{6,7},{7,6},{8,9},{9,8},{10,11... | collective-permute-start | bytes 442376 | tf_op jit(solution)/shard_map/ppermute | solution.py:519
  17.9 0.8 %feature.1 = (f32[128,512]{1,0:T(8,128)S(1)}, f32[24,512]{1,0:T(8,128)S(1)}) custom-call(bf16[128,512]{1,0:T(8,128)(2,1)S(1)} %get-tuple-element.45.rows_ref, bf16[32,512]{1,0:T(8,128)(2,1)S(1)} %collective-permute-done.edge_ref, bf16[128,768]{1,0:T(8,128)(2,1)S(1)} %get-tuple-element.46.projected_ref, ...), custom_call_target="tpu_custom_call" | custom-call | flops 113246208 | bytes 786432 | tf_op jit(solution)/shard_map/feature/pallas_call | solution.py:475
  18.7 1.4 %collective-permute-start.8 = (f32[24,512]{1,0:T(8,128)S(1)}, f32[24,512]{1,0:T(8,128)S(1)}, u32[]{:S(2)}, u32[]{:S(2)}) collective-permute-start(f32[24,512]{1,0:T(8,128)S(1)} %get-tuple-element.54), channel_id=1, source_target_pairs={{0,1},{1,2},{2,3},{3,4},{4,5},{5,6},{6,7},{7,8},{8,9},{9,10},{10,1... | collective-permute-start | bytes 147464 | tf_op jit(solution)/shard_map/ppermute | solution.py:484
  20.1 1.7 %collective-permute-done.2 = bf16[4,144,128]{2,1,0:T(8,128)(2,1)S(1)} collective-permute-done((bf16[4,144,128]{2,1,0:T(8,128)(2,1)S(1)}, bf16[4,144,128]{2,1,0:T(8,128)(2,1)S(1)}, u32[]{:S(2)}, u32[]{:S(2)}) %collective-permute-start.2) | collective-permute-done | bytes 147488 | tf_op jit(solution)/shard_map/ppermute | solution.py:519
  21.9 2.7 %collective-permute-done.4 = bf16[4,144,128]{2,1,0:T(8,128)(2,1)S(1)} collective-permute-done((bf16[4,144,128]{2,1,0:T(8,128)(2,1)S(1)}, bf16[4,144,128]{2,1,0:T(8,128)(2,1)S(1)}, u32[]{:S(2)}, u32[]{:S(2)}) %collective-permute-start.4) | collective-permute-done | bytes 147488 | tf_op jit(solution)/shard_map/ppermute | solution.py:519
  24.5 0.0 collective-permute-done.3
  24.5 0.1 fusion.3
  24.6 3.0 %collective-permute-start.5 = (bf16[144,128]{1,0:T(8,128)(2,1)S(1)}, bf16[144,128]{1,0:T(8,128)(2,1)S(1)}, u32[]{:S(2)}, u32[]{:S(2)}) collective-permute-start(bf16[144,128]{1,0:T(8,128)(2,1)S(1)} %get-tuple-element.68), channel_id=1, source_target_pairs={{0,12},{1,13},{2,14},{3,15},{4,8},{5,9},{6,10},{7,11},{8,4},{9,5},... | collective-permute-start | bytes 110600 | tf_op jit(solution)/shard_map/ppermute | solution.py:519
  27.6 0.6 %collective-permute-start.7 = (bf16[144,128]{1,0:T(8,128)(2,1)S(1)}, bf16[144,128]{1,0:T(8,128)(2,1)S(1)}, u32[]{:S(2)}, u32[]{:S(2)}) collective-permute-start(bf16[144,128]{1,0:T(8,128)(2,1)S(1)} %get-tuple-element.69), channel_id=1, source_target_pairs={{0,8},{1,9},{2,10},{3,11},{4,12},{5,13},{6,14},{7,15},{8,0},{9,1},... | collective-permute-start | bytes 110600 | tf_op jit(solution)/shard_map/ppermute | solution.py:519
  28.3 0.8 %collective-permute-start.6 = (bf16[144,128]{1,0:T(8,128)(2,1)S(1)}, bf16[144,128]{1,0:T(8,128)(2,1)S(1)}, u32[]{:S(2)}, u32[]{:S(2)}) collective-permute-start(bf16[144,128]{1,0:T(8,128)(2,1)S(1)} %get-tuple-element.70), channel_id=1, source_target_pairs={{0,4},{1,5},{2,6},{3,7},{4,0},{5,1},{6,2},{7,3},{8,12},{9,13},{10,... | collective-permute-start | bytes 110600 | tf_op jit(solution)/shard_map/ppermute | solution.py:519
  29.1 0.0 collective-permute-done.8.back_ref
  29.1 0.7 %assemble.1 = (f32[128,512]{1,0:T(8,128)}, f32[1,128]{1,0:T(1,128)}) custom-call(f32[128,512]{1,0:T(8,128)S(1)} %get-tuple-element.52.own_ref, f32[1,128]{1,0:T(1,128)S(1)} %get-tuple-element.53.scores_ref, f32[24,512]{1,0:T(8,128)S(1)} %collective-permute-done.8.back_ref), custom_call_target="tpu_custom_call" | custom-call | flops 65536 | bytes 524288 | tf_op jit(solution)/shard_map/assemble/pallas_call | solution.py:488
  29.8 0.8 %collective-permute-done.5 = bf16[144,128]{1,0:T(8,128)(2,1)S(1)} collective-permute-done((bf16[144,128]{1,0:T(8,128)(2,1)S(1)}, bf16[144,128]{1,0:T(8,128)(2,1)S(1)}, u32[]{:S(2)}, u32[]{:S(2)}) %collective-permute-start.5) | collective-permute-done | bytes 36896 | tf_op jit(solution)/shard_map/ppermute | solution.py:519
  30.6 2.3 %collective-permute-done.7 = bf16[144,128]{1,0:T(8,128)(2,1)S(1)} collective-permute-done((bf16[144,128]{1,0:T(8,128)(2,1)S(1)}, bf16[144,128]{1,0:T(8,128)(2,1)S(1)}, u32[]{:S(2)}, u32[]{:S(2)}) %collective-permute-start.7) | collective-permute-done | bytes 36896 | tf_op jit(solution)/shard_map/ppermute | solution.py:519
  32.9 0.0 collective-permute-done.6
  32.9 0.1 collective-permute-start.9
  33.0 1.2 %collective-permute-done.9.other_ref = bf16[144,128]{1,0:T(8,128)(2,1)S(1)} collective-permute-done((bf16[144,128]{1,0:T(8,128)(2,1)S(1)}, bf16[144,128]{1,0:T(8,128)(2,1)S(1)}, u32[]{:S(2)}, u32[]{:S(2)}) %collective-permute-start.9) | collective-permute-done | bytes 36896 | tf_op jit(solution)/shard_map/ppermute | solution.py:528
  34.2 0.7 %unpack.1 = (f32[4,768]{1,0:T(4,128)}, f32[20,128]{1,0:T(8,128)}, f32[40,256]{1,0:T(8,128)}, f32[80,256]{1,0:T(8,128)}, f32[1,48]{1,0:T(1,128)}) custom-call(bf16[144,128]{1,0:T(8,128)(2,1)S(1)} %fusion.6.mine_ref, bf16[144,128]{1,0:T(8,128)(2,1)S(1)} %collective-permute-done.9.other_ref), custom_call_target="tpu_custom_call" | custom-call | tf_op jit(solution)/shard_map/unpack/pallas_call | solution.py:536
  (4 shorter events, 0.1 us)
Async XLA Ops:
  1.4 4.9 %collective-permute-start = (bf16[32,512]{1,0:T(8,128)(2,1)S(1)}, bf16[32,512]{1,0:T(8,128)(2,1)S(1)}, u32[]{:S(2)}, u32[]{:S(2)}) collective-permute-start(bf16[32,512]{1,0:T(8,128)(2,1)S(1)} %edge.1), channel_id=1, source_target_pairs={{0,16},{1,0},{2,1},{3,2},{4,3},{5,4},{6,5},{7,6},{8,7},{9,8},{10,9... | collective-permute-start | bytes 98312 | tf_op jit(solution)/shard_map/ppermute | solution.py:406
  10.1 2.2 %collective-permute-start.1 = (bf16[4,4,144,128]{3,2,1,0:T(8,128)(2,1)S(1)}, bf16[4,4,144,128]{3,2,1,0:T(8,128)(2,1)S(1)}, u32[]{:S(2)}, u32[]{:S(2)}) collective-permute-start(bf16[4,4,144,128]{3,2,1,0:T(8,128)(2,1)S(1)} %slice_bitcast_fusion), channel_id=1, source_target_pairs={{0,16},{16,0},{1,17},{17,1},{2,18},{18,2},{3,19},{19,3},{4,20},{20... | collective-permute-start | bytes 1769480 | tf_op jit(solution)/shard_map/ppermute | solution.py:516
  12.5 9.4 %collective-permute-start.2 = (bf16[4,144,128]{2,1,0:T(8,128)(2,1)S(1)}, bf16[4,144,128]{2,1,0:T(8,128)(2,1)S(1)}, u32[]{:S(2)}, u32[]{:S(2)}) collective-permute-start(bf16[4,144,128]{2,1,0:T(8,128)(2,1)S(1)} %get-tuple-element.65), channel_id=1, source_target_pairs={{0,3},{1,2},{2,1},{3,0},{4,7},{5,6},{6,5},{7,4},{8,11},{9,10},{10,... | collective-permute-start | bytes 442376 | tf_op jit(solution)/shard_map/ppermute | solution.py:519
  17.2 7.3 %collective-permute-start.4 = (bf16[4,144,128]{2,1,0:T(8,128)(2,1)S(1)}, bf16[4,144,128]{2,1,0:T(8,128)(2,1)S(1)}, u32[]{:S(2)}, u32[]{:S(2)}) collective-permute-start(bf16[4,144,128]{2,1,0:T(8,128)(2,1)S(1)} %get-tuple-element.66), channel_id=1, source_target_pairs={{0,2},{1,3},{2,0},{3,1},{4,6},{5,7},{6,4},{7,5},{8,10},{9,11},{10,... | collective-permute-start | bytes 442376 | tf_op jit(solution)/shard_map/ppermute | solution.py:519
  17.2 7.3 %collective-permute-start.3 = (bf16[4,144,128]{2,1,0:T(8,128)(2,1)S(1)}, bf16[4,144,128]{2,1,0:T(8,128)(2,1)S(1)}, u32[]{:S(2)}, u32[]{:S(2)}) collective-permute-start(bf16[4,144,128]{2,1,0:T(8,128)(2,1)S(1)} %get-tuple-element.67), channel_id=1, source_target_pairs={{0,1},{1,0},{2,3},{3,2},{4,5},{5,4},{6,7},{7,6},{8,9},{9,8},{10,11... | collective-permute-start | bytes 442376 | tf_op jit(solution)/shard_map/ppermute | solution.py:519
  18.7 10.4 %collective-permute-start.8 = (f32[24,512]{1,0:T(8,128)S(1)}, f32[24,512]{1,0:T(8,128)S(1)}, u32[]{:S(2)}, u32[]{:S(2)}) collective-permute-start(f32[24,512]{1,0:T(8,128)S(1)} %get-tuple-element.54), channel_id=1, source_target_pairs={{0,1},{1,2},{2,3},{3,4},{4,5},{5,6},{6,7},{7,8},{8,9},{9,10},{10,1... | collective-permute-start | bytes 147464 | tf_op jit(solution)/shard_map/ppermute | solution.py:484
  24.6 5.9 %collective-permute-start.5 = (bf16[144,128]{1,0:T(8,128)(2,1)S(1)}, bf16[144,128]{1,0:T(8,128)(2,1)S(1)}, u32[]{:S(2)}, u32[]{:S(2)}) collective-permute-start(bf16[144,128]{1,0:T(8,128)(2,1)S(1)} %get-tuple-element.68), channel_id=1, source_target_pairs={{0,12},{1,13},{2,14},{3,15},{4,8},{5,9},{6,10},{7,11},{8,4},{9,5},... | collective-permute-start | bytes 110600 | tf_op jit(solution)/shard_map/ppermute | solution.py:519
  27.6 5.3 %collective-permute-start.7 = (bf16[144,128]{1,0:T(8,128)(2,1)S(1)}, bf16[144,128]{1,0:T(8,128)(2,1)S(1)}, u32[]{:S(2)}, u32[]{:S(2)}) collective-permute-start(bf16[144,128]{1,0:T(8,128)(2,1)S(1)} %get-tuple-element.69), channel_id=1, source_target_pairs={{0,8},{1,9},{2,10},{3,11},{4,12},{5,13},{6,14},{7,15},{8,0},{9,1},... | collective-permute-start | bytes 110600 | tf_op jit(solution)/shard_map/ppermute | solution.py:519
  28.3 4.6 %collective-permute-start.6 = (bf16[144,128]{1,0:T(8,128)(2,1)S(1)}, bf16[144,128]{1,0:T(8,128)(2,1)S(1)}, u32[]{:S(2)}, u32[]{:S(2)}) collective-permute-start(bf16[144,128]{1,0:T(8,128)(2,1)S(1)} %get-tuple-element.70), channel_id=1, source_target_pairs={{0,4},{1,5},{2,6},{3,7},{4,0},{5,1},{6,2},{7,3},{8,12},{9,13},{10,... | collective-permute-start | bytes 110600 | tf_op jit(solution)/shard_map/ppermute | solution.py:519
  32.9 1.3 %collective-permute-start.9 = (bf16[144,128]{1,0:T(8,128)(2,1)S(1)}, bf16[144,128]{1,0:T(8,128)(2,1)S(1)}, u32[]{:S(2)}, u32[]{:S(2)}) collective-permute-start(bf16[144,128]{1,0:T(8,128)(2,1)S(1)} %fusion.6.mine_ref), channel_id=1, source_target_pairs={{0,16},{16,0},{1,17},{17,1},{2,18},{18,2},{3,19},{19,3},{4,20},{20... | collective-permute-start | bytes 110600 | tf_op jit(solution)/shard_map/ppermute | solution.py:528

commit v4 on v3

--- a/solution.py
+++ b/solution.py
@@ -89,12 +89,15 @@
     out_ref[:, :frames] = jnp.where(carries, stack, held[:, :frames].astype(F32)).astype(BF16)
 
 
-def project_kernel(count, *refs):
+def project_kernel(count, final_ref, *refs):
     sources, held = refs[:count], refs[count : 2 * count]
-    projected_ref, hidden_ref, squeezed_ref, sems = refs[2 * count :]
+    final_out, final_held = refs[-3], refs[-2]
+    final_copy = pltpu.make_async_copy(final_ref, final_held, refs[-1].at[count])
+    projected_ref, hidden_ref, squeezed_ref, _, _, sems = refs[2 * count :]
     copies = [pltpu.make_async_copy(a, b, sems.at[i]) for i, (a, b) in enumerate(zip(sources, held))]
     for copy in copies:
         copy.start()
+    final_copy.start()
     for copy in copies[:3]:
         copy.wait()
     projected, hidden, squeezed = forward_rows(held[0][...], held[1][...], held[2][...])
@@ -103,6 +106,8 @@
     squeezed_ref[...] = squeezed
     for copy in copies[3:]:
         copy.wait()
+    final_copy.wait()
+    final_out[...] = final_held[...].reshape(final_out.shape)
 
 
 def shifted(values, taps, sign):
@@ -113,6 +118,14 @@
         moved = values if amount == 0 else pltpu.roll(values, amount, 0)
         pieces.append(moved.astype(BF16))
     return pieces
+
+
+PACK = (264, 160, 0, 240, 284)
+PACKED = 288
+
+
+def final_rows(s, n):
+    return min(s * (PK * C2 // n) // LANES, PK * C2 // LANES - 2)
 
 
 def pieces_of(n, count, rows):
@@ -222,82 +235,67 @@
             )
     upstream = jnp.concatenate(upstream, axis=1)
     slopes.append(slope)
-    grads = []
+    if packed:
+        payload_ref, scratch = outs
+        mine = [seq ^ s for s in range(n)]
+
+        def block(s):
+            q, z = mine[s] & 3, mine[s] >> 2
+            holder = (z ^ (z >> 1)) & 1
+            return holder ^ odd, jnp.where(holder == 0, q, (q >> 1) | ((q & 1) << 1)), z >> 1
+
+    def keep(layer, tap, grad):
+        channels, cols = grad.shape
+        if not packed:
+            outs[layer + 1][tap * channels : (tap + 1) * channels, :] = grad
+            return
+        count = HK * channels // n
+        for s, at, start, offset, length in pieces_of(n, count, channels):
+            if at != tap:
+                continue
+            for h in range(cols // LANES):
+                piece = grad[start : start + length, h * LANES : (h + 1) * LANES]
+                first_row = PACK[layer] + h * count + offset
+                if layer == 2:
+                    payload_ref[(*block(s), slice(first_row, first_row + length))] = piece.astype(BF16)
+                else:
+                    scratch[s, first_row - PACK[1] : first_row - PACK[1] + length, :] = piece
+
     for layer in (2, 1, 0):
         delta = mask(upstream * slopes[layer + 1], inside)
         pieces = shifted(delta, HK, -1)
-        grads.append(dot(inputs[layer], jnp.concatenate(pieces, axis=1), TN))
+        rows = inputs[layer].T
         ref = weights[layer]
         width = ref.shape[0] // HK
         upstream = jnp.zeros((total, width), F32)
         for k, piece in enumerate(pieces):
             upstream = upstream + dot(piece, ref[k * width : (k + 1) * width, :], NT)
-    third, second, first = grads
+        for k, piece in enumerate(pieces):
+            keep(layer, k, dot(rows, piece))
     delta = mask(upstream * slopes[0], inside)
     delta_ref[...] = delta.astype(BF16)
     hidden = jnp.concatenate([hidden_ref[...], edge_hidden], axis=0)
     squeeze_grad = dot(mask(delta, window).astype(BF16), hidden, TN)
 
     if not packed:
-        squeeze_out, first_out, second_out, third_out, final_out = outs
-        squeeze_out[...] = squeeze_grad
-        for out, grad in ((first_out, first), (second_out, second), (third_out, third)):
-            width, cols = grad.shape[0], out.shape[1]
-            for k in range(HK):
-                out[k * width : (k + 1) * width, :] = grad[:, k * cols : (k + 1) * cols]
+        outs[0][...] = squeeze_grad
         for i, part in enumerate(final_grad):
-            final_out[:, i * LANES : (i + 1) * LANES] = part
+            outs[4][:, i * LANES : (i + 1) * LANES] = part
         return
 
-    (payload_ref, scratch) = outs
-    half = payload_ref.shape[3]
-    mine = [(seq ^ s) for s in range(n)]
-
-    def put(s, at, rows):
-        slot = mine[s]
-        while rows.shape[0]:
-            side, start = divmod(at, half)
-            length = min(rows.shape[0], half - start)
-            payload_ref[side ^ odd, slot & 3, slot >> 2, start : start + length, :] = rows[:length]
-            rows = rows[length:]
-            at += length
-
-    base = 0
-    for grad, channels, cols in ((third, C2, C2), (second, C1, C2)):
-        count = HK * channels // n
-        for s, tap, start, offset, length in pieces_of(n, count, channels):
-            for h in range(cols // LANES):
-                lanes = slice(tap * cols + h * LANES, tap * cols + (h + 1) * LANES)
-                scratch[s, base + h * count + offset : base + h * count + offset + length, :] = grad[
-                    start : start + length, lanes
-                ]
-        base += count * (cols // LANES)
     count = C0 // n
     for s in range(n):
         for h in range(squeeze_grad.shape[1] // LANES):
-            scratch[s, base + h * count : base + (h + 1) * count, :] = squeeze_grad[
+            first_row = PACK[3] - PACK[1] + h * count
+            scratch[s, first_row : first_row + count, :] = squeeze_grad[
                 s * count : (s + 1) * count, h * LANES : (h + 1) * LANES
             ]
-    base += count * (squeeze_grad.shape[1] // LANES)
-    count = HK * C0 // n
-    for s, tap, start, offset, length in pieces_of(n, count, C0):
-        scratch[s, base + offset : base + offset + length, :] = first[
-            start : start + length, tap * C1 : (tap + 1) * C1
-        ]
-    base += count
-    final_row = jnp.concatenate(final_grad, axis=1)
-    count = final_row.shape[1] // n
-    for s in range(n):
-        first_half = s * count // LANES * LANES
-        piece = final_row[:, first_half : first_half + 2 * LANES]
-        if piece.shape[1] < 2 * LANES:
-            piece = jnp.concatenate([piece, piece[:, :LANES]], axis=1)
-        amount = (first_half - s * count) % (2 * LANES)
-        piece = piece if amount == 0 else pltpu.roll(jnp.broadcast_to(piece, (8, 2 * LANES)), amount, 1)
-        scratch[s, base : base + 1, :] = piece[0:1, :LANES]
-        scratch[s, base + 1 :, :] = jnp.zeros((scratch.shape[1] - base - 1, LANES), F32)
-    for s in range(n):
-        put(s, 0, scratch[s].astype(BF16))
+        row = final_rows(s, n)
+        first_row = PACK[4] - PACK[1]
+        scratch[s, first_row : first_row + 1, :] = final_grad[row]
+        scratch[s, first_row + 1 : first_row + 2, :] = final_grad[row + 1]
+        scratch[s, first_row + 2 :, :] = jnp.zeros((PACKED - PACK[4] - 2, LANES), F32)
+        payload_ref[(*block(s), slice(PACK[1], PACKED))] = scratch[s].astype(BF16)
 
 
 def feature_kernel(
@@ -333,18 +331,18 @@
     final_scores_ref[...] = jnp.where(low & (lane < REACH), moved[0:1], kept)
 
 
-def unpack_kernel(factor, mine_ref, other_ref, squeeze_ref, first_ref, second_ref, third_ref, final_ref, both):
-    half = mine_ref.shape[0]
-    _, core = here()
-    both[pl.ds(pl.multiple_of(core * half, 16), half), :] = mine_ref[...].astype(F32) * factor
-    both[pl.ds(pl.multiple_of((1 - core) * half, 16), half), :] = other_ref[...].astype(F32) * factor
-    base = 0
-    for ref in (third_ref, second_ref, squeeze_ref, first_ref):
+def unpack_kernel(n, factor, mine_ref, other_ref, squeeze_ref, first_ref, second_ref, third_ref, final_ref, both):
+    both[...] = (mine_ref[...].astype(F32) + other_ref[...].astype(F32)) * factor
+    for base, ref in zip(PACK, (first_ref, second_ref, third_ref, squeeze_ref)):
         count = ref.shape[0]
         for h in range(ref.shape[1] // LANES):
-            ref[:, h * LANES : (h + 1) * LANES] = both[base : base + count, :]
-            base += count
-    final_ref[...] = both[base : base + 1, : final_ref.shape[1]]
+            ref[:, h * LANES : (h + 1) * LANES] = both[base + h * count : base + (h + 1) * count, :]
+    count = final_ref.shape[1]
+    at = here()[0] * count
+    at = at - jnp.minimum(lax.div(at, LANES), PK * C2 // LANES - 2) * LANES
+    pair = jnp.concatenate([both[PACK[4] : PACK[4] + 1, :], both[PACK[4] + 1 : PACK[4] + 2, :]], axis=1)
+    pair = pltpu.roll(jnp.broadcast_to(pair, (8, 2 * LANES)), 2 * LANES - at, 1)
+    final_ref[...] = pair[0:1, :count]
 
 
 def sds(shape, dtype):
@@ -414,26 +412,26 @@
         second_weight,
         third_weight,
     )
-    rows, projection, squeeze, cot, first, second, third, projected, hidden, squeezed = pl.pallas_call(
+    rows, projection, squeeze, cot, first, second, third, projected, hidden, squeezed, final = pl.pallas_call(
         functools.partial(project_kernel, len(sources)),
-        in_specs=[HBM] * len(sources),
-        out_specs=[VMEM] * (len(sources) + 3),
+        in_specs=[HBM] * (1 + len(sources)),
+        out_specs=[VMEM] * (len(sources) + 4),
         out_shape=[
             *[vmem(a.shape, a.dtype) for a in sources],
             vmem((frames, width), BF16),
             vmem((frames, width), BF16),
             vmem((frames, C0), F32),
+            vmem((1, PK * C2), BF16),
         ],
-        scratch_shapes=[pltpu.SemaphoreType.DMA((len(sources),))],
+        scratch_shapes=[pltpu.VMEM((PK * C2,), BF16), pltpu.SemaphoreType.DMA((len(sources) + 1,))],
         compiler_params=params(8),
         cost_estimate=cost(2 * frames * width * (feat + C0), 2 * feat * width),
         name="project",
-    )(*[hbm(a) for a in sources])
+    )(hbm(final_weight), *[hbm(a) for a in sources])
 
     if packed:
-        half = 144
-        grad_shapes = [sds((2, 4, 4, half, LANES), BF16)]
-        scratch = [pltpu.VMEM((n, 2 * half, LANES), F32)]
+        grad_shapes = [sds((2, 4, 2, PACKED, LANES), BF16)]
+        scratch = [pltpu.VMEM((n, PACKED - PACK[1], LANES), F32)]
     else:
         grad_shapes = [
             sds((C0, width), F32),
@@ -468,7 +466,7 @@
         first,
         second,
         third,
-        final_weight.reshape(1, PK * C2),
+        final,
     )
 
     def features_back():
@@ -511,20 +509,22 @@
             total = total + term.astype(F32)
         return total.astype(BF16)
 
+    def mixed(zero, one):
+        return [(i, i ^ zero) for i in range(n)] + [(n + i, n + (i ^ one)) for i in range(n)]
+
     swap = [(0, 1), (1, 0)]
     (payload,) = grads
-    held = added(payload[0], lax.ppermute(payload[1], "dp", swap))
-    for stride in (1, 4):
-        moved = [
-            lax.ppermute(held[j], "seq", [(i, i ^ (j * stride)) for i in range(n)]) for j in (3, 1, 2)
-        ]
-        held = added(held[0], *moved)
-        if stride == 1:
-            own_grad, back = features_back()
-            held, own_grad = lax.optimization_barrier((held, own_grad))
-        else:
-            feature_grad, scores = assembled(own_grad, back)
-            held, feature_grad, scores = lax.optimization_barrier((held, feature_grad, scores))
+    came = lax.ppermute(payload[1], "dp", swap)
+    own_grad, back = features_back()
+    came, own_grad = lax.optimization_barrier((came, own_grad))
+    held = added(payload[0], came)
+    moved = [lax.ppermute(held[j], ("dp", "seq"), mixed(j, (j >> 1) | ((j & 1) << 1))) for j in (1, 3, 2)]
+    held, back = lax.optimization_barrier((added(held[0], *moved), back))
+    held = added(
+        lax.ppermute(held[1], ("dp", "seq"), mixed(12, 8)), lax.ppermute(held[0], ("dp", "seq"), mixed(0, 4))
+    )
+    feature_grad, scores = assembled(own_grad, back)
+    held, feature_grad, scores = lax.optimization_barrier((held, feature_grad, scores))
     other = lax.ppermute(held, "dp", swap)
     shapes = [
         (C0 // n, width),
@@ -534,11 +534,11 @@
         (1, PK * C2 // n),
     ]
     *shares, final = pl.pallas_call(
-        functools.partial(unpack_kernel, factor),
+        functools.partial(unpack_kernel, n, factor),
         in_specs=[VMEM, VMEM],
         out_specs=[VMEM] * 5,
         out_shape=[sds(shape, F32) for shape in shapes],
-        scratch_shapes=[pltpu.VMEM((2 * half, LANES), F32)],
+        scratch_shapes=[pltpu.VMEM((PACKED, LANES), F32)],
         compiler_params=params(4),
         name="unpack",
     )(held, other)

time: 35.1 us -> 33.7 us (0.960)
  starting transfers between devices: 12.4 us -> 11.4 us
  waiting for transfers between devices: 11.9 us -> 12.6 us
  local copies, waits for them, and re-layouts: 0.77 us -> 0.08 us
  Pallas kernels: 8.84 us -> 8.38 us
    ppermute x7 -> x6, starting transfers between devices: 10.4 us -> 9.05 us  [the longest x3 5.41 us: shards(): lax.ppermute(held[j], ('dp', 'seq'), mixed(j, j >> 1 | (j & 1) << 1))]
    reshape x1 -> x0, local copies, waits for them, and re-layouts: 0.68 us -> none  [shards(): final_weight.reshape(1, PK * C2)]
    ppermute x1, waiting for transfers between devices: 1.58 us -> 2.25 us  [shards(): edge = lax.ppermute(edge, ('dp', 'seq'), along)]
    pallas_call x1, Pallas kernels: 3.74 us -> 3.26 us  [shards(): pl.pallas_call(functools.partial(head_kernel, n, packed), in_specs=[VMEM]...]
    ppermute x7 -> x6, waiting for transfers between devices: 9.11 us -> 9.43 us  [the longest x3 5.88 us: shards(): lax.ppermute(held[j], ('dp', 'seq'), mixed(j, j >> 1 | (j & 1) << 1))]
  transfers between devices with their start and end apart: 10 -> 9, of which waited for: 7 -> 6; matrix products, arithmetic and copies ran while one was open for 2% -> 0% of each run, Pallas kernels for 10% -> 11%
where the time goes in v4:
time: 33.7 us; the launch traced here: 33.5 us
  waiting for transfers between devices  12.6 us (37%)
  starting transfers between devices  11.4 us (34%)
  Pallas kernels  8.38 us (25%)
  between operations  0.73 us (2%)
    ppermute x3, waiting for transfers between devices, shards(): lax.ppermute(held[j], ('dp', 'seq'), mixed(j, j >> 1 | (j & 1) << 1))  5.88 us
    ppermute x3, starting transfers between devices, shards(): lax.ppermute(held[j], ('dp', 'seq'), mixed(j, j >> 1 | (j & 1) << 1))  5.41 us
    pallas_call x1, Pallas kernels, shards(): pl.pallas_call(functools.partial(head_kernel, n, packed), in_specs=[VMEM]...  3.26 us
    ppermute x1, starting transfers between devices, shards(): lax.ppermute(held[1], ('dp', 'seq'), mixed(12, 8))  2.93 us
    ppermute x1, waiting for transfers between devices, shards(): lax.ppermute(held[1], ('dp', 'seq'), mixed(12, 8))  2.36 us
    ppermute x1, waiting for transfers between devices, shards(): edge = lax.ppermute(edge, ('dp', 'seq'), along)  2.25 us
    pallas_call x1, Pallas kernels, shards(): pl.pallas_call(functools.partial(project_kernel, len(sources)), in_specs=...  2.12 us
    ppermute x1, starting transfers between devices, features_back(): back = lax.ppermute(back, ('dp', 'seq'), returning)  1.46 us
  transfers between devices with their start and end apart: 9, of which 6 were waited for; matrix products, arithmetic and copies ran while one was open for 0% of the time, Pallas kernels for 11%

profile of v4, /device:TPU:0, one launch (start us, length us, event | category | flops | bytes accessed | tf_op | source)
XLA Modules:
  0.0 33.5 jit_solution(13827186857581532178)
XLA Ops:
  0.6 0.8 %edge.1 = bf16[32,512]{1,0:T(8,128)(2,1)S(1)} custom-call(bf16[128,512]{1,0:T(8,128)(2,1)} %bitcast.23, f32[1,128]{1,0:T(1,128)} %cot_ref.1), custom_call_target="tpu_custom_call" | custom-call | tf_op jit(solution)/shard_map/edge/pallas_call | solution.py:396
  1.4 0.5 %collective-permute-start = (bf16[32,512]{1,0:T(8,128)(2,1)S(1)}, bf16[32,512]{1,0:T(8,128)(2,1)S(1)}, u32[]{:S(2)}, u32[]{:S(2)}) collective-permute-start(bf16[32,512]{1,0:T(8,128)(2,1)S(1)} %edge.1), channel_id=1, source_target_pairs={{0,16},{1,0},{2,1},{3,2},{4,3},{5,4},{6,5},{7,6},{8,7},{9,8},{10,9... | collective-permute-start | bytes 98312 | tf_op jit(solution)/shard_map/ppermute | solution.py:404
  1.9 2.1 %project.1 = (bf16[128,512]{1,0:T(8,128)(2,1)S(1)}, bf16[512,768]{1,0:T(8,128)(2,1)S(1)}, bf16[64,768]{1,0:T(8,128)(2,1)S(1)}, f32[1,128]{1,0:T(1,128)S(1)}, bf1...) custom-call(bf16[768]{0:T(1024)(128)(2,1)} %final_ref.1, ...), custom_call_target="tpu_custom_call" | custom-call | flops 113246208 | bytes 786432 | tf_op jit(solution)/shard_map/project/pallas_call | solution.py:415
  4.1 2.2 %collective-permute-done.edge_ref = bf16[32,512]{1,0:T(8,128)(2,1)S(1)} collective-permute-done((bf16[32,512]{1,0:T(8,128)(2,1)S(1)}, bf16[32,512]{1,0:T(8,128)(2,1)S(1)}, u32[]{:S(2)}, u32[]{:S(2)}) %collective-permute-start) | collective-permute-done | bytes 32800 | tf_op jit(solution)/shard_map/ppermute | solution.py:404
  6.3 3.3 %head.1 = (f32[1,128]{1,0:T(1,128)S(1)}, f32[1,128]{1,0:T(1,128)S(1)}, bf16[160,64]{1,0:T(8,128)(2,1)S(1)}, bf16[32,768]{1,0:T(8,128)(2,1)S(1)}, bf16[2,4,2,288,128]{4,3,2,1,0:T(8,128)(2,1)S(1)}) custom-call(f32[128,64]{1,0:T(8,128)S(1)} %get-tuple-element.39.squeezed_ref, bf16[32,512]{1,0:T(8,128)(2,1)S(1)} %collective-permute-done.edge_ref, ...), custom_call_target="tpu_custom_call" | custom-call | flops 1000000000 | bytes 4000000 | tf_op jit(solution)/shard_map/head/pallas_call | solution.py:444
  9.6 0.1 collective-permute-start.1
  9.7 0.8 %feature.1 = (f32[128,512]{1,0:T(8,128)S(1)}, f32[24,512]{1,0:T(8,128)S(1)}) custom-call(bf16[128,512]{1,0:T(8,128)(2,1)S(1)} %get-tuple-element.49.rows_ref, bf16[32,512]{1,0:T(8,128)(2,1)S(1)} %collective-permute-done.edge_ref, bf16[128,768]{1,0:T(8,128)(2,1)S(1)} %get-tuple-element.50.projected_ref, ...), custom_call_target="tpu_custom_call" | custom-call | flops 113246208 | bytes 786432 | tf_op jit(solution)/shard_map/feature/pallas_call | solution.py:473
  10.5 1.2 %collective-permute-done.1 = bf16[4,2,288,128]{3,2,1,0:T(8,128)(2,1)S(1)} collective-permute-done((bf16[4,2,288,128]{3,2,1,0:T(8,128)(2,1)S(1)}, bf16[4,2,288,128]{3,2,1,0:T(8,128)(2,1)S(1)}, u32[]{:S(2)}, u32[]{:S(2)}) %collective-permute-start.1) | collective-permute-done | bytes 589856 | tf_op jit(solution)/shard_map/ppermute | solution.py:517
  11.7 0.2 fusion
  11.9 3.0 %collective-permute-start.2 = (bf16[2,288,128]{2,1,0:T(8,128)(2,1)S(1)}, bf16[2,288,128]{2,1,0:T(8,128)(2,1)S(1)}, u32[]{:S(2)}, u32[]{:S(2)}) collective-permute-start(bf16[2,288,128]{2,1,0:T(8,128)(2,1)S(1)} %get-tuple-element.71), channel_id=1, source_target_pairs={{0,1},{1,0},{2,3},{3,2},{4,5},{5,4},{6,7},{7,6},{8,9},{9,8},{10,11... | collective-permute-start | bytes 442376 | tf_op jit(solution)/shard_map/ppermute | solution.py:521
  14.9 2.4 %collective-permute-start.4 = (bf16[2,288,128]{2,1,0:T(8,128)(2,1)S(1)}, bf16[2,288,128]{2,1,0:T(8,128)(2,1)S(1)}, u32[]{:S(2)}, u32[]{:S(2)}) collective-permute-start(bf16[2,288,128]{2,1,0:T(8,128)(2,1)S(1)} %get-tuple-element.72), channel_id=1, source_target_pairs={{0,2},{1,3},{2,0},{3,1},{4,6},{5,7},{6,4},{7,5},{8,10},{9,11},{10,... | collective-permute-start | bytes 442376 | tf_op jit(solution)/shard_map/ppermute | solution.py:521
  17.3 0.0 collective-permute-start.3
  17.3 1.5 %collective-permute-start.5 = (f32[24,512]{1,0:T(8,128)S(1)}, f32[24,512]{1,0:T(8,128)S(1)}, u32[]{:S(2)}, u32[]{:S(2)}) collective-permute-start(f32[24,512]{1,0:T(8,128)S(1)} %get-tuple-element.56), channel_id=1, source_target_pairs={{0,1},{1,2},{2,3},{3,4},{4,5},{5,6},{6,7},{7,8},{8,9},{9,10},{10,1... | collective-permute-start | bytes 147464 | tf_op jit(solution)/shard_map/ppermute | solution.py:482
  18.8 0.0 collective-permute-done.2
  18.8 4.9 %collective-permute-done.4 = bf16[2,288,128]{2,1,0:T(8,128)(2,1)S(1)} collective-permute-done((bf16[2,288,128]{2,1,0:T(8,128)(2,1)S(1)}, bf16[2,288,128]{2,1,0:T(8,128)(2,1)S(1)}, u32[]{:S(2)}, u32[]{:S(2)}) %collective-permute-start.4) | collective-permute-done | bytes 147488 | tf_op jit(solution)/shard_map/ppermute | solution.py:521
  23.7 1.0 %collective-permute-done.3 = bf16[2,288,128]{2,1,0:T(8,128)(2,1)S(1)} collective-permute-done((bf16[2,288,128]{2,1,0:T(8,128)(2,1)S(1)}, bf16[2,288,128]{2,1,0:T(8,128)(2,1)S(1)}, u32[]{:S(2)}, u32[]{:S(2)}) %collective-permute-start.3) | collective-permute-done | bytes 147488 | tf_op jit(solution)/shard_map/ppermute | solution.py:521
  24.7 0.1 fusion.3
  24.8 0.0 collective-permute-done.5.back_ref
  24.8 2.9 %collective-permute-start.6 = (bf16[288,128]{1,0:T(8,128)(2,1)S(1)}, bf16[288,128]{1,0:T(8,128)(2,1)S(1)}, u32[]{:S(2)}, u32[]{:S(2)}) collective-permute-start(bf16[288,128]{1,0:T(8,128)(2,1)S(1)} %get-tuple-element.74), channel_id=1, source_target_pairs={{0,12},{1,13},{2,14},{3,15},{4,8},{5,9},{6,10},{7,11},{8,4},{9,5},... | collective-permute-start | bytes 221192 | tf_op jit(solution)/shard_map/ppermute | solution.py:524
  27.7 0.7 %collective-permute-start.7 = (bf16[288,128]{1,0:T(8,128)(2,1)S(1)}, bf16[288,128]{1,0:T(8,128)(2,1)S(1)}, u32[]{:S(2)}, u32[]{:S(2)}) collective-permute-start(bf16[288,128]{1,0:T(8,128)(2,1)S(1)} %get-tuple-element.75), channel_id=1, source_target_pairs={{0,0},{1,1},{2,2},{3,3},{4,4},{5,5},{6,6},{7,7},{8,8},{9,9},{10,10... | collective-permute-start | bytes 221192 | tf_op jit(solution)/shard_map/ppermute | solution.py:524
  28.4 0.7 %assemble.1 = (f32[128,512]{1,0:T(8,128)}, f32[1,128]{1,0:T(1,128)}) custom-call(f32[128,512]{1,0:T(8,128)S(1)} %get-tuple-element.58.own_ref, f32[1,128]{1,0:T(1,128)S(1)} %get-tuple-element.59.scores_ref, f32[24,512]{1,0:T(8,128)S(1)} %collective-permute-done.5.back_ref), custom_call_target="tpu_custom_call" | custom-call | flops 65536 | bytes 524288 | tf_op jit(solution)/shard_map/assemble/pallas_call | solution.py:486
  29.1 2.4 %collective-permute-done.6 = bf16[288,128]{1,0:T(8,128)(2,1)S(1)} collective-permute-done((bf16[288,128]{1,0:T(8,128)(2,1)S(1)}, bf16[288,128]{1,0:T(8,128)(2,1)S(1)}, u32[]{:S(2)}, u32[]{:S(2)}) %collective-permute-start.6) | collective-permute-done | bytes 73760 | tf_op jit(solution)/shard_map/ppermute | solution.py:524
  31.5 0.0 collective-permute-done.7
  31.5 0.4 %collective-permute-start.8 = (bf16[288,128]{1,0:T(8,128)(2,1)S(1)}, bf16[288,128]{1,0:T(8,128)(2,1)S(1)}, u32[]{:S(2)}, u32[]{:S(2)}) collective-permute-start(bf16[288,128]{1,0:T(8,128)(2,1)S(1)} %add_convert_fusion.mine_ref), channel_id=1, source_target_pairs={{0,16},{16,0},{1,17},{17,1},{2,18},{18,2},{3,19},{19,3},{4,20},{20... | collective-permute-start | bytes 221192 | tf_op jit(solution)/shard_map/ppermute | solution.py:528
  31.9 0.9 %collective-permute-done.8.other_ref = bf16[288,128]{1,0:T(8,128)(2,1)S(1)} collective-permute-done((bf16[288,128]{1,0:T(8,128)(2,1)S(1)}, bf16[288,128]{1,0:T(8,128)(2,1)S(1)}, u32[]{:S(2)}, u32[]{:S(2)}) %collective-permute-start.8) | collective-permute-done | bytes 73760 | tf_op jit(solution)/shard_map/ppermute | solution.py:528
  32.8 0.7 %unpack.1 = (f32[4,768]{1,0:T(4,128)}, f32[20,128]{1,0:T(8,128)}, f32[40,256]{1,0:T(8,128)}, f32[80,256]{1,0:T(8,128)}, f32[1,48]{1,0:T(1,128)}) custom-call(bf16[288,128]{1,0:T(8,128)(2,1)S(1)} %add_convert_fusion.mine_ref, bf16[288,128]{1,0:T(8,128)(2,1)S(1)} %collective-permute-done.8.other_ref), custom_call_target="tpu_custom_call" | custom-call | tf_op jit(solution)/shard_map/unpack/pallas_call | solution.py:536
  (4 shorter events, 0.1 us)
Async XLA Ops:
  1.4 4.9 %collective-permute-start = (bf16[32,512]{1,0:T(8,128)(2,1)S(1)}, bf16[32,512]{1,0:T(8,128)(2,1)S(1)}, u32[]{:S(2)}, u32[]{:S(2)}) collective-permute-start(bf16[32,512]{1,0:T(8,128)(2,1)S(1)} %edge.1), channel_id=1, source_target_pairs={{0,16},{1,0},{2,1},{3,2},{4,3},{5,4},{6,5},{7,6},{8,7},{9,8},{10,9... | collective-permute-start | bytes 98312 | tf_op jit(solution)/shard_map/ppermute | solution.py:404
  9.6 2.1 %collective-permute-start.1 = (bf16[4,2,288,128]{3,2,1,0:T(8,128)(2,1)S(1)}, bf16[4,2,288,128]{3,2,1,0:T(8,128)(2,1)S(1)}, u32[]{:S(2)}, u32[]{:S(2)}) collective-permute-start(bf16[4,2,288,128]{3,2,1,0:T(8,128)(2,1)S(1)} %slice_bitcast_fusion), channel_id=1, source_target_pairs={{0,16},{16,0},{1,17},{17,1},{2,18},{18,2},{3,19},{19,3},{4,20},{20... | collective-permute-start | bytes 1769480 | tf_op jit(solution)/shard_map/ppermute | solution.py:517
  11.9 6.9 %collective-permute-start.2 = (bf16[2,288,128]{2,1,0:T(8,128)(2,1)S(1)}, bf16[2,288,128]{2,1,0:T(8,128)(2,1)S(1)}, u32[]{:S(2)}, u32[]{:S(2)}) collective-permute-start(bf16[2,288,128]{2,1,0:T(8,128)(2,1)S(1)} %get-tuple-element.71), channel_id=1, source_target_pairs={{0,1},{1,0},{2,3},{3,2},{4,5},{5,4},{6,7},{7,6},{8,9},{9,8},{10,11... | collective-permute-start | bytes 442376 | tf_op jit(solution)/shard_map/ppermute | solution.py:521
  14.9 8.8 %collective-permute-start.4 = (bf16[2,288,128]{2,1,0:T(8,128)(2,1)S(1)}, bf16[2,288,128]{2,1,0:T(8,128)(2,1)S(1)}, u32[]{:S(2)}, u32[]{:S(2)}) collective-permute-start(bf16[2,288,128]{2,1,0:T(8,128)(2,1)S(1)} %get-tuple-element.72), channel_id=1, source_target_pairs={{0,2},{1,3},{2,0},{3,1},{4,6},{5,7},{6,4},{7,5},{8,10},{9,11},{10,... | collective-permute-start | bytes 442376 | tf_op jit(solution)/shard_map/ppermute | solution.py:521
  17.3 7.4 %collective-permute-start.3 = (bf16[2,288,128]{2,1,0:T(8,128)(2,1)S(1)}, bf16[2,288,128]{2,1,0:T(8,128)(2,1)S(1)}, u32[]{:S(2)}, u32[]{:S(2)}) collective-permute-start(bf16[2,288,128]{2,1,0:T(8,128)(2,1)S(1)} %get-tuple-element.73), channel_id=1, source_target_pairs={{0,3},{1,2},{2,1},{3,0},{4,7},{5,6},{6,5},{7,4},{8,11},{9,10},{10,... | collective-permute-start | bytes 442376 | tf_op jit(solution)/shard_map/ppermute | solution.py:521
  17.3 7.4 %collective-permute-start.5 = (f32[24,512]{1,0:T(8,128)S(1)}, f32[24,512]{1,0:T(8,128)S(1)}, u32[]{:S(2)}, u32[]{:S(2)}) collective-permute-start(f32[24,512]{1,0:T(8,128)S(1)} %get-tuple-element.56), channel_id=1, source_target_pairs={{0,1},{1,2},{2,3},{3,4},{4,5},{5,6},{6,7},{7,8},{8,9},{9,10},{10,1... | collective-permute-start | bytes 147464 | tf_op jit(solution)/shard_map/ppermute | solution.py:482
  24.8 6.7 %collective-permute-start.6 = (bf16[288,128]{1,0:T(8,128)(2,1)S(1)}, bf16[288,128]{1,0:T(8,128)(2,1)S(1)}, u32[]{:S(2)}, u32[]{:S(2)}) collective-permute-start(bf16[288,128]{1,0:T(8,128)(2,1)S(1)} %get-tuple-element.74), channel_id=1, source_target_pairs={{0,12},{1,13},{2,14},{3,15},{4,8},{5,9},{6,10},{7,11},{8,4},{9,5},... | collective-permute-start | bytes 221192 | tf_op jit(solution)/shard_map/ppermute | solution.py:524
  27.7 3.8 %collective-permute-start.7 = (bf16[288,128]{1,0:T(8,128)(2,1)S(1)}, bf16[288,128]{1,0:T(8,128)(2,1)S(1)}, u32[]{:S(2)}, u32[]{:S(2)}) collective-permute-start(bf16[288,128]{1,0:T(8,128)(2,1)S(1)} %get-tuple-element.75), channel_id=1, source_target_pairs={{0,0},{1,1},{2,2},{3,3},{4,4},{5,5},{6,6},{7,7},{8,8},{9,9},{10,10... | collective-permute-start | bytes 221192 | tf_op jit(solution)/shard_map/ppermute | solution.py:524
  31.5 1.3 %collective-permute-start.8 = (bf16[288,128]{1,0:T(8,128)(2,1)S(1)}, bf16[288,128]{1,0:T(8,128)(2,1)S(1)}, u32[]{:S(2)}, u32[]{:S(2)}) collective-permute-start(bf16[288,128]{1,0:T(8,128)(2,1)S(1)} %add_convert_fusion.mine_ref), channel_id=1, source_target_pairs={{0,16},{16,0},{1,17},{17,1},{2,18},{18,2},{3,19},{19,3},{4,20},{20... | collective-permute-start | bytes 221192 | tf_op jit(solution)/shard_map/ppermute | solution.py:528

commit v5 on v4

--- a/solution.py
+++ b/solution.py
@@ -209,9 +209,13 @@
         slopes.append(slope)
         inputs.append(mask(unit, window).astype(BF16))
         width = unit.shape[1]
-        act = jnp.zeros((total, ref.shape[1]), F32)
-        for k, piece in enumerate(shifted(unit, HK, 1)):
-            act = act + dot(piece, ref[k * width : (k + 1) * width, :])
+        pieces = shifted(unit, HK, 1)
+        if width % LANES == 0:
+            act = dot(jnp.concatenate(pieces, axis=1), ref[...])
+        else:
+            act = jnp.zeros((total, ref.shape[1]), F32)
+            for k, piece in enumerate(pieces):
+                act = act + dot(piece, ref[k * width : (k + 1) * width, :])
     unit, slope = leaky_pair(act)
     final_in = mask(unit, inside).astype(BF16).astype(F32)
     taps = shifted(final_in, PK, 1)
@@ -299,7 +303,7 @@
 
 
 def feature_kernel(
-    rows_ref, edge_ref, projected_ref, edge_projected_ref, delta_ref, after_ref, squeeze_ref, projection_ref, out_ref, back_ref
+    rows_ref, edge_ref, projected_ref, edge_projected_ref, delta_ref, edge_scores_ref, squeeze_ref, projection_ref, out_ref, back_ref
 ):
     hidden_upstream = dot(delta_ref[...], squeeze_ref[...])
     projected = jnp.concatenate([projected_ref[...], edge_projected_ref[...]], axis=0)
@@ -311,8 +315,9 @@
     grad = normalize_back(normed_grad, normed, inverse)
     out_ref[...] = grad[:-EDGE]
     back_ref[:BACK, :] = jnp.where(here()[1] == 0, grad[-EDGE : BACK - EDGE], grad[-BACK:])
-    back_ref[BACK:, :LANES] = jnp.broadcast_to(after_ref[...], (8, LANES))
-    back_ref[BACK:, LANES:] = jnp.zeros((8, back_ref.shape[1] - LANES), F32)
+    row = lax.broadcasted_iota(jnp.int32, (BACK, LANES), 0)
+    spare = jnp.where(here()[1] == 0, row, BACK - 1 - row) >= REACH
+    back_ref[:, :LANES] = jnp.where(spare, edge_scores_ref[...], back_ref[:, :LANES])
 
 
 def assemble_kernel(n, own_ref, scores_ref, back_ref, grad_ref, final_scores_ref):
@@ -324,11 +329,12 @@
     came = back_ref[:BACK, :]
     grad_ref[:BACK, :] = jnp.where(low & (row < REACH), came, own_ref[:BACK, :])
     grad_ref[frames - BACK :, :] = jnp.where(high & (row >= BACK - REACH), came, own_ref[frames - BACK :, :])
-    scores = back_ref[BACK:, :LANES]
+    scores = back_ref[:8, :LANES]
+    scores = jnp.where(odd == 0, back_ref[BACK - 8 :, :LANES], scores)
     moved = pltpu.roll(scores, EDGE, 1)
     lane = lax.broadcasted_iota(jnp.int32, (1, frames), 1)
     kept = jnp.where(high & (lane >= frames - REACH), scores[0:1], scores_ref[...])
-    final_scores_ref[...] = jnp.where(low & (lane < REACH), moved[0:1], kept)
+    final_scores_ref[...] = jnp.where(low & (lane < REACH), moved[7:8], kept)
 
 
 def unpack_kernel(n, factor, mine_ref, other_ref, squeeze_ref, first_ref, second_ref, third_ref, final_ref, both):
@@ -474,7 +480,7 @@
             feature_kernel,
             in_specs=[VMEM] * 8,
             out_specs=[VMEM] * 2,
-            out_shape=[sds((frames, feat), F32), sds((BACK + 8, feat), F32)],
+            out_shape=[sds((frames, feat), F32), sds((BACK, feat), F32)],
             compiler_params=params(8),
             cost_estimate=cost(2 * frames * width * (feat + C0), 2 * feat * width),
             name="feature",

time: 33.7 us -> 33.3 us (0.988)
  no operation moved by 1% of the time
where the time goes in v5:
time: 33.3 us; the launch traced here: 33.1 us
  waiting for transfers between devices  12.5 us (38%)
  starting transfers between devices  11.4 us (34%)
  Pallas kernels  8.15 us (24%)
  between operations  0.73 us (2%)
    ppermute x3, waiting for transfers between devices, shards(): lax.ppermute(held[j], ('dp', 'seq'), mixed(j, j >> 1 | (j & 1) << 1))  5.71 us
    ppermute x3, starting transfers between devices, shards(): lax.ppermute(held[j], ('dp', 'seq'), mixed(j, j >> 1 | (j & 1) << 1))  5.41 us
    pallas_call x1, Pallas kernels, shards(): pl.pallas_call(functools.partial(head_kernel, n, packed), in_specs=[VMEM]...  3.02 us
    ppermute x1, starting transfers between devices, shards(): lax.ppermute(held[1], ('dp', 'seq'), mixed(12, 8))  2.92 us
    ppermute x1, waiting for transfers between devices, shards(): lax.ppermute(held[1], ('dp', 'seq'), mixed(12, 8))  2.36 us
    ppermute x1, waiting for transfers between devices, shards(): edge = lax.ppermute(edge, ('dp', 'seq'), along)  2.25 us
    pallas_call x1, Pallas kernels, shards(): pl.pallas_call(functools.partial(project_kernel, len(sources)), in_specs=...  2.12 us
    ppermute x1, starting transfers between devices, features_back(): back = lax.ppermute(back, ('dp', 'seq'), returning)  1.46 us
  transfers between devices with their start and end apart: 9, of which 6 were waited for; matrix products, arithmetic and copies ran while one was open for 0% of the time, Pallas kernels for 11%

profile of v5, /device:TPU:0, one launch (start us, length us, event | category | flops | bytes accessed | tf_op | source)
XLA Modules:
  0.0 33.1 jit_solution(18411411680415450542)
XLA Ops:
  0.6 0.8 %edge.1 = bf16[32,512]{1,0:T(8,128)(2,1)S(1)} custom-call(bf16[128,512]{1,0:T(8,128)(2,1)} %bitcast.23, f32[1,128]{1,0:T(1,128)} %cot_ref.1), custom_call_target="tpu_custom_call" | custom-call | tf_op jit(solution)/shard_map/edge/pallas_call | solution.py:402
  1.4 0.5 %collective-permute-start = (bf16[32,512]{1,0:T(8,128)(2,1)S(1)}, bf16[32,512]{1,0:T(8,128)(2,1)S(1)}, u32[]{:S(2)}, u32[]{:S(2)}) collective-permute-start(bf16[32,512]{1,0:T(8,128)(2,1)S(1)} %edge.1), channel_id=1, source_target_pairs={{0,16},{1,0},{2,1},{3,2},{4,3},{5,4},{6,5},{7,6},{8,7},{9,8},{10,9... | collective-permute-start | bytes 98312 | tf_op jit(solution)/shard_map/ppermute | solution.py:410
  1.9 2.1 %project.1 = (bf16[128,512]{1,0:T(8,128)(2,1)S(1)}, bf16[512,768]{1,0:T(8,128)(2,1)S(1)}, bf16[64,768]{1,0:T(8,128)(2,1)S(1)}, f32[1,128]{1,0:T(1,128)S(1)}, bf1...) custom-call(bf16[768]{0:T(1024)(128)(2,1)} %final_ref.1, ...), custom_call_target="tpu_custom_call" | custom-call | flops 113246208 | bytes 786432 | tf_op jit(solution)/shard_map/project/pallas_call | solution.py:421
  4.1 2.2 %collective-permute-done.edge_ref = bf16[32,512]{1,0:T(8,128)(2,1)S(1)} collective-permute-done((bf16[32,512]{1,0:T(8,128)(2,1)S(1)}, bf16[32,512]{1,0:T(8,128)(2,1)S(1)}, u32[]{:S(2)}, u32[]{:S(2)}) %collective-permute-start) | collective-permute-done | bytes 32800 | tf_op jit(solution)/shard_map/ppermute | solution.py:410
  6.3 3.0 %head.1 = (f32[1,128]{1,0:T(1,128)S(1)}, f32[1,128]{1,0:T(1,128)S(1)}, bf16[160,64]{1,0:T(8,128)(2,1)S(1)}, bf16[32,768]{1,0:T(8,128)(2,1)S(1)}, bf16[2,4,2,288,128]{4,3,2,1,0:T(8,128)(2,1)S(1)}) custom-call(f32[128,64]{1,0:T(8,128)S(1)} %get-tuple-element.39.squeezed_ref, bf16[32,512]{1,0:T(8,128)(2,1)S(1)} %collective-permute-done.edge_ref, ...), custom_call_target="tpu_custom_call" | custom-call | flops 1000000000 | bytes 4000000 | tf_op jit(solution)/shard_map/head/pallas_call | solution.py:450
  9.4 0.1 collective-permute-start.1
  9.5 0.8 %feature.1 = (f32[128,512]{1,0:T(8,128)S(1)}, f32[16,512]{1,0:T(8,128)S(1)}) custom-call(bf16[128,512]{1,0:T(8,128)(2,1)S(1)} %get-tuple-element.49.rows_ref, bf16[32,512]{1,0:T(8,128)(2,1)S(1)} %collective-permute-done.edge_ref, bf16[128,768]{1,0:T(8,128)(2,1)S(1)} %get-tuple-element.50.projected_ref, ...), custom_call_target="tpu_custom_call" | custom-call | flops 113246208 | bytes 786432 | tf_op jit(solution)/shard_map/feature/pallas_call | solution.py:479
  10.3 1.2 %collective-permute-done.1 = bf16[4,2,288,128]{3,2,1,0:T(8,128)(2,1)S(1)} collective-permute-done((bf16[4,2,288,128]{3,2,1,0:T(8,128)(2,1)S(1)}, bf16[4,2,288,128]{3,2,1,0:T(8,128)(2,1)S(1)}, u32[]{:S(2)}, u32[]{:S(2)}) %collective-permute-start.1) | collective-permute-done | bytes 589856 | tf_op jit(solution)/shard_map/ppermute | solution.py:523
  11.5 0.2 fusion
  11.7 3.0 %collective-permute-start.2 = (bf16[2,288,128]{2,1,0:T(8,128)(2,1)S(1)}, bf16[2,288,128]{2,1,0:T(8,128)(2,1)S(1)}, u32[]{:S(2)}, u32[]{:S(2)}) collective-permute-start(bf16[2,288,128]{2,1,0:T(8,128)(2,1)S(1)} %get-tuple-element.71), channel_id=1, source_target_pairs={{0,1},{1,0},{2,3},{3,2},{4,5},{5,4},{6,7},{7,6},{8,9},{9,8},{10,11... | collective-permute-start | bytes 442376 | tf_op jit(solution)/shard_map/ppermute | solution.py:527
  14.7 2.4 %collective-permute-start.4 = (bf16[2,288,128]{2,1,0:T(8,128)(2,1)S(1)}, bf16[2,288,128]{2,1,0:T(8,128)(2,1)S(1)}, u32[]{:S(2)}, u32[]{:S(2)}) collective-permute-start(bf16[2,288,128]{2,1,0:T(8,128)(2,1)S(1)} %get-tuple-element.72), channel_id=1, source_target_pairs={{0,2},{1,3},{2,0},{3,1},{4,6},{5,7},{6,4},{7,5},{8,10},{9,11},{10,... | collective-permute-start | bytes 442376 | tf_op jit(solution)/shard_map/ppermute | solution.py:527
  17.1 0.0 collective-permute-start.3
  17.1 1.5 %collective-permute-start.5 = (f32[16,512]{1,0:T(8,128)S(1)}, f32[16,512]{1,0:T(8,128)S(1)}, u32[]{:S(2)}, u32[]{:S(2)}) collective-permute-start(f32[16,512]{1,0:T(8,128)S(1)} %get-tuple-element.56), channel_id=1, source_target_pairs={{0,1},{1,2},{2,3},{3,4},{4,5},{5,6},{6,7},{7,8},{8,9},{9,10},{10,1... | collective-permute-start | bytes 98312 | tf_op jit(solution)/shard_map/ppermute | solution.py:488
  18.6 0.0 collective-permute-done.2
  18.6 4.7 %collective-permute-done.4 = bf16[2,288,128]{2,1,0:T(8,128)(2,1)S(1)} collective-permute-done((bf16[2,288,128]{2,1,0:T(8,128)(2,1)S(1)}, bf16[2,288,128]{2,1,0:T(8,128)(2,1)S(1)}, u32[]{:S(2)}, u32[]{:S(2)}) %collective-permute-start.4) | collective-permute-done | bytes 147488 | tf_op jit(solution)/shard_map/ppermute | solution.py:527
  23.3 1.0 %collective-permute-done.3 = bf16[2,288,128]{2,1,0:T(8,128)(2,1)S(1)} collective-permute-done((bf16[2,288,128]{2,1,0:T(8,128)(2,1)S(1)}, bf16[2,288,128]{2,1,0:T(8,128)(2,1)S(1)}, u32[]{:S(2)}, u32[]{:S(2)}) %collective-permute-start.3) | collective-permute-done | bytes 147488 | tf_op jit(solution)/shard_map/ppermute | solution.py:527
  24.3 0.1 fusion.3
  24.4 0.0 collective-permute-done.5.back_ref
  24.4 2.9 %collective-permute-start.6 = (bf16[288,128]{1,0:T(8,128)(2,1)S(1)}, bf16[288,128]{1,0:T(8,128)(2,1)S(1)}, u32[]{:S(2)}, u32[]{:S(2)}) collective-permute-start(bf16[288,128]{1,0:T(8,128)(2,1)S(1)} %get-tuple-element.74), channel_id=1, source_target_pairs={{0,12},{1,13},{2,14},{3,15},{4,8},{5,9},{6,10},{7,11},{8,4},{9,5},... | collective-permute-start | bytes 221192 | tf_op jit(solution)/shard_map/ppermute | solution.py:530
  27.3 0.7 %collective-permute-start.7 = (bf16[288,128]{1,0:T(8,128)(2,1)S(1)}, bf16[288,128]{1,0:T(8,128)(2,1)S(1)}, u32[]{:S(2)}, u32[]{:S(2)}) collective-permute-start(bf16[288,128]{1,0:T(8,128)(2,1)S(1)} %get-tuple-element.75), channel_id=1, source_target_pairs={{0,0},{1,1},{2,2},{3,3},{4,4},{5,5},{6,6},{7,7},{8,8},{9,9},{10,10... | collective-permute-start | bytes 221192 | tf_op jit(solution)/shard_map/ppermute | solution.py:530
  28.0 0.7 %assemble.1 = (f32[128,512]{1,0:T(8,128)}, f32[1,128]{1,0:T(1,128)}) custom-call(f32[128,512]{1,0:T(8,128)S(1)} %get-tuple-element.58.own_ref, f32[1,128]{1,0:T(1,128)S(1)} %get-tuple-element.59.scores_ref, f32[16,512]{1,0:T(8,128)S(1)} %collective-permute-done.5.back_ref), custom_call_target="tpu_custom_call" | custom-call | flops 65536 | bytes 524288 | tf_op jit(solution)/shard_map/assemble/pallas_call | solution.py:492
  28.7 2.4 %collective-permute-done.6 = bf16[288,128]{1,0:T(8,128)(2,1)S(1)} collective-permute-done((bf16[288,128]{1,0:T(8,128)(2,1)S(1)}, bf16[288,128]{1,0:T(8,128)(2,1)S(1)}, u32[]{:S(2)}, u32[]{:S(2)}) %collective-permute-start.6) | collective-permute-done | bytes 73760 | tf_op jit(solution)/shard_map/ppermute | solution.py:530
  31.1 0.0 collective-permute-done.7
  31.1 0.4 %collective-permute-start.8 = (bf16[288,128]{1,0:T(8,128)(2,1)S(1)}, bf16[288,128]{1,0:T(8,128)(2,1)S(1)}, u32[]{:S(2)}, u32[]{:S(2)}) collective-permute-start(bf16[288,128]{1,0:T(8,128)(2,1)S(1)} %add_convert_fusion.mine_ref), channel_id=1, source_target_pairs={{0,16},{16,0},{1,17},{17,1},{2,18},{18,2},{3,19},{19,3},{4,20},{20... | collective-permute-start | bytes 221192 | tf_op jit(solution)/shard_map/ppermute | solution.py:534
  31.5 1.0 %collective-permute-done.8.other_ref = bf16[288,128]{1,0:T(8,128)(2,1)S(1)} collective-permute-done((bf16[288,128]{1,0:T(8,128)(2,1)S(1)}, bf16[288,128]{1,0:T(8,128)(2,1)S(1)}, u32[]{:S(2)}, u32[]{:S(2)}) %collective-permute-start.8) | collective-permute-done | bytes 73760 | tf_op jit(solution)/shard_map/ppermute | solution.py:534
  32.4 0.7 %unpack.1 = (f32[4,768]{1,0:T(4,128)}, f32[20,128]{1,0:T(8,128)}, f32[40,256]{1,0:T(8,128)}, f32[80,256]{1,0:T(8,128)}, f32[1,48]{1,0:T(1,128)}) custom-call(bf16[288,128]{1,0:T(8,128)(2,1)S(1)} %add_convert_fusion.mine_ref, bf16[288,128]{1,0:T(8,128)(2,1)S(1)} %collective-permute-done.8.other_ref), custom_call_target="tpu_custom_call" | custom-call | tf_op jit(solution)/shard_map/unpack/pallas_call | solution.py:542
  (4 shorter events, 0.1 us)
Async XLA Ops:
  1.4 4.9 %collective-permute-start = (bf16[32,512]{1,0:T(8,128)(2,1)S(1)}, bf16[32,512]{1,0:T(8,128)(2,1)S(1)}, u32[]{:S(2)}, u32[]{:S(2)}) collective-permute-start(bf16[32,512]{1,0:T(8,128)(2,1)S(1)} %edge.1), channel_id=1, source_target_pairs={{0,16},{1,0},{2,1},{3,2},{4,3},{5,4},{6,5},{7,6},{8,7},{9,8},{10,9... | collective-permute-start | bytes 98312 | tf_op jit(solution)/shard_map/ppermute | solution.py:410
  9.4 2.1 %collective-permute-start.1 = (bf16[4,2,288,128]{3,2,1,0:T(8,128)(2,1)S(1)}, bf16[4,2,288,128]{3,2,1,0:T(8,128)(2,1)S(1)}, u32[]{:S(2)}, u32[]{:S(2)}) collective-permute-start(bf16[4,2,288,128]{3,2,1,0:T(8,128)(2,1)S(1)} %slice_bitcast_fusion), channel_id=1, source_target_pairs={{0,16},{16,0},{1,17},{17,1},{2,18},{18,2},{3,19},{19,3},{4,20},{20... | collective-permute-start | bytes 1769480 | tf_op jit(solution)/shard_map/ppermute | solution.py:523
  11.7 6.9 %collective-permute-start.2 = (bf16[2,288,128]{2,1,0:T(8,128)(2,1)S(1)}, bf16[2,288,128]{2,1,0:T(8,128)(2,1)S(1)}, u32[]{:S(2)}, u32[]{:S(2)}) collective-permute-start(bf16[2,288,128]{2,1,0:T(8,128)(2,1)S(1)} %get-tuple-element.71), channel_id=1, source_target_pairs={{0,1},{1,0},{2,3},{3,2},{4,5},{5,4},{6,7},{7,6},{8,9},{9,8},{10,11... | collective-permute-start | bytes 442376 | tf_op jit(solution)/shard_map/ppermute | solution.py:527
  14.7 8.6 %collective-permute-start.4 = (bf16[2,288,128]{2,1,0:T(8,128)(2,1)S(1)}, bf16[2,288,128]{2,1,0:T(8,128)(2,1)S(1)}, u32[]{:S(2)}, u32[]{:S(2)}) collective-permute-start(bf16[2,288,128]{2,1,0:T(8,128)(2,1)S(1)} %get-tuple-element.72), channel_id=1, source_target_pairs={{0,2},{1,3},{2,0},{3,1},{4,6},{5,7},{6,4},{7,5},{8,10},{9,11},{10,... | collective-permute-start | bytes 442376 | tf_op jit(solution)/shard_map/ppermute | solution.py:527
  17.1 7.2 %collective-permute-start.3 = (bf16[2,288,128]{2,1,0:T(8,128)(2,1)S(1)}, bf16[2,288,128]{2,1,0:T(8,128)(2,1)S(1)}, u32[]{:S(2)}, u32[]{:S(2)}) collective-permute-start(bf16[2,288,128]{2,1,0:T(8,128)(2,1)S(1)} %get-tuple-element.73), channel_id=1, source_target_pairs={{0,3},{1,2},{2,1},{3,0},{4,7},{5,6},{6,5},{7,4},{8,11},{9,10},{10,... | collective-permute-start | bytes 442376 | tf_op jit(solution)/shard_map/ppermute | solution.py:527
  17.1 7.3 %collective-permute-start.5 = (f32[16,512]{1,0:T(8,128)S(1)}, f32[16,512]{1,0:T(8,128)S(1)}, u32[]{:S(2)}, u32[]{:S(2)}) collective-permute-start(f32[16,512]{1,0:T(8,128)S(1)} %get-tuple-element.56), channel_id=1, source_target_pairs={{0,1},{1,2},{2,3},{3,4},{4,5},{5,6},{6,7},{7,8},{8,9},{9,10},{10,1... | collective-permute-start | bytes 98312 | tf_op jit(solution)/shard_map/ppermute | solution.py:488
  24.4 6.7 %collective-permute-start.6 = (bf16[288,128]{1,0:T(8,128)(2,1)S(1)}, bf16[288,128]{1,0:T(8,128)(2,1)S(1)}, u32[]{:S(2)}, u32[]{:S(2)}) collective-permute-start(bf16[288,128]{1,0:T(8,128)(2,1)S(1)} %get-tuple-element.74), channel_id=1, source_target_pairs={{0,12},{1,13},{2,14},{3,15},{4,8},{5,9},{6,10},{7,11},{8,4},{9,5},... | collective-permute-start | bytes 221192 | tf_op jit(solution)/shard_map/ppermute | solution.py:530
  27.3 3.8 %collective-permute-start.7 = (bf16[288,128]{1,0:T(8,128)(2,1)S(1)}, bf16[288,128]{1,0:T(8,128)(2,1)S(1)}, u32[]{:S(2)}, u32[]{:S(2)}) collective-permute-start(bf16[288,128]{1,0:T(8,128)(2,1)S(1)} %get-tuple-element.75), channel_id=1, source_target_pairs={{0,0},{1,1},{2,2},{3,3},{4,4},{5,5},{6,6},{7,7},{8,8},{9,9},{10,10... | collective-permute-start | bytes 221192 | tf_op jit(solution)/shard_map/ppermute | solution.py:530
  31.1 1.3 %collective-permute-start.8 = (bf16[288,128]{1,0:T(8,128)(2,1)S(1)}, bf16[288,128]{1,0:T(8,128)(2,1)S(1)}, u32[]{:S(2)}, u32[]{:S(2)}) collective-permute-start(bf16[288,128]{1,0:T(8,128)(2,1)S(1)} %add_convert_fusion.mine_ref), channel_id=1, source_target_pairs={{0,16},{16,0},{1,17},{17,1},{2,18},{18,2},{3,19},{19,3},{4,20},{20... | collective-permute-start | bytes 221192 | tf_op jit(solution)/shard_map/ppermute | solution.py:534

commit v6 on v5

--- a/solution.py
+++ b/solution.py
@@ -56,13 +56,23 @@
 def forward_rows(rows, projection, squeeze):
     normed, _ = normalize(rows.astype(F32))
     projected = dot(normed.astype(BF16), projection).astype(BF16)
-    hidden_normed, _ = normalize(projected.astype(F32))
-    hidden = hidden_normed.astype(BF16)
-    return projected, hidden, dot(hidden, squeeze, NT)
+    wide = projected.astype(F32)
+    average = jnp.mean(wide, axis=-1, keepdims=True)
+    centred = wide - average
+    inverse = lax.rsqrt(jnp.mean(centred * centred, axis=-1, keepdims=True) + EPSILON)
+    sums = dot(jnp.ones((8, squeeze.shape[1]), BF16), squeeze, NT)[0:1]
+    squeezed = (dot(projected, squeeze, NT) - average * sums) * inverse
+    return projected, (centred * inverse).astype(BF16), squeezed
 
 
 def here():
     return lax.axis_index("seq"), lax.rem(lax.axis_index("dp"), 2)
+
+
+def in_parts(values):
+    high = values.astype(BF16).astype(F32)
+    middle = (values - high).astype(BF16).astype(F32)
+    return jnp.concatenate([high, middle, values - high - middle, jnp.zeros_like(values)], axis=0)
 
 
 def edge_kernel(rows_ref, cot_ref, out_ref, held, cot_held, sems):
@@ -77,11 +87,7 @@
         copy.start()
     copies[0].wait()
     cot = cot_held[...]
-    high = cot.astype(BF16).astype(F32)
-    middle = (cot - high).astype(BF16).astype(F32)
-    low = cot - high - middle
-    stack = jnp.concatenate([high, middle, low, jnp.zeros((MORE - 3, frames), F32)], axis=0)
-    stack = jnp.concatenate([stack] * (EDGE // MORE), axis=0)
+    stack = jnp.concatenate([in_parts(cot)] * (EDGE // 4), axis=0)
     row = lax.broadcasted_iota(jnp.int32, (EDGE, frames), 0)
     carries = (row < MORE) & (odd == 1) | (row >= EDGE - MORE) & (odd == 0)
     copies[1].wait()
@@ -314,10 +320,12 @@
     normed, inverse = normalize(rows.astype(F32))
     grad = normalize_back(normed_grad, normed, inverse)
     out_ref[...] = grad[:-EDGE]
-    back_ref[:BACK, :] = jnp.where(here()[1] == 0, grad[-EDGE : BACK - EDGE], grad[-BACK:])
+    gone = jnp.where(here()[1] == 0, grad[-EDGE : BACK - EDGE], grad[-BACK:])
     row = lax.broadcasted_iota(jnp.int32, (BACK, LANES), 0)
     spare = jnp.where(here()[1] == 0, row, BACK - 1 - row) >= REACH
-    back_ref[:, :LANES] = jnp.where(spare, edge_scores_ref[...], back_ref[:, :LANES])
+    back_ref[:, LANES:] = gone[:, LANES:].astype(BF16)
+    parts = jnp.concatenate([in_parts(edge_scores_ref[...])] * (BACK // 4), axis=0)
+    back_ref[:, :LANES] = jnp.where(spare, parts, gone[:, :LANES]).astype(BF16)
 
 
 def assemble_kernel(n, own_ref, scores_ref, back_ref, grad_ref, final_scores_ref):
@@ -326,15 +334,15 @@
     low, high = (odd == 0) & (seq > 0), (odd == 1) & (seq < n - 1)
     grad_ref[BACK : frames - BACK, :] = own_ref[BACK : frames - BACK, :]
     row = lax.broadcasted_iota(jnp.int32, (BACK, own_ref.shape[1]), 0)
-    came = back_ref[:BACK, :]
+    came = back_ref[...].astype(F32)
     grad_ref[:BACK, :] = jnp.where(low & (row < REACH), came, own_ref[:BACK, :])
     grad_ref[frames - BACK :, :] = jnp.where(high & (row >= BACK - REACH), came, own_ref[frames - BACK :, :])
-    scores = back_ref[:8, :LANES]
-    scores = jnp.where(odd == 0, back_ref[BACK - 8 :, :LANES], scores)
+    parts = jnp.where(odd == 0, came[BACK - 4 :, :LANES], came[:4, :LANES])
+    scores = jnp.broadcast_to(parts[0:1] + parts[1:2] + parts[2:3], (8, LANES))
     moved = pltpu.roll(scores, EDGE, 1)
     lane = lax.broadcasted_iota(jnp.int32, (1, frames), 1)
     kept = jnp.where(high & (lane >= frames - REACH), scores[0:1], scores_ref[...])
-    final_scores_ref[...] = jnp.where(low & (lane < REACH), moved[7:8], kept)
+    final_scores_ref[...] = jnp.where(low & (lane < REACH), moved[0:1], kept)
 
 
 def unpack_kernel(n, factor, mine_ref, other_ref, squeeze_ref, first_ref, second_ref, third_ref, final_ref, both):
@@ -480,7 +488,7 @@
             feature_kernel,
             in_specs=[VMEM] * 8,
             out_specs=[VMEM] * 2,
-            out_shape=[sds((frames, feat), F32), sds((BACK, feat), F32)],
+            out_shape=[sds((frames, feat), F32), sds((BACK, feat), BF16)],
             compiler_params=params(8),
             cost_estimate=cost(2 * frames * width * (feat + C0), 2 * feat * width),
             name="feature",
@@ -523,9 +531,10 @@
     came = lax.ppermute(payload[1], "dp", swap)
     own_grad, back = features_back()
     came, own_grad = lax.optimization_barrier((came, own_grad))
-    held = added(payload[0], came)
+    held = [added(payload[0, j], came[j]) for j in range(4)]
     moved = [lax.ppermute(held[j], ("dp", "seq"), mixed(j, (j >> 1) | ((j & 1) << 1))) for j in (1, 3, 2)]
-    held, back = lax.optimization_barrier((added(held[0], *moved), back))
+    held = [added(held[0][i], *(part[i] for part in moved)) for i in range(2)]
+    held, back = lax.optimization_barrier((held, back))
     held = added(
         lax.ppermute(held[1], ("dp", "seq"), mixed(12, 8)), lax.ppermute(held[0], ("dp", "seq"), mixed(0, 4))
     )

time: 33.3 us -> 32.9 us (0.988)
  Pallas kernels: 8.15 us -> 7.81 us
    ppermute x1, starting transfers between devices: 0.38 us -> 1.26 us  [shards(): other = lax.ppermute(held, 'dp', swap)]
    ppermute x3, waiting for transfers between devices: 5.71 us -> 4.96 us  [shards(): lax.ppermute(held[j], ('dp', 'seq'), mixed(j, j >> 1 | (j & 1) << 1))]
    ppermute x1, starting transfers between devices: 2.92 us -> 2.28 us  [shards(): lax.ppermute(held[1], ('dp', 'seq'), mixed(12, 8))]
    ppermute x1, waiting for transfers between devices: 2.36 us -> 2.7 us  [shards(): lax.ppermute(held[1], ('dp', 'seq'), mixed(12, 8))]
where the time goes in v6:
time: 32.9 us; the launch traced here: 32.7 us
  waiting for transfers between devices  12.2 us (37%)
  starting transfers between devices  11.7 us (36%)
  Pallas kernels  7.81 us (24%)
  between operations  0.71 us (2%)
    ppermute x3, starting transfers between devices, shards(): lax.ppermute(held[j], ('dp', 'seq'), mixed(j, j >> 1 | (j & 1) << 1))  5.4 us
    ppermute x3, waiting for transfers between devices, shards(): lax.ppermute(held[j], ('dp', 'seq'), mixed(j, j >> 1 | (j & 1) << 1))  4.96 us
    pallas_call x1, Pallas kernels, shards(): pl.pallas_call(functools.partial(head_kernel, n, packed), in_specs=[VMEM]...  2.84 us
    ppermute x1, waiting for transfers between devices, shards(): lax.ppermute(held[1], ('dp', 'seq'), mixed(12, 8))  2.7 us
    ppermute x1, waiting for transfers between devices, shards(): edge = lax.ppermute(edge, ('dp', 'seq'), along)  2.4 us
    ppermute x1, starting transfers between devices, shards(): lax.ppermute(held[1], ('dp', 'seq'), mixed(12, 8))  2.28 us
    pallas_call x1, Pallas kernels, shards(): pl.pallas_call(functools.partial(project_kernel, len(sources)), in_specs=...  1.97 us
    ppermute x1, starting transfers between devices, features_back(): back = lax.ppermute(back, ('dp', 'seq'), returning)  1.54 us
  transfers between devices with their start and end apart: 9, of which 6 were waited for; matrix products, arithmetic and copies ran while one was open for 0% of the time, Pallas kernels for 11%

profile of v6, /device:TPU:0, one launch (start us, length us, event | category | flops | bytes accessed | tf_op | source)
XLA Modules:
  0.0 32.7 jit_solution(6327930655994859102)
XLA Ops:
  0.6 0.8 %edge.1 = bf16[32,512]{1,0:T(8,128)(2,1)S(1)} custom-call(bf16[128,512]{1,0:T(8,128)(2,1)} %bitcast.33, f32[1,128]{1,0:T(1,128)} %cot_ref.1), custom_call_target="tpu_custom_call" | custom-call | tf_op jit(solution)/shard_map/edge/pallas_call | solution.py:410
  1.4 0.5 %collective-permute-start = (bf16[32,512]{1,0:T(8,128)(2,1)S(1)}, bf16[32,512]{1,0:T(8,128)(2,1)S(1)}, u32[]{:S(2)}, u32[]{:S(2)}) collective-permute-start(bf16[32,512]{1,0:T(8,128)(2,1)S(1)} %edge.1), channel_id=1, source_target_pairs={{0,16},{1,0},{2,1},{3,2},{4,3},{5,4},{6,5},{7,6},{8,7},{9,8},{10,9... | collective-permute-start | bytes 98312 | tf_op jit(solution)/shard_map/ppermute | solution.py:418
  1.9 2.0 %project.1 = (bf16[128,512]{1,0:T(8,128)(2,1)S(1)}, bf16[512,768]{1,0:T(8,128)(2,1)S(1)}, bf16[64,768]{1,0:T(8,128)(2,1)S(1)}, f32[1,128]{1,0:T(1,128)S(1)}, bf1...) custom-call(bf16[768]{0:T(1024)(128)(2,1)} %final_ref.1, ...), custom_call_target="tpu_custom_call" | custom-call | flops 113246208 | bytes 786432 | tf_op jit(solution)/shard_map/project/pallas_call | solution.py:429
  3.9 2.4 %collective-permute-done.edge_ref = bf16[32,512]{1,0:T(8,128)(2,1)S(1)} collective-permute-done((bf16[32,512]{1,0:T(8,128)(2,1)S(1)}, bf16[32,512]{1,0:T(8,128)(2,1)S(1)}, u32[]{:S(2)}, u32[]{:S(2)}) %collective-permute-start) | collective-permute-done | bytes 32800 | tf_op jit(solution)/shard_map/ppermute | solution.py:418
  6.3 2.8 %head.1 = (f32[1,128]{1,0:T(1,128)S(1)}, f32[1,128]{1,0:T(1,128)S(1)}, bf16[160,64]{1,0:T(8,128)(2,1)S(1)}, bf16[32,768]{1,0:T(8,128)(2,1)S(1)}, bf16[2,4,2,288,128]{4,3,2,1,0:T(8,128)(2,1)S(1)}) custom-call(f32[128,64]{1,0:T(8,128)S(1)} %get-tuple-element.40.squeezed_ref, bf16[32,512]{1,0:T(8,128)(2,1)S(1)} %collective-permute-done.edge_ref, ...), custom_call_target="tpu_custom_call" | custom-call | flops 1000000000 | bytes 4000000 | tf_op jit(solution)/shard_map/head/pallas_call | solution.py:458
  9.2 0.1 collective-permute-start.1
  9.3 0.8 %feature.1 = (f32[128,512]{1,0:T(8,128)S(1)}, bf16[16,512]{1,0:T(8,128)(2,1)S(1)}) custom-call(bf16[128,512]{1,0:T(8,128)(2,1)S(1)} %get-tuple-element.50.rows_ref, bf16[32,512]{1,0:T(8,128)(2,1)S(1)} %collective-permute-done.edge_ref, bf16[128,768]{1,0:T(8,128)(2,1)S(1)} %get-tuple-element.51.projected_ref, ...), custom_call_target="tpu_custom_call" | custom-call | flops 113246208 | bytes 786432 | tf_op jit(solution)/shard_map/feature/pallas_call | solution.py:487
  10.1 1.2 %collective-permute-done.1 = bf16[4,2,288,128]{3,2,1,0:T(8,128)(2,1)S(1)} collective-permute-done((bf16[4,2,288,128]{3,2,1,0:T(8,128)(2,1)S(1)}, bf16[4,2,288,128]{3,2,1,0:T(8,128)(2,1)S(1)}, u32[]{:S(2)}, u32[]{:S(2)}) %collective-permute-start.1) | collective-permute-done | bytes 589856 | tf_op jit(solution)/shard_map/ppermute | solution.py:531
  11.3 0.2 fusion.3
  11.5 2.1 %collective-permute-start.4 = (bf16[2,288,128]{2,1,0:T(8,128)(2,1)S(1)}, bf16[2,288,128]{2,1,0:T(8,128)(2,1)S(1)}, u32[]{:S(2)}, u32[]{:S(2)}) collective-permute-start(bf16[2,288,128]{2,1,0:T(8,128)(2,1)S(1)} %get-tuple-element.74), channel_id=1, source_target_pairs={{0,2},{1,3},{2,0},{3,1},{4,6},{5,7},{6,4},{7,5},{8,10},{9,11},{10,... | collective-permute-start | bytes 442376 | tf_op jit(solution)/shard_map/ppermute | solution.py:535
  13.6 2.8 %collective-permute-start.3 = (bf16[2,288,128]{2,1,0:T(8,128)(2,1)S(1)}, bf16[2,288,128]{2,1,0:T(8,128)(2,1)S(1)}, u32[]{:S(2)}, u32[]{:S(2)}) collective-permute-start(bf16[2,288,128]{2,1,0:T(8,128)(2,1)S(1)} %get-tuple-element.75), channel_id=1, source_target_pairs={{0,3},{1,2},{2,1},{3,0},{4,7},{5,6},{6,5},{7,4},{8,11},{9,10},{10,... | collective-permute-start | bytes 442376 | tf_op jit(solution)/shard_map/ppermute | solution.py:535
  16.4 0.5 %collective-permute-start.2 = (bf16[2,288,128]{2,1,0:T(8,128)(2,1)S(1)}, bf16[2,288,128]{2,1,0:T(8,128)(2,1)S(1)}, u32[]{:S(2)}, u32[]{:S(2)}) collective-permute-start(bf16[2,288,128]{2,1,0:T(8,128)(2,1)S(1)} %get-tuple-element.76), channel_id=1, source_target_pairs={{0,1},{1,0},{2,3},{3,2},{4,5},{5,4},{6,7},{7,6},{8,9},{9,8},{10,11... | collective-permute-start | bytes 442376 | tf_op jit(solution)/shard_map/ppermute | solution.py:535
  16.9 1.5 %collective-permute-start.5 = (bf16[16,512]{1,0:T(8,128)(2,1)S(1)}, bf16[16,512]{1,0:T(8,128)(2,1)S(1)}, u32[]{:S(2)}, u32[]{:S(2)}) collective-permute-start(bf16[16,512]{1,0:T(8,128)(2,1)S(1)} %get-tuple-element.57), channel_id=1, source_target_pairs={{0,1},{1,2},{2,3},{3,4},{4,5},{5,6},{6,7},{7,8},{8,9},{9,10},{10,1... | collective-permute-start | bytes 49160 | tf_op jit(solution)/shard_map/ppermute | solution.py:496
  18.4 0.0 collective-permute-done.4
  18.4 2.8 %collective-permute-done.3 = bf16[2,288,128]{2,1,0:T(8,128)(2,1)S(1)} collective-permute-done((bf16[2,288,128]{2,1,0:T(8,128)(2,1)S(1)}, bf16[2,288,128]{2,1,0:T(8,128)(2,1)S(1)}, u32[]{:S(2)}, u32[]{:S(2)}) %collective-permute-start.3) | collective-permute-done | bytes 147488 | tf_op jit(solution)/shard_map/ppermute | solution.py:535
  21.3 2.1 %collective-permute-done.2 = bf16[2,288,128]{2,1,0:T(8,128)(2,1)S(1)} collective-permute-done((bf16[2,288,128]{2,1,0:T(8,128)(2,1)S(1)}, bf16[2,288,128]{2,1,0:T(8,128)(2,1)S(1)}, u32[]{:S(2)}, u32[]{:S(2)}) %collective-permute-start.2) | collective-permute-done | bytes 147488 | tf_op jit(solution)/shard_map/ppermute | solution.py:535
  23.4 0.1 fusion.5
  23.5 0.0 collective-permute-done.5.back_ref
  23.5 2.3 %collective-permute-start.6 = (bf16[288,128]{1,0:T(8,128)(2,1)S(1)}, bf16[288,128]{1,0:T(8,128)(2,1)S(1)}, u32[]{:S(2)}, u32[]{:S(2)}) collective-permute-start(bf16[288,128]{1,0:T(8,128)(2,1)S(1)} %get-tuple-element.58), channel_id=1, source_target_pairs={{0,12},{1,13},{2,14},{3,15},{4,8},{5,9},{6,10},{7,11},{8,4},{9,5},... | collective-permute-start | bytes 221192 | tf_op jit(solution)/shard_map/ppermute | solution.py:539
  25.7 0.7 %collective-permute-start.7 = (bf16[288,128]{1,0:T(8,128)(2,1)S(1)}, bf16[288,128]{1,0:T(8,128)(2,1)S(1)}, u32[]{:S(2)}, u32[]{:S(2)}) collective-permute-start(bf16[288,128]{1,0:T(8,128)(2,1)S(1)} %get-tuple-element.59), channel_id=1, source_target_pairs={{0,0},{1,1},{2,2},{3,3},{4,4},{5,5},{6,6},{7,7},{8,8},{9,9},{10,10... | collective-permute-start | bytes 221192 | tf_op jit(solution)/shard_map/ppermute | solution.py:539
  26.4 0.7 %assemble.1 = (f32[128,512]{1,0:T(8,128)}, f32[1,128]{1,0:T(1,128)}) custom-call(f32[128,512]{1,0:T(8,128)S(1)} %get-tuple-element.60.own_ref, f32[1,128]{1,0:T(1,128)S(1)} %get-tuple-element.61.scores_ref, bf16[16,512]{1,0:T(8,128)(2,1)S(1)} %collective-permute-done.5.back_ref), custom_call_target="tpu_custom_call" | custom-call | flops 65536 | bytes 524288 | tf_op jit(solution)/shard_map/assemble/pallas_call | solution.py:500
  27.1 2.7 %collective-permute-done.6 = bf16[288,128]{1,0:T(8,128)(2,1)S(1)} collective-permute-done((bf16[288,128]{1,0:T(8,128)(2,1)S(1)}, bf16[288,128]{1,0:T(8,128)(2,1)S(1)}, u32[]{:S(2)}, u32[]{:S(2)}) %collective-permute-start.6) | collective-permute-done | bytes 73760 | tf_op jit(solution)/shard_map/ppermute | solution.py:539
  29.8 0.0 collective-permute-done.7
  29.9 1.3 %collective-permute-start.8 = (bf16[288,128]{1,0:T(8,128)(2,1)S(1)}, bf16[288,128]{1,0:T(8,128)(2,1)S(1)}, u32[]{:S(2)}, u32[]{:S(2)}) collective-permute-start(bf16[288,128]{1,0:T(8,128)(2,1)S(1)} %add_convert_fusion.mine_ref), channel_id=1, source_target_pairs={{0,16},{16,0},{1,17},{17,1},{2,18},{18,2},{3,19},{19,3},{4,20},{20... | collective-permute-start | bytes 221192 | tf_op jit(solution)/shard_map/ppermute | solution.py:543
  31.1 0.9 %collective-permute-done.8.other_ref = bf16[288,128]{1,0:T(8,128)(2,1)S(1)} collective-permute-done((bf16[288,128]{1,0:T(8,128)(2,1)S(1)}, bf16[288,128]{1,0:T(8,128)(2,1)S(1)}, u32[]{:S(2)}, u32[]{:S(2)}) %collective-permute-start.8) | collective-permute-done | bytes 73760 | tf_op jit(solution)/shard_map/ppermute | solution.py:543
  32.0 0.7 %unpack.1 = (f32[4,768]{1,0:T(4,128)}, f32[20,128]{1,0:T(8,128)}, f32[40,256]{1,0:T(8,128)}, f32[80,256]{1,0:T(8,128)}, f32[1,48]{1,0:T(1,128)}) custom-call(bf16[288,128]{1,0:T(8,128)(2,1)S(1)} %add_convert_fusion.mine_ref, bf16[288,128]{1,0:T(8,128)(2,1)S(1)} %collective-permute-done.8.other_ref), custom_call_target="tpu_custom_call" | custom-call | tf_op jit(solution)/shard_map/unpack/pallas_call | solution.py:551
  (2 shorter events, 0.1 us)
Async XLA Ops:
  1.4 4.9 %collective-permute-start = (bf16[32,512]{1,0:T(8,128)(2,1)S(1)}, bf16[32,512]{1,0:T(8,128)(2,1)S(1)}, u32[]{:S(2)}, u32[]{:S(2)}) collective-permute-start(bf16[32,512]{1,0:T(8,128)(2,1)S(1)} %edge.1), channel_id=1, source_target_pairs={{0,16},{1,0},{2,1},{3,2},{4,3},{5,4},{6,5},{7,6},{8,7},{9,8},{10,9... | collective-permute-start | bytes 98312 | tf_op jit(solution)/shard_map/ppermute | solution.py:418
  9.2 2.1 %collective-permute-start.1 = (bf16[4,2,288,128]{3,2,1,0:T(8,128)(2,1)S(1)}, bf16[4,2,288,128]{3,2,1,0:T(8,128)(2,1)S(1)}, u32[]{:S(2)}, u32[]{:S(2)}) collective-permute-start(bf16[4,2,288,128]{3,2,1,0:T(8,128)(2,1)S(1)} %slice_bitcast_fusion), channel_id=1, source_target_pairs={{0,16},{16,0},{1,17},{17,1},{2,18},{18,2},{3,19},{19,3},{4,20},{20... | collective-permute-start | bytes 1769480 | tf_op jit(solution)/shard_map/ppermute | solution.py:531
  11.5 6.9 %collective-permute-start.4 = (bf16[2,288,128]{2,1,0:T(8,128)(2,1)S(1)}, bf16[2,288,128]{2,1,0:T(8,128)(2,1)S(1)}, u32[]{:S(2)}, u32[]{:S(2)}) collective-permute-start(bf16[2,288,128]{2,1,0:T(8,128)(2,1)S(1)} %get-tuple-element.74), channel_id=1, source_target_pairs={{0,2},{1,3},{2,0},{3,1},{4,6},{5,7},{6,4},{7,5},{8,10},{9,11},{10,... | collective-permute-start | bytes 442376 | tf_op jit(solution)/shard_map/ppermute | solution.py:535
  13.6 7.7 %collective-permute-start.3 = (bf16[2,288,128]{2,1,0:T(8,128)(2,1)S(1)}, bf16[2,288,128]{2,1,0:T(8,128)(2,1)S(1)}, u32[]{:S(2)}, u32[]{:S(2)}) collective-permute-start(bf16[2,288,128]{2,1,0:T(8,128)(2,1)S(1)} %get-tuple-element.75), channel_id=1, source_target_pairs={{0,3},{1,2},{2,1},{3,0},{4,7},{5,6},{6,5},{7,4},{8,11},{9,10},{10,... | collective-permute-start | bytes 442376 | tf_op jit(solution)/shard_map/ppermute | solution.py:535
  16.4 7.0 %collective-permute-start.2 = (bf16[2,288,128]{2,1,0:T(8,128)(2,1)S(1)}, bf16[2,288,128]{2,1,0:T(8,128)(2,1)S(1)}, u32[]{:S(2)}, u32[]{:S(2)}) collective-permute-start(bf16[2,288,128]{2,1,0:T(8,128)(2,1)S(1)} %get-tuple-element.76), channel_id=1, source_target_pairs={{0,1},{1,0},{2,3},{3,2},{4,5},{5,4},{6,7},{7,6},{8,9},{9,8},{10,11... | collective-permute-start | bytes 442376 | tf_op jit(solution)/shard_map/ppermute | solution.py:535
  16.9 6.6 %collective-permute-start.5 = (bf16[16,512]{1,0:T(8,128)(2,1)S(1)}, bf16[16,512]{1,0:T(8,128)(2,1)S(1)}, u32[]{:S(2)}, u32[]{:S(2)}) collective-permute-start(bf16[16,512]{1,0:T(8,128)(2,1)S(1)} %get-tuple-element.57), channel_id=1, source_target_pairs={{0,1},{1,2},{2,3},{3,4},{4,5},{5,6},{6,7},{7,8},{8,9},{9,10},{10,1... | collective-permute-start | bytes 49160 | tf_op jit(solution)/shard_map/ppermute | solution.py:496
  23.5 6.4 %collective-permute-start.6 = (bf16[288,128]{1,0:T(8,128)(2,1)S(1)}, bf16[288,128]{1,0:T(8,128)(2,1)S(1)}, u32[]{:S(2)}, u32[]{:S(2)}) collective-permute-start(bf16[288,128]{1,0:T(8,128)(2,1)S(1)} %get-tuple-element.58), channel_id=1, source_target_pairs={{0,12},{1,13},{2,14},{3,15},{4,8},{5,9},{6,10},{7,11},{8,4},{9,5},... | collective-permute-start | bytes 221192 | tf_op jit(solution)/shard_map/ppermute | solution.py:539
  25.7 4.1 %collective-permute-start.7 = (bf16[288,128]{1,0:T(8,128)(2,1)S(1)}, bf16[288,128]{1,0:T(8,128)(2,1)S(1)}, u32[]{:S(2)}, u32[]{:S(2)}) collective-permute-start(bf16[288,128]{1,0:T(8,128)(2,1)S(1)} %get-tuple-element.59), channel_id=1, source_target_pairs={{0,0},{1,1},{2,2},{3,3},{4,4},{5,5},{6,6},{7,7},{8,8},{9,9},{10,10... | collective-permute-start | bytes 221192 | tf_op jit(solution)/shard_map/ppermute | solution.py:539
  29.9 2.2 %collective-permute-start.8 = (bf16[288,128]{1,0:T(8,128)(2,1)S(1)}, bf16[288,128]{1,0:T(8,128)(2,1)S(1)}, u32[]{:S(2)}, u32[]{:S(2)}) collective-permute-start(bf16[288,128]{1,0:T(8,128)(2,1)S(1)} %add_convert_fusion.mine_ref), channel_id=1, source_target_pairs={{0,16},{16,0},{1,17},{17,1},{2,18},{18,2},{3,19},{19,3},{4,20},{20... | collective-permute-start | bytes 221192 | tf_op jit(solution)/shard_map/ppermute | solution.py:543

commit v7 on v6

--- a/solution.py
+++ b/solution.py
@@ -530,11 +530,10 @@
     (payload,) = grads
     came = lax.ppermute(payload[1], "dp", swap)
     own_grad, back = features_back()
-    came, own_grad = lax.optimization_barrier((came, own_grad))
     held = [added(payload[0, j], came[j]) for j in range(4)]
     moved = [lax.ppermute(held[j], ("dp", "seq"), mixed(j, (j >> 1) | ((j & 1) << 1))) for j in (1, 3, 2)]
     held = [added(held[0][i], *(part[i] for part in moved)) for i in range(2)]
-    held, back = lax.optimization_barrier((held, back))
+    held, back, own_grad = lax.optimization_barrier((held, back, own_grad))
     held = added(
         lax.ppermute(held[1], ("dp", "seq"), mixed(12, 8)), lax.ppermute(held[0], ("dp", "seq"), mixed(0, 4))
     )

time: 32.9 us -> 32.8 us (level)
  waiting for transfers between devices: 12.2 us -> 11.7 us
  starting transfers between devices: 11.7 us -> 12.1 us
    ppermute x3, waiting for transfers between devices: 4.96 us -> 4.11 us  [shards(): lax.ppermute(held[j], ('dp', 'seq'), mixed(j, j >> 1 | (j & 1) << 1))]
    ppermute x1, waiting for transfers between devices: 1.19 us -> 1.99 us  [shards(): came = lax.ppermute(payload[1], 'dp', swap)]
    ppermute x1, waiting for transfers between devices: 2.7 us -> 2.26 us  [shards(): lax.ppermute(held[1], ('dp', 'seq'), mixed(12, 8))]
    ppermute x1, starting transfers between devices: 2.28 us -> 2.62 us  [shards(): lax.ppermute(held[1], ('dp', 'seq'), mixed(12, 8))]
where the time goes in v7:
time: 32.8 us; the launch traced here: 32.6 us
  starting transfers between devices  12.1 us (37%)
  waiting for transfers between devices  11.7 us (36%)
  Pallas kernels  7.8 us (24%)
  between operations  0.71 us (2%)
    ppermute x3, starting transfers between devices, shards(): lax.ppermute(held[j], ('dp', 'seq'), mixed(j, j >> 1 | (j & 1) << 1))  5.4 us
    ppermute x3, waiting for transfers between devices, shards(): lax.ppermute(held[j], ('dp', 'seq'), mixed(j, j >> 1 | (j & 1) << 1))  4.11 us
    pallas_call x1, Pallas kernels, shards(): pl.pallas_call(functools.partial(head_kernel, n, packed), in_specs=[VMEM]...  2.84 us
    ppermute x1, starting transfers between devices, shards(): lax.ppermute(held[1], ('dp', 'seq'), mixed(12, 8))  2.62 us
    ppermute x1, waiting for transfers between devices, shards(): edge = lax.ppermute(edge, ('dp', 'seq'), along)  2.4 us
    ppermute x1, waiting for transfers between devices, shards(): lax.ppermute(held[1], ('dp', 'seq'), mixed(12, 8))  2.26 us
    ppermute x1, waiting for transfers between devices, shards(): came = lax.ppermute(payload[1], 'dp', swap)  1.99 us
    pallas_call x1, Pallas kernels, shards(): pl.pallas_call(functools.partial(project_kernel, len(sources)), in_specs=...  1.97 us
  transfers between devices with their start and end apart: 9, of which 6 were waited for; matrix products, arithmetic and copies ran while one was open for 0% of the time, Pallas kernels for 11%

profile of v7, /device:TPU:0, one launch (start us, length us, event | category | flops | bytes accessed | tf_op | source)
XLA Modules:
  0.0 32.6 jit_solution(12884795129942751296)
XLA Ops:
  0.6 0.8 %edge.1 = bf16[32,512]{1,0:T(8,128)(2,1)S(1)} custom-call(bf16[128,512]{1,0:T(8,128)(2,1)} %bitcast.41, f32[1,128]{1,0:T(1,128)} %cot_ref.1), custom_call_target="tpu_custom_call" | custom-call | tf_op jit(solution)/shard_map/edge/pallas_call | solution.py:410
  1.4 0.5 %collective-permute-start = (bf16[32,512]{1,0:T(8,128)(2,1)S(1)}, bf16[32,512]{1,0:T(8,128)(2,1)S(1)}, u32[]{:S(2)}, u32[]{:S(2)}) collective-permute-start(bf16[32,512]{1,0:T(8,128)(2,1)S(1)} %edge.1), channel_id=1, source_target_pairs={{0,16},{1,0},{2,1},{3,2},{4,3},{5,4},{6,5},{7,6},{8,7},{9,8},{10,9... | collective-permute-start | bytes 98312 | tf_op jit(solution)/shard_map/ppermute | solution.py:418
  1.9 2.0 %project.1 = (bf16[128,512]{1,0:T(8,128)(2,1)S(1)}, bf16[512,768]{1,0:T(8,128)(2,1)S(1)}, bf16[64,768]{1,0:T(8,128)(2,1)S(1)}, f32[1,128]{1,0:T(1,128)S(1)}, bf1...) custom-call(bf16[768]{0:T(1024)(128)(2,1)} %final_ref.1, ...), custom_call_target="tpu_custom_call" | custom-call | flops 113246208 | bytes 786432 | tf_op jit(solution)/shard_map/project/pallas_call | solution.py:429
  3.9 2.4 %collective-permute-done.edge_ref = bf16[32,512]{1,0:T(8,128)(2,1)S(1)} collective-permute-done((bf16[32,512]{1,0:T(8,128)(2,1)S(1)}, bf16[32,512]{1,0:T(8,128)(2,1)S(1)}, u32[]{:S(2)}, u32[]{:S(2)}) %collective-permute-start) | collective-permute-done | bytes 32800 | tf_op jit(solution)/shard_map/ppermute | solution.py:418
  6.3 2.8 %head.1 = (f32[1,128]{1,0:T(1,128)S(1)}, f32[1,128]{1,0:T(1,128)S(1)}, bf16[160,64]{1,0:T(8,128)(2,1)S(1)}, bf16[32,768]{1,0:T(8,128)(2,1)S(1)}, bf16[2,4,2,288,128]{4,3,2,1,0:T(8,128)(2,1)S(1)}) custom-call(f32[128,64]{1,0:T(8,128)S(1)} %get-tuple-element.39.squeezed_ref, bf16[32,512]{1,0:T(8,128)(2,1)S(1)} %collective-permute-done.edge_ref, ...), custom_call_target="tpu_custom_call" | custom-call | flops 1000000000 | bytes 4000000 | tf_op jit(solution)/shard_map/head/pallas_call | solution.py:458
  9.2 0.1 collective-permute-start.1
  9.3 2.0 %collective-permute-done.1 = bf16[4,2,288,128]{3,2,1,0:T(8,128)(2,1)S(1)} collective-permute-done((bf16[4,2,288,128]{3,2,1,0:T(8,128)(2,1)S(1)}, bf16[4,2,288,128]{3,2,1,0:T(8,128)(2,1)S(1)}, u32[]{:S(2)}, u32[]{:S(2)}) %collective-permute-start.1) | collective-permute-done | bytes 589856 | tf_op jit(solution)/shard_map/ppermute | solution.py:531
  11.3 0.2 fusion.3
  11.5 2.1 %collective-permute-start.4 = (bf16[2,288,128]{2,1,0:T(8,128)(2,1)S(1)}, bf16[2,288,128]{2,1,0:T(8,128)(2,1)S(1)}, u32[]{:S(2)}, u32[]{:S(2)}) collective-permute-start(bf16[2,288,128]{2,1,0:T(8,128)(2,1)S(1)} %get-tuple-element.72), channel_id=1, source_target_pairs={{0,2},{1,3},{2,0},{3,1},{4,6},{5,7},{6,4},{7,5},{8,10},{9,11},{10,... | collective-permute-start | bytes 442376 | tf_op jit(solution)/shard_map/ppermute | solution.py:534
  13.6 2.8 %collective-permute-start.3 = (bf16[2,288,128]{2,1,0:T(8,128)(2,1)S(1)}, bf16[2,288,128]{2,1,0:T(8,128)(2,1)S(1)}, u32[]{:S(2)}, u32[]{:S(2)}) collective-permute-start(bf16[2,288,128]{2,1,0:T(8,128)(2,1)S(1)} %get-tuple-element.73), channel_id=1, source_target_pairs={{0,3},{1,2},{2,1},{3,0},{4,7},{5,6},{6,5},{7,4},{8,11},{9,10},{10,... | collective-permute-start | bytes 442376 | tf_op jit(solution)/shard_map/ppermute | solution.py:534
  16.4 0.5 %collective-permute-start.2 = (bf16[2,288,128]{2,1,0:T(8,128)(2,1)S(1)}, bf16[2,288,128]{2,1,0:T(8,128)(2,1)S(1)}, u32[]{:S(2)}, u32[]{:S(2)}) collective-permute-start(bf16[2,288,128]{2,1,0:T(8,128)(2,1)S(1)} %get-tuple-element.74), channel_id=1, source_target_pairs={{0,1},{1,0},{2,3},{3,2},{4,5},{5,4},{6,7},{7,6},{8,9},{9,8},{10,11... | collective-permute-start | bytes 442376 | tf_op jit(solution)/shard_map/ppermute | solution.py:534
  16.9 0.8 %feature.1 = (f32[128,512]{1,0:T(8,128)S(1)}, bf16[16,512]{1,0:T(8,128)(2,1)S(1)}) custom-call(bf16[128,512]{1,0:T(8,128)(2,1)S(1)} %get-tuple-element.49.rows_ref, bf16[32,512]{1,0:T(8,128)(2,1)S(1)} %collective-permute-done.edge_ref, bf16[128,768]{1,0:T(8,128)(2,1)S(1)} %get-tuple-element.50.projected_ref, ...), custom_call_target="tpu_custom_call" | custom-call | flops 113246208 | bytes 786432 | tf_op jit(solution)/shard_map/feature/pallas_call | solution.py:487
  17.7 1.6 %collective-permute-start.5 = (bf16[16,512]{1,0:T(8,128)(2,1)S(1)}, bf16[16,512]{1,0:T(8,128)(2,1)S(1)}, u32[]{:S(2)}, u32[]{:S(2)}) collective-permute-start(bf16[16,512]{1,0:T(8,128)(2,1)S(1)} %get-tuple-element.54), channel_id=1, source_target_pairs={{0,1},{1,2},{2,3},{3,4},{4,5},{5,6},{6,7},{7,8},{8,9},{9,10},{10,1... | collective-permute-start | bytes 49160 | tf_op jit(solution)/shard_map/ppermute | solution.py:496
  19.3 0.0 collective-permute-done.4
  19.3 2.0 %collective-permute-done.3 = bf16[2,288,128]{2,1,0:T(8,128)(2,1)S(1)} collective-permute-done((bf16[2,288,128]{2,1,0:T(8,128)(2,1)S(1)}, bf16[2,288,128]{2,1,0:T(8,128)(2,1)S(1)}, u32[]{:S(2)}, u32[]{:S(2)}) %collective-permute-start.3) | collective-permute-done | bytes 147488 | tf_op jit(solution)/shard_map/ppermute | solution.py:534
  21.3 2.1 %collective-permute-done.2 = bf16[2,288,128]{2,1,0:T(8,128)(2,1)S(1)} collective-permute-done((bf16[2,288,128]{2,1,0:T(8,128)(2,1)S(1)}, bf16[2,288,128]{2,1,0:T(8,128)(2,1)S(1)}, u32[]{:S(2)}, u32[]{:S(2)}) %collective-permute-start.2) | collective-permute-done | bytes 147488 | tf_op jit(solution)/shard_map/ppermute | solution.py:534
  23.4 0.1 fusion.5
  23.5 0.0 collective-permute-done.5.back_ref
  23.5 2.6 %collective-permute-start.6 = (bf16[288,128]{1,0:T(8,128)(2,1)S(1)}, bf16[288,128]{1,0:T(8,128)(2,1)S(1)}, u32[]{:S(2)}, u32[]{:S(2)}) collective-permute-start(bf16[288,128]{1,0:T(8,128)(2,1)S(1)} %get-tuple-element.56), channel_id=1, source_target_pairs={{0,12},{1,13},{2,14},{3,15},{4,8},{5,9},{6,10},{7,11},{8,4},{9,5},... | collective-permute-start | bytes 221192 | tf_op jit(solution)/shard_map/ppermute | solution.py:538
  26.1 0.7 %collective-permute-start.7 = (bf16[288,128]{1,0:T(8,128)(2,1)S(1)}, bf16[288,128]{1,0:T(8,128)(2,1)S(1)}, u32[]{:S(2)}, u32[]{:S(2)}) collective-permute-start(bf16[288,128]{1,0:T(8,128)(2,1)S(1)} %get-tuple-element.57), channel_id=1, source_target_pairs={{0,0},{1,1},{2,2},{3,3},{4,4},{5,5},{6,6},{7,7},{8,8},{9,9},{10,10... | collective-permute-start | bytes 221192 | tf_op jit(solution)/shard_map/ppermute | solution.py:538
  26.7 0.7 %assemble.1 = (f32[128,512]{1,0:T(8,128)}, f32[1,128]{1,0:T(1,128)}) custom-call(f32[128,512]{1,0:T(8,128)S(1)} %get-tuple-element.58.own_ref, f32[1,128]{1,0:T(1,128)S(1)} %get-tuple-element.59.scores_ref, bf16[16,512]{1,0:T(8,128)(2,1)S(1)} %collective-permute-done.5.back_ref), custom_call_target="tpu_custom_call" | custom-call | flops 65536 | bytes 524288 | tf_op jit(solution)/shard_map/assemble/pallas_call | solution.py:500
  27.5 2.3 %collective-permute-done.6 = bf16[288,128]{1,0:T(8,128)(2,1)S(1)} collective-permute-done((bf16[288,128]{1,0:T(8,128)(2,1)S(1)}, bf16[288,128]{1,0:T(8,128)(2,1)S(1)}, u32[]{:S(2)}, u32[]{:S(2)}) %collective-permute-start.6) | collective-permute-done | bytes 73760 | tf_op jit(solution)/shard_map/ppermute | solution.py:538
  29.7 0.0 collective-permute-done.7
  29.8 1.2 %collective-permute-start.8 = (bf16[288,128]{1,0:T(8,128)(2,1)S(1)}, bf16[288,128]{1,0:T(8,128)(2,1)S(1)}, u32[]{:S(2)}, u32[]{:S(2)}) collective-permute-start(bf16[288,128]{1,0:T(8,128)(2,1)S(1)} %add_convert_fusion.mine_ref), channel_id=1, source_target_pairs={{0,16},{16,0},{1,17},{17,1},{2,18},{18,2},{3,19},{19,3},{4,20},{20... | collective-permute-start | bytes 221192 | tf_op jit(solution)/shard_map/ppermute | solution.py:542
  31.0 0.9 %collective-permute-done.8.other_ref = bf16[288,128]{1,0:T(8,128)(2,1)S(1)} collective-permute-done((bf16[288,128]{1,0:T(8,128)(2,1)S(1)}, bf16[288,128]{1,0:T(8,128)(2,1)S(1)}, u32[]{:S(2)}, u32[]{:S(2)}) %collective-permute-start.8) | collective-permute-done | bytes 73760 | tf_op jit(solution)/shard_map/ppermute | solution.py:542
  31.9 0.7 %unpack.1 = (f32[4,768]{1,0:T(4,128)}, f32[20,128]{1,0:T(8,128)}, f32[40,256]{1,0:T(8,128)}, f32[80,256]{1,0:T(8,128)}, f32[1,48]{1,0:T(1,128)}) custom-call(bf16[288,128]{1,0:T(8,128)(2,1)S(1)} %add_convert_fusion.mine_ref, bf16[288,128]{1,0:T(8,128)(2,1)S(1)} %collective-permute-done.8.other_ref), custom_call_target="tpu_custom_call" | custom-call | tf_op jit(solution)/shard_map/unpack/pallas_call | solution.py:550
  (2 shorter events, 0.1 us)
Async XLA Ops:
  1.4 4.9 %collective-permute-start = (bf16[32,512]{1,0:T(8,128)(2,1)S(1)}, bf16[32,512]{1,0:T(8,128)(2,1)S(1)}, u32[]{:S(2)}, u32[]{:S(2)}) collective-permute-start(bf16[32,512]{1,0:T(8,128)(2,1)S(1)} %edge.1), channel_id=1, source_target_pairs={{0,16},{1,0},{2,1},{3,2},{4,3},{5,4},{6,5},{7,6},{8,7},{9,8},{10,9... | collective-permute-start | bytes 98312 | tf_op jit(solution)/shard_map/ppermute | solution.py:418
  9.2 2.1 %collective-permute-start.1 = (bf16[4,2,288,128]{3,2,1,0:T(8,128)(2,1)S(1)}, bf16[4,2,288,128]{3,2,1,0:T(8,128)(2,1)S(1)}, u32[]{:S(2)}, u32[]{:S(2)}) collective-permute-start(bf16[4,2,288,128]{3,2,1,0:T(8,128)(2,1)S(1)} %slice_bitcast_fusion), channel_id=1, source_target_pairs={{0,16},{16,0},{1,17},{17,1},{2,18},{18,2},{3,19},{19,3},{4,20},{20... | collective-permute-start | bytes 1769480 | tf_op jit(solution)/shard_map/ppermute | solution.py:531
  11.5 7.8 %collective-permute-start.4 = (bf16[2,288,128]{2,1,0:T(8,128)(2,1)S(1)}, bf16[2,288,128]{2,1,0:T(8,128)(2,1)S(1)}, u32[]{:S(2)}, u32[]{:S(2)}) collective-permute-start(bf16[2,288,128]{2,1,0:T(8,128)(2,1)S(1)} %get-tuple-element.72), channel_id=1, source_target_pairs={{0,2},{1,3},{2,0},{3,1},{4,6},{5,7},{6,4},{7,5},{8,10},{9,11},{10,... | collective-permute-start | bytes 442376 | tf_op jit(solution)/shard_map/ppermute | solution.py:534
  13.6 7.7 %collective-permute-start.3 = (bf16[2,288,128]{2,1,0:T(8,128)(2,1)S(1)}, bf16[2,288,128]{2,1,0:T(8,128)(2,1)S(1)}, u32[]{:S(2)}, u32[]{:S(2)}) collective-permute-start(bf16[2,288,128]{2,1,0:T(8,128)(2,1)S(1)} %get-tuple-element.73), channel_id=1, source_target_pairs={{0,3},{1,2},{2,1},{3,0},{4,7},{5,6},{6,5},{7,4},{8,11},{9,10},{10,... | collective-permute-start | bytes 442376 | tf_op jit(solution)/shard_map/ppermute | solution.py:534
  16.4 7.0 %collective-permute-start.2 = (bf16[2,288,128]{2,1,0:T(8,128)(2,1)S(1)}, bf16[2,288,128]{2,1,0:T(8,128)(2,1)S(1)}, u32[]{:S(2)}, u32[]{:S(2)}) collective-permute-start(bf16[2,288,128]{2,1,0:T(8,128)(2,1)S(1)} %get-tuple-element.74), channel_id=1, source_target_pairs={{0,1},{1,0},{2,3},{3,2},{4,5},{5,4},{6,7},{7,6},{8,9},{9,8},{10,11... | collective-permute-start | bytes 442376 | tf_op jit(solution)/shard_map/ppermute | solution.py:534
  17.7 5.8 %collective-permute-start.5 = (bf16[16,512]{1,0:T(8,128)(2,1)S(1)}, bf16[16,512]{1,0:T(8,128)(2,1)S(1)}, u32[]{:S(2)}, u32[]{:S(2)}) collective-permute-start(bf16[16,512]{1,0:T(8,128)(2,1)S(1)} %get-tuple-element.54), channel_id=1, source_target_pairs={{0,1},{1,2},{2,3},{3,4},{4,5},{5,6},{6,7},{7,8},{8,9},{9,10},{10,1... | collective-permute-start | bytes 49160 | tf_op jit(solution)/shard_map/ppermute | solution.py:496
  23.5 6.3 %collective-permute-start.6 = (bf16[288,128]{1,0:T(8,128)(2,1)S(1)}, bf16[288,128]{1,0:T(8,128)(2,1)S(1)}, u32[]{:S(2)}, u32[]{:S(2)}) collective-permute-start(bf16[288,128]{1,0:T(8,128)(2,1)S(1)} %get-tuple-element.56), channel_id=1, source_target_pairs={{0,12},{1,13},{2,14},{3,15},{4,8},{5,9},{6,10},{7,11},{8,4},{9,5},... | collective-permute-start | bytes 221192 | tf_op jit(solution)/shard_map/ppermute | solution.py:538
  26.1 3.7 %collective-permute-start.7 = (bf16[288,128]{1,0:T(8,128)(2,1)S(1)}, bf16[288,128]{1,0:T(8,128)(2,1)S(1)}, u32[]{:S(2)}, u32[]{:S(2)}) collective-permute-start(bf16[288,128]{1,0:T(8,128)(2,1)S(1)} %get-tuple-element.57), channel_id=1, source_target_pairs={{0,0},{1,1},{2,2},{3,3},{4,4},{5,5},{6,6},{7,7},{8,8},{9,9},{10,10... | collective-permute-start | bytes 221192 | tf_op jit(solution)/shard_map/ppermute | solution.py:538
  29.8 2.2 %collective-permute-start.8 = (bf16[288,128]{1,0:T(8,128)(2,1)S(1)}, bf16[288,128]{1,0:T(8,128)(2,1)S(1)}, u32[]{:S(2)}, u32[]{:S(2)}) collective-permute-start(bf16[288,128]{1,0:T(8,128)(2,1)S(1)} %add_convert_fusion.mine_ref), channel_id=1, source_target_pairs={{0,16},{16,0},{1,17},{17,1},{2,18},{18,2},{3,19},{19,3},{4,20},{20... | collective-permute-start | bytes 221192 | tf_op jit(solution)/shard_map/ppermute | solution.py:542

commit v8 on v7

--- a/solution.py
+++ b/solution.py
@@ -53,14 +53,13 @@
     return lax.dot_general(a, b, dims, preferred_element_type=F32)
 
 
-def forward_rows(rows, projection, squeeze):
+def forward_rows(rows, projection, squeeze, sums):
     normed, _ = normalize(rows.astype(F32))
     projected = dot(normed.astype(BF16), projection).astype(BF16)
     wide = projected.astype(F32)
     average = jnp.mean(wide, axis=-1, keepdims=True)
     centred = wide - average
     inverse = lax.rsqrt(jnp.mean(centred * centred, axis=-1, keepdims=True) + EPSILON)
-    sums = dot(jnp.ones((8, squeeze.shape[1]), BF16), squeeze, NT)[0:1]
     squeezed = (dot(projected, squeeze, NT) - average * sums) * inverse
     return projected, (centred * inverse).astype(BF16), squeezed
 
@@ -99,14 +98,16 @@
     sources, held = refs[:count], refs[count : 2 * count]
     final_out, final_held = refs[-3], refs[-2]
     final_copy = pltpu.make_async_copy(final_ref, final_held, refs[-1].at[count])
-    projected_ref, hidden_ref, squeezed_ref, _, _, sems = refs[2 * count :]
+    projected_ref, hidden_ref, squeezed_ref, sums_ref, _, _, sems = refs[2 * count :]
     copies = [pltpu.make_async_copy(a, b, sems.at[i]) for i, (a, b) in enumerate(zip(sources, held))]
     for copy in copies:
         copy.start()
     final_copy.start()
     for copy in copies[:3]:
         copy.wait()
-    projected, hidden, squeezed = forward_rows(held[0][...], held[1][...], held[2][...])
+    sums = dot(jnp.ones((8, held[2].shape[1]), BF16), held[2][...], NT)
+    sums_ref[...] = sums
+    projected, hidden, squeezed = forward_rows(held[0][...], held[1][...], held[2][...], sums[0:1])
     projected_ref[...] = projected
     hidden_ref[...] = hidden
     squeezed_ref[...] = squeezed
@@ -150,6 +151,7 @@
     n,
     packed,
     squeezed_ref,
+    sums_ref,
     edge_ref,
     cot_ref,
     hidden_ref,
@@ -186,7 +188,7 @@
         )
 
     edge_projected, edge_hidden, edge_squeezed = forward_rows(
-        edge_ref[...], projection_ref[...], squeeze_ref[...]
+        edge_ref[...], projection_ref[...], squeeze_ref[...], sums_ref[0:1, :]
     )
     edge_projected_ref[...] = edge_projected
     squeezed = jnp.concatenate([squeezed_ref[...], edge_squeezed], axis=0)
@@ -277,9 +279,8 @@
         rows = inputs[layer].T
         ref = weights[layer]
         width = ref.shape[0] // HK
-        upstream = jnp.zeros((total, width), F32)
-        for k, piece in enumerate(pieces):
-            upstream = upstream + dot(piece, ref[k * width : (k + 1) * width, :], NT)
+        whole = jnp.concatenate([ref[k * width : (k + 1) * width, :] for k in range(HK)], axis=1)
+        upstream = dot(jnp.concatenate(pieces, axis=1), whole, NT)
         for k, piece in enumerate(pieces):
             keep(layer, k, dot(rows, piece))
     delta = mask(upstream * slopes[0], inside)
@@ -355,7 +356,7 @@
     at = here()[0] * count
     at = at - jnp.minimum(lax.div(at, LANES), PK * C2 // LANES - 2) * LANES
     pair = jnp.concatenate([both[PACK[4] : PACK[4] + 1, :], both[PACK[4] + 1 : PACK[4] + 2, :]], axis=1)
-    pair = pltpu.roll(jnp.broadcast_to(pair, (8, 2 * LANES)), 2 * LANES - at, 1)
+    pair = pltpu.roll(jnp.broadcast_to(pair, (8, 2 * LANES)), lax.rem(2 * LANES - at, 2 * LANES), 1)
     final_ref[...] = pair[0:1, :count]
 
 
@@ -426,15 +427,16 @@
         second_weight,
         third_weight,
     )
-    rows, projection, squeeze, cot, first, second, third, projected, hidden, squeezed, final = pl.pallas_call(
+    rows, projection, squeeze, cot, first, second, third, projected, hidden, squeezed, sums, final = pl.pallas_call(
         functools.partial(project_kernel, len(sources)),
         in_specs=[HBM] * (1 + len(sources)),
-        out_specs=[VMEM] * (len(sources) + 4),
+        out_specs=[VMEM] * (len(sources) + 5),
         out_shape=[
             *[vmem(a.shape, a.dtype) for a in sources],
             vmem((frames, width), BF16),
             vmem((frames, width), BF16),
             vmem((frames, C0), F32),
+            vmem((8, C0), F32),
             vmem((1, PK * C2), BF16),
         ],
         scratch_shapes=[pltpu.VMEM((PK * C2,), BF16), pltpu.SemaphoreType.DMA((len(sources) + 1,))],
@@ -457,7 +459,7 @@
         scratch = []
     own_scores, after, delta, edge_projected, *grads = pl.pallas_call(
         functools.partial(head_kernel, n, packed),
-        in_specs=[VMEM] * 10,
+        in_specs=[VMEM] * 11,
         out_specs=[VMEM] * (4 + len(grad_shapes)),
         out_shape=[
             sds((1, frames), F32),
@@ -472,6 +474,7 @@
         name="head",
     )(
         squeezed,
+        sums,
         edge,
         cot,
         hidden,

time: 32.8 us -> 32.8 us (level)
  no operation moved by 1% of the time
where the time goes in v8:
time: 32.8 us; the launch traced here: 32.5 us
  starting transfers between devices  12 us (37%)
  waiting for transfers between devices  11.7 us (36%)
  Pallas kernels  7.82 us (24%)
  between operations  0.71 us (2%)
    ppermute x3, starting transfers between devices, shards(): lax.ppermute(held[j], ('dp', 'seq'), mixed(j, j >> 1 | (j & 1) << 1))  5.41 us
    ppermute x3, waiting for transfers between devices, shards(): lax.ppermute(held[j], ('dp', 'seq'), mixed(j, j >> 1 | (j & 1) << 1))  4.1 us
    pallas_call x1, Pallas kernels, shards(): pl.pallas_call(functools.partial(head_kernel, n, packed), in_specs=[VMEM]...  2.85 us
    ppermute x1, starting transfers between devices, shards(): lax.ppermute(held[1], ('dp', 'seq'), mixed(12, 8))  2.6 us
    ppermute x1, waiting for transfers between devices, shards(): edge = lax.ppermute(edge, ('dp', 'seq'), along)  2.4 us
    ppermute x1, waiting for transfers between devices, shards(): lax.ppermute(held[1], ('dp', 'seq'), mixed(12, 8))  2.28 us
    ppermute x1, waiting for transfers between devices, shards(): came = lax.ppermute(payload[1], 'dp', swap)  1.99 us
    pallas_call x1, Pallas kernels, shards(): pl.pallas_call(functools.partial(project_kernel, len(sources)), in_specs=...  1.97 us
  transfers between devices with their start and end apart: 9, of which 6 were waited for; matrix products, arithmetic and copies ran while one was open for 0% of the time, Pallas kernels for 11%

profile of v8, /device:TPU:0, one launch (start us, length us, event | category | flops | bytes accessed | tf_op | source)
XLA Modules:
  0.0 32.5 jit_solution(6380480144536184283)
XLA Ops:
  0.6 0.8 %edge.1 = bf16[32,512]{1,0:T(8,128)(2,1)S(1)} custom-call(bf16[128,512]{1,0:T(8,128)(2,1)} %bitcast.41, f32[1,128]{1,0:T(1,128)} %cot_ref.1), custom_call_target="tpu_custom_call" | custom-call | tf_op jit(solution)/shard_map/edge/pallas_call | solution.py:411
  1.4 0.5 %collective-permute-start = (bf16[32,512]{1,0:T(8,128)(2,1)S(1)}, bf16[32,512]{1,0:T(8,128)(2,1)S(1)}, u32[]{:S(2)}, u32[]{:S(2)}) collective-permute-start(bf16[32,512]{1,0:T(8,128)(2,1)S(1)} %edge.1), channel_id=1, source_target_pairs={{0,16},{1,0},{2,1},{3,2},{4,3},{5,4},{6,5},{7,6},{8,7},{9,8},{10,9... | collective-permute-start | bytes 98312 | tf_op jit(solution)/shard_map/ppermute | solution.py:419
  1.9 2.0 %project.1 = (bf16[128,512]{1,0:T(8,128)(2,1)S(1)}, bf16[512,768]{1,0:T(8,128)(2,1)S(1)}, bf16[64,768]{1,0:T(8,128)(2,1)S(1)}, f32[1,128]{1,0:T(1,128)S(1)}, bf1...) custom-call(bf16[768]{0:T(1024)(128)(2,1)} %final_ref.1, ...), custom_call_target="tpu_custom_call" | custom-call | flops 113246208 | bytes 786432 | tf_op jit(solution)/shard_map/project/pallas_call | solution.py:430
  3.9 2.4 %collective-permute-done.edge_ref = bf16[32,512]{1,0:T(8,128)(2,1)S(1)} collective-permute-done((bf16[32,512]{1,0:T(8,128)(2,1)S(1)}, bf16[32,512]{1,0:T(8,128)(2,1)S(1)}, u32[]{:S(2)}, u32[]{:S(2)}) %collective-permute-start) | collective-permute-done | bytes 32800 | tf_op jit(solution)/shard_map/ppermute | solution.py:419
  6.3 2.8 %head.1 = (f32[1,128]{1,0:T(1,128)S(1)}, f32[1,128]{1,0:T(1,128)S(1)}, bf16[160,64]{1,0:T(8,128)(2,1)S(1)}, bf16[32,768]{1,0:T(8,128)(2,1)S(1)}, bf16[2,4,2,288,128]{4,3,2,1,0:T(8,128)(2,1)S(1)}) custom-call(f32[128,64]{1,0:T(8,128)S(1)} %get-tuple-element.40.squeezed_ref, f32[8,64]{1,0:T(8,128)S(1)} %get-tuple-element.41.sums_ref, ...), custom_call_target="tpu_custom_call" | custom-call | flops 1000000000 | bytes 4000000 | tf_op jit(solution)/shard_map/head/pallas_call | solution.py:460
  9.2 0.1 collective-permute-start.1
  9.3 2.0 %collective-permute-done.1 = bf16[4,2,288,128]{3,2,1,0:T(8,128)(2,1)S(1)} collective-permute-done((bf16[4,2,288,128]{3,2,1,0:T(8,128)(2,1)S(1)}, bf16[4,2,288,128]{3,2,1,0:T(8,128)(2,1)S(1)}, u32[]{:S(2)}, u32[]{:S(2)}) %collective-permute-start.1) | collective-permute-done | bytes 589856 | tf_op jit(solution)/shard_map/ppermute | solution.py:534
  11.3 0.2 fusion.3
  11.5 2.1 %collective-permute-start.4 = (bf16[2,288,128]{2,1,0:T(8,128)(2,1)S(1)}, bf16[2,288,128]{2,1,0:T(8,128)(2,1)S(1)}, u32[]{:S(2)}, u32[]{:S(2)}) collective-permute-start(bf16[2,288,128]{2,1,0:T(8,128)(2,1)S(1)} %get-tuple-element.74), channel_id=1, source_target_pairs={{0,2},{1,3},{2,0},{3,1},{4,6},{5,7},{6,4},{7,5},{8,10},{9,11},{10,... | collective-permute-start | bytes 442376 | tf_op jit(solution)/shard_map/ppermute | solution.py:537
  13.6 2.8 %collective-permute-start.3 = (bf16[2,288,128]{2,1,0:T(8,128)(2,1)S(1)}, bf16[2,288,128]{2,1,0:T(8,128)(2,1)S(1)}, u32[]{:S(2)}, u32[]{:S(2)}) collective-permute-start(bf16[2,288,128]{2,1,0:T(8,128)(2,1)S(1)} %get-tuple-element.75), channel_id=1, source_target_pairs={{0,3},{1,2},{2,1},{3,0},{4,7},{5,6},{6,5},{7,4},{8,11},{9,10},{10,... | collective-permute-start | bytes 442376 | tf_op jit(solution)/shard_map/ppermute | solution.py:537
  16.4 0.5 %collective-permute-start.2 = (bf16[2,288,128]{2,1,0:T(8,128)(2,1)S(1)}, bf16[2,288,128]{2,1,0:T(8,128)(2,1)S(1)}, u32[]{:S(2)}, u32[]{:S(2)}) collective-permute-start(bf16[2,288,128]{2,1,0:T(8,128)(2,1)S(1)} %get-tuple-element.76), channel_id=1, source_target_pairs={{0,1},{1,0},{2,3},{3,2},{4,5},{5,4},{6,7},{7,6},{8,9},{9,8},{10,11... | collective-permute-start | bytes 442376 | tf_op jit(solution)/shard_map/ppermute | solution.py:537
  16.9 0.8 %feature.1 = (f32[128,512]{1,0:T(8,128)S(1)}, bf16[16,512]{1,0:T(8,128)(2,1)S(1)}) custom-call(bf16[128,512]{1,0:T(8,128)(2,1)S(1)} %get-tuple-element.51.rows_ref, bf16[32,512]{1,0:T(8,128)(2,1)S(1)} %collective-permute-done.edge_ref, bf16[128,768]{1,0:T(8,128)(2,1)S(1)} %get-tuple-element.52.projected_ref, ...), custom_call_target="tpu_custom_call" | custom-call | flops 113246208 | bytes 786432 | tf_op jit(solution)/shard_map/feature/pallas_call | solution.py:490
  17.7 1.6 %collective-permute-start.5 = (bf16[16,512]{1,0:T(8,128)(2,1)S(1)}, bf16[16,512]{1,0:T(8,128)(2,1)S(1)}, u32[]{:S(2)}, u32[]{:S(2)}) collective-permute-start(bf16[16,512]{1,0:T(8,128)(2,1)S(1)} %get-tuple-element.56), channel_id=1, source_target_pairs={{0,1},{1,2},{2,3},{3,4},{4,5},{5,6},{6,7},{7,8},{8,9},{9,10},{10,1... | collective-permute-start | bytes 49160 | tf_op jit(solution)/shard_map/ppermute | solution.py:499
  19.3 0.0 collective-permute-done.4
  19.3 2.0 %collective-permute-done.3 = bf16[2,288,128]{2,1,0:T(8,128)(2,1)S(1)} collective-permute-done((bf16[2,288,128]{2,1,0:T(8,128)(2,1)S(1)}, bf16[2,288,128]{2,1,0:T(8,128)(2,1)S(1)}, u32[]{:S(2)}, u32[]{:S(2)}) %collective-permute-start.3) | collective-permute-done | bytes 147488 | tf_op jit(solution)/shard_map/ppermute | solution.py:537
  21.3 2.1 %collective-permute-done.2 = bf16[2,288,128]{2,1,0:T(8,128)(2,1)S(1)} collective-permute-done((bf16[2,288,128]{2,1,0:T(8,128)(2,1)S(1)}, bf16[2,288,128]{2,1,0:T(8,128)(2,1)S(1)}, u32[]{:S(2)}, u32[]{:S(2)}) %collective-permute-start.2) | collective-permute-done | bytes 147488 | tf_op jit(solution)/shard_map/ppermute | solution.py:537
  23.4 0.1 fusion.5
  23.5 0.0 collective-permute-done.5.back_ref
  23.5 2.6 %collective-permute-start.6 = (bf16[288,128]{1,0:T(8,128)(2,1)S(1)}, bf16[288,128]{1,0:T(8,128)(2,1)S(1)}, u32[]{:S(2)}, u32[]{:S(2)}) collective-permute-start(bf16[288,128]{1,0:T(8,128)(2,1)S(1)} %get-tuple-element.58), channel_id=1, source_target_pairs={{0,12},{1,13},{2,14},{3,15},{4,8},{5,9},{6,10},{7,11},{8,4},{9,5},... | collective-permute-start | bytes 221192 | tf_op jit(solution)/shard_map/ppermute | solution.py:541
  26.1 0.7 %collective-permute-start.7 = (bf16[288,128]{1,0:T(8,128)(2,1)S(1)}, bf16[288,128]{1,0:T(8,128)(2,1)S(1)}, u32[]{:S(2)}, u32[]{:S(2)}) collective-permute-start(bf16[288,128]{1,0:T(8,128)(2,1)S(1)} %get-tuple-element.59), channel_id=1, source_target_pairs={{0,0},{1,1},{2,2},{3,3},{4,4},{5,5},{6,6},{7,7},{8,8},{9,9},{10,10... | collective-permute-start | bytes 221192 | tf_op jit(solution)/shard_map/ppermute | solution.py:541
  26.7 0.7 %assemble.1 = (f32[128,512]{1,0:T(8,128)}, f32[1,128]{1,0:T(1,128)}) custom-call(f32[128,512]{1,0:T(8,128)S(1)} %get-tuple-element.60.own_ref, f32[1,128]{1,0:T(1,128)S(1)} %get-tuple-element.61.scores_ref, bf16[16,512]{1,0:T(8,128)(2,1)S(1)} %collective-permute-done.5.back_ref), custom_call_target="tpu_custom_call" | custom-call | flops 65536 | bytes 524288 | tf_op jit(solution)/shard_map/assemble/pallas_call | solution.py:503
  27.5 2.3 %collective-permute-done.6 = bf16[288,128]{1,0:T(8,128)(2,1)S(1)} collective-permute-done((bf16[288,128]{1,0:T(8,128)(2,1)S(1)}, bf16[288,128]{1,0:T(8,128)(2,1)S(1)}, u32[]{:S(2)}, u32[]{:S(2)}) %collective-permute-start.6) | collective-permute-done | bytes 73760 | tf_op jit(solution)/shard_map/ppermute | solution.py:541
  29.7 0.0 collective-permute-done.7
  29.8 1.2 %collective-permute-start.8 = (bf16[288,128]{1,0:T(8,128)(2,1)S(1)}, bf16[288,128]{1,0:T(8,128)(2,1)S(1)}, u32[]{:S(2)}, u32[]{:S(2)}) collective-permute-start(bf16[288,128]{1,0:T(8,128)(2,1)S(1)} %add_convert_fusion.mine_ref), channel_id=1, source_target_pairs={{0,16},{16,0},{1,17},{17,1},{2,18},{18,2},{3,19},{19,3},{4,20},{20... | collective-permute-start | bytes 221192 | tf_op jit(solution)/shard_map/ppermute | solution.py:545
  31.0 0.9 %collective-permute-done.8.other_ref = bf16[288,128]{1,0:T(8,128)(2,1)S(1)} collective-permute-done((bf16[288,128]{1,0:T(8,128)(2,1)S(1)}, bf16[288,128]{1,0:T(8,128)(2,1)S(1)}, u32[]{:S(2)}, u32[]{:S(2)}) %collective-permute-start.8) | collective-permute-done | bytes 73760 | tf_op jit(solution)/shard_map/ppermute | solution.py:545
  31.9 0.7 %unpack.1 = (f32[4,768]{1,0:T(4,128)}, f32[20,128]{1,0:T(8,128)}, f32[40,256]{1,0:T(8,128)}, f32[80,256]{1,0:T(8,128)}, f32[1,48]{1,0:T(1,128)}) custom-call(bf16[288,128]{1,0:T(8,128)(2,1)S(1)} %add_convert_fusion.mine_ref, bf16[288,128]{1,0:T(8,128)(2,1)S(1)} %collective-permute-done.8.other_ref), custom_call_target="tpu_custom_call" | custom-call | tf_op jit(solution)/shard_map/unpack/pallas_call | solution.py:553
  (2 shorter events, 0.1 us)
Async XLA Ops:
  1.4 4.9 %collective-permute-start = (bf16[32,512]{1,0:T(8,128)(2,1)S(1)}, bf16[32,512]{1,0:T(8,128)(2,1)S(1)}, u32[]{:S(2)}, u32[]{:S(2)}) collective-permute-start(bf16[32,512]{1,0:T(8,128)(2,1)S(1)} %edge.1), channel_id=1, source_target_pairs={{0,16},{1,0},{2,1},{3,2},{4,3},{5,4},{6,5},{7,6},{8,7},{9,8},{10,9... | collective-permute-start | bytes 98312 | tf_op jit(solution)/shard_map/ppermute | solution.py:419
  9.2 2.1 %collective-permute-start.1 = (bf16[4,2,288,128]{3,2,1,0:T(8,128)(2,1)S(1)}, bf16[4,2,288,128]{3,2,1,0:T(8,128)(2,1)S(1)}, u32[]{:S(2)}, u32[]{:S(2)}) collective-permute-start(bf16[4,2,288,128]{3,2,1,0:T(8,128)(2,1)S(1)} %slice_bitcast_fusion), channel_id=1, source_target_pairs={{0,16},{16,0},{1,17},{17,1},{2,18},{18,2},{3,19},{19,3},{4,20},{20... | collective-permute-start | bytes 1769480 | tf_op jit(solution)/shard_map/ppermute | solution.py:534
  11.5 7.8 %collective-permute-start.4 = (bf16[2,288,128]{2,1,0:T(8,128)(2,1)S(1)}, bf16[2,288,128]{2,1,0:T(8,128)(2,1)S(1)}, u32[]{:S(2)}, u32[]{:S(2)}) collective-permute-start(bf16[2,288,128]{2,1,0:T(8,128)(2,1)S(1)} %get-tuple-element.74), channel_id=1, source_target_pairs={{0,2},{1,3},{2,0},{3,1},{4,6},{5,7},{6,4},{7,5},{8,10},{9,11},{10,... | collective-permute-start | bytes 442376 | tf_op jit(solution)/shard_map/ppermute | solution.py:537
  13.6 7.7 %collective-permute-start.3 = (bf16[2,288,128]{2,1,0:T(8,128)(2,1)S(1)}, bf16[2,288,128]{2,1,0:T(8,128)(2,1)S(1)}, u32[]{:S(2)}, u32[]{:S(2)}) collective-permute-start(bf16[2,288,128]{2,1,0:T(8,128)(2,1)S(1)} %get-tuple-element.75), channel_id=1, source_target_pairs={{0,3},{1,2},{2,1},{3,0},{4,7},{5,6},{6,5},{7,4},{8,11},{9,10},{10,... | collective-permute-start | bytes 442376 | tf_op jit(solution)/shard_map/ppermute | solution.py:537
  16.4 7.0 %collective-permute-start.2 = (bf16[2,288,128]{2,1,0:T(8,128)(2,1)S(1)}, bf16[2,288,128]{2,1,0:T(8,128)(2,1)S(1)}, u32[]{:S(2)}, u32[]{:S(2)}) collective-permute-start(bf16[2,288,128]{2,1,0:T(8,128)(2,1)S(1)} %get-tuple-element.76), channel_id=1, source_target_pairs={{0,1},{1,0},{2,3},{3,2},{4,5},{5,4},{6,7},{7,6},{8,9},{9,8},{10,11... | collective-permute-start | bytes 442376 | tf_op jit(solution)/shard_map/ppermute | solution.py:537
  17.7 5.8 %collective-permute-start.5 = (bf16[16,512]{1,0:T(8,128)(2,1)S(1)}, bf16[16,512]{1,0:T(8,128)(2,1)S(1)}, u32[]{:S(2)}, u32[]{:S(2)}) collective-permute-start(bf16[16,512]{1,0:T(8,128)(2,1)S(1)} %get-tuple-element.56), channel_id=1, source_target_pairs={{0,1},{1,2},{2,3},{3,4},{4,5},{5,6},{6,7},{7,8},{8,9},{9,10},{10,1... | collective-permute-start | bytes 49160 | tf_op jit(solution)/shard_map/ppermute | solution.py:499
  23.5 6.3 %collective-permute-start.6 = (bf16[288,128]{1,0:T(8,128)(2,1)S(1)}, bf16[288,128]{1,0:T(8,128)(2,1)S(1)}, u32[]{:S(2)}, u32[]{:S(2)}) collective-permute-start(bf16[288,128]{1,0:T(8,128)(2,1)S(1)} %get-tuple-element.58), channel_id=1, source_target_pairs={{0,12},{1,13},{2,14},{3,15},{4,8},{5,9},{6,10},{7,11},{8,4},{9,5},... | collective-permute-start | bytes 221192 | tf_op jit(solution)/shard_map/ppermute | solution.py:541
  26.1 3.7 %collective-permute-start.7 = (bf16[288,128]{1,0:T(8,128)(2,1)S(1)}, bf16[288,128]{1,0:T(8,128)(2,1)S(1)}, u32[]{:S(2)}, u32[]{:S(2)}) collective-permute-start(bf16[288,128]{1,0:T(8,128)(2,1)S(1)} %get-tuple-element.59), channel_id=1, source_target_pairs={{0,0},{1,1},{2,2},{3,3},{4,4},{5,5},{6,6},{7,7},{8,8},{9,9},{10,10... | collective-permute-start | bytes 221192 | tf_op jit(solution)/shard_map/ppermute | solution.py:541
  29.8 2.1 %collective-permute-start.8 = (bf16[288,128]{1,0:T(8,128)(2,1)S(1)}, bf16[288,128]{1,0:T(8,128)(2,1)S(1)}, u32[]{:S(2)}, u32[]{:S(2)}) collective-permute-start(bf16[288,128]{1,0:T(8,128)(2,1)S(1)} %add_convert_fusion.mine_ref), channel_id=1, source_target_pairs={{0,16},{16,0},{1,17},{17,1},{2,18},{18,2},{3,19},{19,3},{4,20},{20... | collective-permute-start | bytes 221192 | tf_op jit(solution)/shard_map/ppermute | solution.py:545

commit v9 on v8

--- a/solution.py
+++ b/solution.py
@@ -129,6 +129,10 @@
 
 PACK = (264, 160, 0, 240, 284)
 PACKED = 288
+
+
+ORDERS = ((1, 3, 2), (2, 1, 3))
+SLOTS = [sum((k + 1) << (4 * bits) for k, bits in enumerate(order)) for order in ORDERS]
 
 
 def final_rows(s, n):
@@ -254,7 +258,7 @@
         def block(s):
             q, z = mine[s] & 3, mine[s] >> 2
             holder = (z ^ (z >> 1)) & 1
-            return holder ^ odd, jnp.where(holder == 0, q, (q >> 1) | ((q & 1) << 1)), z >> 1
+            return holder ^ odd, (jnp.where(holder == 0, SLOTS[0], SLOTS[1]) >> (4 * q)) & 3, z >> 1
 
     def keep(layer, tap, grad):
         channels, cols = grad.shape
@@ -534,7 +538,7 @@
     came = lax.ppermute(payload[1], "dp", swap)
     own_grad, back = features_back()
     held = [added(payload[0, j], came[j]) for j in range(4)]
-    moved = [lax.ppermute(held[j], ("dp", "seq"), mixed(j, (j >> 1) | ((j & 1) << 1))) for j in (1, 3, 2)]
+    moved = [lax.ppermute(held[1 + k], ("dp", "seq"), mixed(*pair)) for k, pair in enumerate(zip(*ORDERS))]
     held = [added(held[0][i], *(part[i] for part in moved)) for i in range(2)]
     held, back, own_grad = lax.optimization_barrier((held, back, own_grad))
     held = added(

time: 32.8 us -> 32.4 us (0.988)
  starting transfers between devices: 12 us -> 11.2 us
  waiting for transfers between devices: 11.7 us -> 12.1 us
    ppermute x1, starting transfers between devices: 1.19 us -> 0.32 us  [shards(): other = lax.ppermute(held, 'dp', swap)]
    ppermute x1, waiting for transfers between devices: 2.28 us -> 2.61 us  [shards(): lax.ppermute(held[1], ('dp', 'seq'), mixed(12, 8))]
  transfers between devices with their start and end apart: 9 -> 9, of which waited for: 6 -> 7; matrix products, arithmetic and copies ran while one was open for 0% -> 0% of each run, Pallas kernels for 11% -> 11%
where the time goes in v9:
time: 32.4 us; the launch traced here: 32.1 us
  waiting for transfers between devices  12.1 us (37%)
  starting transfers between devices  11.2 us (35%)
  Pallas kernels  7.81 us (24%)
  between operations  0.71 us (2%)
    ppermute x3, starting transfers between devices, shards(): lax.ppermute(held[1 + k], ('dp', 'seq'), mixed(*pair))  5.41 us
    ppermute x3, waiting for transfers between devices, shards(): lax.ppermute(held[1 + k], ('dp', 'seq'), mixed(*pair))  4.05 us
    pallas_call x1, Pallas kernels, shards(): pl.pallas_call(functools.partial(head_kernel, n, packed), in_specs=[VMEM]...  2.84 us
    ppermute x1, starting transfers between devices, shards(): lax.ppermute(held[1], ('dp', 'seq'), mixed(12, 8))  2.68 us
    ppermute x1, waiting for transfers between devices, shards(): lax.ppermute(held[1], ('dp', 'seq'), mixed(12, 8))  2.61 us
    ppermute x1, waiting for transfers between devices, shards(): edge = lax.ppermute(edge, ('dp', 'seq'), along)  2.4 us
    ppermute x1, waiting for transfers between devices, shards(): came = lax.ppermute(payload[1], 'dp', swap)  1.99 us
    pallas_call x1, Pallas kernels, shards(): pl.pallas_call(functools.partial(project_kernel, len(sources)), in_specs=...  1.97 us
  transfers between devices with their start and end apart: 9, of which 7 were waited for; matrix products, arithmetic and copies ran while one was open for 0% of the time, Pallas kernels for 11%

profile of v9, /device:TPU:0, one launch (start us, length us, event | category | flops | bytes accessed | tf_op | source)
XLA Modules:
  0.0 32.1 jit_solution(13928528596647125329)
XLA Ops:
  0.6 0.8 %edge.1 = bf16[32,512]{1,0:T(8,128)(2,1)S(1)} custom-call(bf16[128,512]{1,0:T(8,128)(2,1)} %bitcast.41, f32[1,128]{1,0:T(1,128)} %cot_ref.1), custom_call_target="tpu_custom_call" | custom-call | tf_op jit(solution)/shard_map/edge/pallas_call | solution.py:415
  1.4 0.5 %collective-permute-start = (bf16[32,512]{1,0:T(8,128)(2,1)S(1)}, bf16[32,512]{1,0:T(8,128)(2,1)S(1)}, u32[]{:S(2)}, u32[]{:S(2)}) collective-permute-start(bf16[32,512]{1,0:T(8,128)(2,1)S(1)} %edge.1), channel_id=1, source_target_pairs={{0,16},{1,0},{2,1},{3,2},{4,3},{5,4},{6,5},{7,6},{8,7},{9,8},{10,9... | collective-permute-start | bytes 98312 | tf_op jit(solution)/shard_map/ppermute | solution.py:423
  1.9 2.0 %project.1 = (bf16[128,512]{1,0:T(8,128)(2,1)S(1)}, bf16[512,768]{1,0:T(8,128)(2,1)S(1)}, bf16[64,768]{1,0:T(8,128)(2,1)S(1)}, f32[1,128]{1,0:T(1,128)S(1)}, bf1...) custom-call(bf16[768]{0:T(1024)(128)(2,1)} %final_ref.1, ...), custom_call_target="tpu_custom_call" | custom-call | flops 113246208 | bytes 786432 | tf_op jit(solution)/shard_map/project/pallas_call | solution.py:434
  3.9 2.4 %collective-permute-done.edge_ref = bf16[32,512]{1,0:T(8,128)(2,1)S(1)} collective-permute-done((bf16[32,512]{1,0:T(8,128)(2,1)S(1)}, bf16[32,512]{1,0:T(8,128)(2,1)S(1)}, u32[]{:S(2)}, u32[]{:S(2)}) %collective-permute-start) | collective-permute-done | bytes 32800 | tf_op jit(solution)/shard_map/ppermute | solution.py:423
  6.3 2.8 %head.1 = (f32[1,128]{1,0:T(1,128)S(1)}, f32[1,128]{1,0:T(1,128)S(1)}, bf16[160,64]{1,0:T(8,128)(2,1)S(1)}, bf16[32,768]{1,0:T(8,128)(2,1)S(1)}, bf16[2,4,2,288,128]{4,3,2,1,0:T(8,128)(2,1)S(1)}) custom-call(f32[128,64]{1,0:T(8,128)S(1)} %get-tuple-element.40.squeezed_ref, f32[8,64]{1,0:T(8,128)S(1)} %get-tuple-element.41.sums_ref, ...), custom_call_target="tpu_custom_call" | custom-call | flops 1000000000 | bytes 4000000 | tf_op jit(solution)/shard_map/head/pallas_call | solution.py:464
  9.2 0.1 collective-permute-start.1
  9.3 2.0 %collective-permute-done.1 = bf16[4,2,288,128]{3,2,1,0:T(8,128)(2,1)S(1)} collective-permute-done((bf16[4,2,288,128]{3,2,1,0:T(8,128)(2,1)S(1)}, bf16[4,2,288,128]{3,2,1,0:T(8,128)(2,1)S(1)}, u32[]{:S(2)}, u32[]{:S(2)}) %collective-permute-start.1) | collective-permute-done | bytes 589856 | tf_op jit(solution)/shard_map/ppermute | solution.py:538
  11.3 0.2 fusion.3
  11.5 2.1 %collective-permute-start.4 = (bf16[2,288,128]{2,1,0:T(8,128)(2,1)S(1)}, bf16[2,288,128]{2,1,0:T(8,128)(2,1)S(1)}, u32[]{:S(2)}, u32[]{:S(2)}) collective-permute-start(bf16[2,288,128]{2,1,0:T(8,128)(2,1)S(1)} %get-tuple-element.74), channel_id=1, source_target_pairs={{0,2},{1,3},{2,0},{3,1},{4,6},{5,7},{6,4},{7,5},{8,10},{9,11},{10,... | collective-permute-start | bytes 442376 | tf_op jit(solution)/shard_map/ppermute | solution.py:541
  13.6 2.8 %collective-permute-start.3 = (bf16[2,288,128]{2,1,0:T(8,128)(2,1)S(1)}, bf16[2,288,128]{2,1,0:T(8,128)(2,1)S(1)}, u32[]{:S(2)}, u32[]{:S(2)}) collective-permute-start(bf16[2,288,128]{2,1,0:T(8,128)(2,1)S(1)} %get-tuple-element.75), channel_id=1, source_target_pairs={{0,3},{1,2},{2,1},{3,0},{4,7},{5,6},{6,5},{7,4},{8,11},{9,10},{10,... | collective-permute-start | bytes 442376 | tf_op jit(solution)/shard_map/ppermute | solution.py:541
  16.4 0.5 %collective-permute-start.2 = (bf16[2,288,128]{2,1,0:T(8,128)(2,1)S(1)}, bf16[2,288,128]{2,1,0:T(8,128)(2,1)S(1)}, u32[]{:S(2)}, u32[]{:S(2)}) collective-permute-start(bf16[2,288,128]{2,1,0:T(8,128)(2,1)S(1)} %get-tuple-element.76), channel_id=1, source_target_pairs={{0,1},{1,0},{2,3},{3,2},{4,5},{5,4},{6,7},{7,6},{8,9},{9,8},{10,11... | collective-permute-start | bytes 442376 | tf_op jit(solution)/shard_map/ppermute | solution.py:541
  16.9 0.8 %feature.1 = (f32[128,512]{1,0:T(8,128)S(1)}, bf16[16,512]{1,0:T(8,128)(2,1)S(1)}) custom-call(bf16[128,512]{1,0:T(8,128)(2,1)S(1)} %get-tuple-element.51.rows_ref, bf16[32,512]{1,0:T(8,128)(2,1)S(1)} %collective-permute-done.edge_ref, bf16[128,768]{1,0:T(8,128)(2,1)S(1)} %get-tuple-element.52.projected_ref, ...), custom_call_target="tpu_custom_call" | custom-call | flops 113246208 | bytes 786432 | tf_op jit(solution)/shard_map/feature/pallas_call | solution.py:494
  17.7 1.6 %collective-permute-start.5 = (bf16[16,512]{1,0:T(8,128)(2,1)S(1)}, bf16[16,512]{1,0:T(8,128)(2,1)S(1)}, u32[]{:S(2)}, u32[]{:S(2)}) collective-permute-start(bf16[16,512]{1,0:T(8,128)(2,1)S(1)} %get-tuple-element.56), channel_id=1, source_target_pairs={{0,1},{1,2},{2,3},{3,4},{4,5},{5,6},{6,7},{7,8},{8,9},{9,10},{10,1... | collective-permute-start | bytes 49160 | tf_op jit(solution)/shard_map/ppermute | solution.py:503
  19.3 0.4 %collective-permute-done.4 = bf16[2,288,128]{2,1,0:T(8,128)(2,1)S(1)} collective-permute-done((bf16[2,288,128]{2,1,0:T(8,128)(2,1)S(1)}, bf16[2,288,128]{2,1,0:T(8,128)(2,1)S(1)}, u32[]{:S(2)}, u32[]{:S(2)}) %collective-permute-start.4) | collective-permute-done | bytes 147488 | tf_op jit(solution)/shard_map/ppermute | solution.py:541
  19.7 1.5 %collective-permute-done.3 = bf16[2,288,128]{2,1,0:T(8,128)(2,1)S(1)} collective-permute-done((bf16[2,288,128]{2,1,0:T(8,128)(2,1)S(1)}, bf16[2,288,128]{2,1,0:T(8,128)(2,1)S(1)}, u32[]{:S(2)}, u32[]{:S(2)}) %collective-permute-start.3) | collective-permute-done | bytes 147488 | tf_op jit(solution)/shard_map/ppermute | solution.py:541
  21.1 2.2 %collective-permute-done.2 = bf16[2,288,128]{2,1,0:T(8,128)(2,1)S(1)} collective-permute-done((bf16[2,288,128]{2,1,0:T(8,128)(2,1)S(1)}, bf16[2,288,128]{2,1,0:T(8,128)(2,1)S(1)}, u32[]{:S(2)}, u32[]{:S(2)}) %collective-permute-start.2) | collective-permute-done | bytes 147488 | tf_op jit(solution)/shard_map/ppermute | solution.py:541
  23.3 0.1 fusion.5
  23.4 0.0 collective-permute-done.5.back_ref
  23.4 2.7 %collective-permute-start.6 = (bf16[288,128]{1,0:T(8,128)(2,1)S(1)}, bf16[288,128]{1,0:T(8,128)(2,1)S(1)}, u32[]{:S(2)}, u32[]{:S(2)}) collective-permute-start(bf16[288,128]{1,0:T(8,128)(2,1)S(1)} %get-tuple-element.58), channel_id=1, source_target_pairs={{0,12},{1,13},{2,14},{3,15},{4,8},{5,9},{6,10},{7,11},{8,4},{9,5},... | collective-permute-start | bytes 221192 | tf_op jit(solution)/shard_map/ppermute | solution.py:545
  26.1 0.7 %collective-permute-start.7 = (bf16[288,128]{1,0:T(8,128)(2,1)S(1)}, bf16[288,128]{1,0:T(8,128)(2,1)S(1)}, u32[]{:S(2)}, u32[]{:S(2)}) collective-permute-start(bf16[288,128]{1,0:T(8,128)(2,1)S(1)} %get-tuple-element.59), channel_id=1, source_target_pairs={{0,0},{1,1},{2,2},{3,3},{4,4},{5,5},{6,6},{7,7},{8,8},{9,9},{10,10... | collective-permute-start | bytes 221192 | tf_op jit(solution)/shard_map/ppermute | solution.py:545
  26.8 0.7 %assemble.1 = (f32[128,512]{1,0:T(8,128)}, f32[1,128]{1,0:T(1,128)}) custom-call(f32[128,512]{1,0:T(8,128)S(1)} %get-tuple-element.60.own_ref, f32[1,128]{1,0:T(1,128)S(1)} %get-tuple-element.61.scores_ref, bf16[16,512]{1,0:T(8,128)(2,1)S(1)} %collective-permute-done.5.back_ref), custom_call_target="tpu_custom_call" | custom-call | flops 65536 | bytes 524288 | tf_op jit(solution)/shard_map/assemble/pallas_call | solution.py:507
  27.5 2.6 %collective-permute-done.6 = bf16[288,128]{1,0:T(8,128)(2,1)S(1)} collective-permute-done((bf16[288,128]{1,0:T(8,128)(2,1)S(1)}, bf16[288,128]{1,0:T(8,128)(2,1)S(1)}, u32[]{:S(2)}, u32[]{:S(2)}) %collective-permute-start.6) | collective-permute-done | bytes 73760 | tf_op jit(solution)/shard_map/ppermute | solution.py:545
  30.1 0.0 collective-permute-done.7
  30.1 0.3 collective-permute-start.8
  30.5 1.0 %collective-permute-done.8.other_ref = bf16[288,128]{1,0:T(8,128)(2,1)S(1)} collective-permute-done((bf16[288,128]{1,0:T(8,128)(2,1)S(1)}, bf16[288,128]{1,0:T(8,128)(2,1)S(1)}, u32[]{:S(2)}, u32[]{:S(2)}) %collective-permute-start.8) | collective-permute-done | bytes 73760 | tf_op jit(solution)/shard_map/ppermute | solution.py:549
  31.5 0.7 %unpack.1 = (f32[4,768]{1,0:T(4,128)}, f32[20,128]{1,0:T(8,128)}, f32[40,256]{1,0:T(8,128)}, f32[80,256]{1,0:T(8,128)}, f32[1,48]{1,0:T(1,128)}) custom-call(bf16[288,128]{1,0:T(8,128)(2,1)S(1)} %add_convert_fusion.mine_ref, bf16[288,128]{1,0:T(8,128)(2,1)S(1)} %collective-permute-done.8.other_ref), custom_call_target="tpu_custom_call" | custom-call | tf_op jit(solution)/shard_map/unpack/pallas_call | solution.py:557
  (2 shorter events, 0.1 us)
Async XLA Ops:
  1.4 4.9 %collective-permute-start = (bf16[32,512]{1,0:T(8,128)(2,1)S(1)}, bf16[32,512]{1,0:T(8,128)(2,1)S(1)}, u32[]{:S(2)}, u32[]{:S(2)}) collective-permute-start(bf16[32,512]{1,0:T(8,128)(2,1)S(1)} %edge.1), channel_id=1, source_target_pairs={{0,16},{1,0},{2,1},{3,2},{4,3},{5,4},{6,5},{7,6},{8,7},{9,8},{10,9... | collective-permute-start | bytes 98312 | tf_op jit(solution)/shard_map/ppermute | solution.py:423
  9.2 2.1 %collective-permute-start.1 = (bf16[4,2,288,128]{3,2,1,0:T(8,128)(2,1)S(1)}, bf16[4,2,288,128]{3,2,1,0:T(8,128)(2,1)S(1)}, u32[]{:S(2)}, u32[]{:S(2)}) collective-permute-start(bf16[4,2,288,128]{3,2,1,0:T(8,128)(2,1)S(1)} %slice_bitcast_fusion), channel_id=1, source_target_pairs={{0,16},{16,0},{1,17},{17,1},{2,18},{18,2},{3,19},{19,3},{4,20},{20... | collective-permute-start | bytes 1769480 | tf_op jit(solution)/shard_map/ppermute | solution.py:538
  11.5 8.2 %collective-permute-start.4 = (bf16[2,288,128]{2,1,0:T(8,128)(2,1)S(1)}, bf16[2,288,128]{2,1,0:T(8,128)(2,1)S(1)}, u32[]{:S(2)}, u32[]{:S(2)}) collective-permute-start(bf16[2,288,128]{2,1,0:T(8,128)(2,1)S(1)} %get-tuple-element.74), channel_id=1, source_target_pairs={{0,2},{1,3},{2,0},{3,1},{4,6},{5,7},{6,4},{7,5},{8,10},{9,11},{10,... | collective-permute-start | bytes 442376 | tf_op jit(solution)/shard_map/ppermute | solution.py:541
  13.6 7.6 %collective-permute-start.3 = (bf16[2,288,128]{2,1,0:T(8,128)(2,1)S(1)}, bf16[2,288,128]{2,1,0:T(8,128)(2,1)S(1)}, u32[]{:S(2)}, u32[]{:S(2)}) collective-permute-start(bf16[2,288,128]{2,1,0:T(8,128)(2,1)S(1)} %get-tuple-element.75), channel_id=1, source_target_pairs={{0,3},{1,2},{2,1},{3,0},{4,7},{5,6},{6,5},{7,4},{8,11},{9,10},{10,... | collective-permute-start | bytes 442376 | tf_op jit(solution)/shard_map/ppermute | solution.py:541
  16.4 6.9 %collective-permute-start.2 = (bf16[2,288,128]{2,1,0:T(8,128)(2,1)S(1)}, bf16[2,288,128]{2,1,0:T(8,128)(2,1)S(1)}, u32[]{:S(2)}, u32[]{:S(2)}) collective-permute-start(bf16[2,288,128]{2,1,0:T(8,128)(2,1)S(1)} %get-tuple-element.76), channel_id=1, source_target_pairs={{0,1},{1,0},{2,3},{3,2},{4,5},{5,4},{6,7},{7,6},{8,9},{9,8},{10,11... | collective-permute-start | bytes 442376 | tf_op jit(solution)/shard_map/ppermute | solution.py:541
  17.7 5.7 %collective-permute-start.5 = (bf16[16,512]{1,0:T(8,128)(2,1)S(1)}, bf16[16,512]{1,0:T(8,128)(2,1)S(1)}, u32[]{:S(2)}, u32[]{:S(2)}) collective-permute-start(bf16[16,512]{1,0:T(8,128)(2,1)S(1)} %get-tuple-element.56), channel_id=1, source_target_pairs={{0,1},{1,2},{2,3},{3,4},{4,5},{5,6},{6,7},{7,8},{8,9},{9,10},{10,1... | collective-permute-start | bytes 49160 | tf_op jit(solution)/shard_map/ppermute | solution.py:503
  23.4 6.7 %collective-permute-start.6 = (bf16[288,128]{1,0:T(8,128)(2,1)S(1)}, bf16[288,128]{1,0:T(8,128)(2,1)S(1)}, u32[]{:S(2)}, u32[]{:S(2)}) collective-permute-start(bf16[288,128]{1,0:T(8,128)(2,1)S(1)} %get-tuple-element.58), channel_id=1, source_target_pairs={{0,12},{1,13},{2,14},{3,15},{4,8},{5,9},{6,10},{7,11},{8,4},{9,5},... | collective-permute-start | bytes 221192 | tf_op jit(solution)/shard_map/ppermute | solution.py:545
  26.1 4.0 %collective-permute-start.7 = (bf16[288,128]{1,0:T(8,128)(2,1)S(1)}, bf16[288,128]{1,0:T(8,128)(2,1)S(1)}, u32[]{:S(2)}, u32[]{:S(2)}) collective-permute-start(bf16[288,128]{1,0:T(8,128)(2,1)S(1)} %get-tuple-element.59), channel_id=1, source_target_pairs={{0,0},{1,1},{2,2},{3,3},{4,4},{5,5},{6,6},{7,7},{8,8},{9,9},{10,10... | collective-permute-start | bytes 221192 | tf_op jit(solution)/shard_map/ppermute | solution.py:545
  30.1 1.3 %collective-permute-start.8 = (bf16[288,128]{1,0:T(8,128)(2,1)S(1)}, bf16[288,128]{1,0:T(8,128)(2,1)S(1)}, u32[]{:S(2)}, u32[]{:S(2)}) collective-permute-start(bf16[288,128]{1,0:T(8,128)(2,1)S(1)} %add_convert_fusion.mine_ref), channel_id=1, source_target_pairs={{0,16},{16,0},{1,17},{17,1},{2,18},{18,2},{3,19},{19,3},{4,20},{20... | collective-permute-start | bytes 221192 | tf_op jit(solution)/shard_map/ppermute | solution.py:549

commit v10 on v9

--- a/solution.py
+++ b/solution.py
@@ -285,8 +285,10 @@
         width = ref.shape[0] // HK
         whole = jnp.concatenate([ref[k * width : (k + 1) * width, :] for k in range(HK)], axis=1)
         upstream = dot(jnp.concatenate(pieces, axis=1), whole, NT)
-        for k, piece in enumerate(pieces):
-            keep(layer, k, dot(rows, piece))
+        grad = dot(rows, jnp.concatenate(pieces, axis=1))
+        cols = grad.shape[1] // HK
+        for k in range(HK):
+            keep(layer, k, grad[:, k * cols : (k + 1) * cols])
     delta = mask(upstream * slopes[0], inside)
     delta_ref[...] = delta.astype(BF16)
     hidden = jnp.concatenate([hidden_ref[...], edge_hidden], axis=0)
@@ -537,10 +539,11 @@
     (payload,) = grads
     came = lax.ppermute(payload[1], "dp", swap)
     own_grad, back = features_back()
+    came, own_grad = lax.optimization_barrier((came, own_grad))
     held = [added(payload[0, j], came[j]) for j in range(4)]
     moved = [lax.ppermute(held[1 + k], ("dp", "seq"), mixed(*pair)) for k, pair in enumerate(zip(*ORDERS))]
     held = [added(held[0][i], *(part[i] for part in moved)) for i in range(2)]
-    held, back, own_grad = lax.optimization_barrier((held, back, own_grad))
+    held, back = lax.optimization_barrier((held, back))
     held = added(
         lax.ppermute(held[1], ("dp", "seq"), mixed(12, 8)), lax.ppermute(held[0], ("dp", "seq"), mixed(0, 4))
     )

time: 32.4 us -> 32.4 us (level)
    ppermute x3, waiting for transfers between devices: 4.05 us -> 4.91 us  [shards(): lax.ppermute(held[1 + k], ('dp', 'seq'), mixed(*pair))]
    ppermute x1, waiting for transfers between devices: 1.99 us -> 1.18 us  [shards(): came = lax.ppermute(payload[1], 'dp', swap)]
where the time goes in v10:
time: 32.4 us; the launch traced here: 32.1 us
  waiting for transfers between devices  11.9 us (37%)
  starting transfers between devices  11.3 us (35%)
  Pallas kernels  7.81 us (24%)
  between operations  0.71 us (2%)
    ppermute x3, starting transfers between devices, shards(): lax.ppermute(held[1 + k], ('dp', 'seq'), mixed(*pair))  5.41 us
    ppermute x3, waiting for transfers between devices, shards(): lax.ppermute(held[1 + k], ('dp', 'seq'), mixed(*pair))  4.91 us
    pallas_call x1, Pallas kernels, shards(): pl.pallas_call(functools.partial(head_kernel, n, packed), in_specs=[VMEM]...  2.84 us
    ppermute x1, starting transfers between devices, shards(): lax.ppermute(held[1], ('dp', 'seq'), mixed(12, 8))  2.71 us
    ppermute x1, waiting for transfers between devices, shards(): lax.ppermute(held[1], ('dp', 'seq'), mixed(12, 8))  2.51 us
    ppermute x1, waiting for transfers between devices, shards(): edge = lax.ppermute(edge, ('dp', 'seq'), along)  2.4 us
    pallas_call x1, Pallas kernels, shards(): pl.pallas_call(functools.partial(project_kernel, len(sources)), in_specs=...  1.97 us
    ppermute x1, starting transfers between devices, features_back(): back = lax.ppermute(back, ('dp', 'seq'), returning)  1.54 us
  transfers between devices with their start and end apart: 9, of which 7 were waited for; matrix products, arithmetic and copies ran while one was open for 0% of the time, Pallas kernels for 11%

profile of v10, /device:TPU:0, one launch (start us, length us, event | category | flops | bytes accessed | tf_op | source)
XLA Modules:
  0.0 32.1 jit_solution(10136056622991901616)
XLA Ops:
  0.6 0.8 %edge.1 = bf16[32,512]{1,0:T(8,128)(2,1)S(1)} custom-call(bf16[128,512]{1,0:T(8,128)(2,1)} %bitcast.33, f32[1,128]{1,0:T(1,128)} %cot_ref.1), custom_call_target="tpu_custom_call" | custom-call | tf_op jit(solution)/shard_map/edge/pallas_call | solution.py:417
  1.4 0.5 %collective-permute-start = (bf16[32,512]{1,0:T(8,128)(2,1)S(1)}, bf16[32,512]{1,0:T(8,128)(2,1)S(1)}, u32[]{:S(2)}, u32[]{:S(2)}) collective-permute-start(bf16[32,512]{1,0:T(8,128)(2,1)S(1)} %edge.1), channel_id=1, source_target_pairs={{0,16},{1,0},{2,1},{3,2},{4,3},{5,4},{6,5},{7,6},{8,7},{9,8},{10,9... | collective-permute-start | bytes 98312 | tf_op jit(solution)/shard_map/ppermute | solution.py:425
  1.9 2.0 %project.1 = (bf16[128,512]{1,0:T(8,128)(2,1)S(1)}, bf16[512,768]{1,0:T(8,128)(2,1)S(1)}, bf16[64,768]{1,0:T(8,128)(2,1)S(1)}, f32[1,128]{1,0:T(1,128)S(1)}, bf1...) custom-call(bf16[768]{0:T(1024)(128)(2,1)} %final_ref.1, ...), custom_call_target="tpu_custom_call" | custom-call | flops 113246208 | bytes 786432 | tf_op jit(solution)/shard_map/project/pallas_call | solution.py:436
  3.9 2.4 %collective-permute-done.edge_ref = bf16[32,512]{1,0:T(8,128)(2,1)S(1)} collective-permute-done((bf16[32,512]{1,0:T(8,128)(2,1)S(1)}, bf16[32,512]{1,0:T(8,128)(2,1)S(1)}, u32[]{:S(2)}, u32[]{:S(2)}) %collective-permute-start) | collective-permute-done | bytes 32800 | tf_op jit(solution)/shard_map/ppermute | solution.py:425
  6.3 2.8 %head.1 = (f32[1,128]{1,0:T(1,128)S(1)}, f32[1,128]{1,0:T(1,128)S(1)}, bf16[160,64]{1,0:T(8,128)(2,1)S(1)}, bf16[32,768]{1,0:T(8,128)(2,1)S(1)}, bf16[2,4,2,288,128]{4,3,2,1,0:T(8,128)(2,1)S(1)}) custom-call(f32[128,64]{1,0:T(8,128)S(1)} %get-tuple-element.41.squeezed_ref, f32[8,64]{1,0:T(8,128)S(1)} %get-tuple-element.42.sums_ref, ...), custom_call_target="tpu_custom_call" | custom-call | flops 1000000000 | bytes 4000000 | tf_op jit(solution)/shard_map/head/pallas_call | solution.py:466
  9.2 0.1 collective-permute-start.1
  9.3 0.8 %feature.1 = (f32[128,512]{1,0:T(8,128)S(1)}, bf16[16,512]{1,0:T(8,128)(2,1)S(1)}) custom-call(bf16[128,512]{1,0:T(8,128)(2,1)S(1)} %get-tuple-element.52.rows_ref, bf16[32,512]{1,0:T(8,128)(2,1)S(1)} %collective-permute-done.edge_ref, bf16[128,768]{1,0:T(8,128)(2,1)S(1)} %get-tuple-element.53.projected_ref, ...), custom_call_target="tpu_custom_call" | custom-call | flops 113246208 | bytes 786432 | tf_op jit(solution)/shard_map/feature/pallas_call | solution.py:496
  10.1 1.2 %collective-permute-done.1 = bf16[4,2,288,128]{3,2,1,0:T(8,128)(2,1)S(1)} collective-permute-done((bf16[4,2,288,128]{3,2,1,0:T(8,128)(2,1)S(1)}, bf16[4,2,288,128]{3,2,1,0:T(8,128)(2,1)S(1)}, u32[]{:S(2)}, u32[]{:S(2)}) %collective-permute-start.1) | collective-permute-done | bytes 589856 | tf_op jit(solution)/shard_map/ppermute | solution.py:540
  11.3 0.2 fusion.3
  11.4 2.1 %collective-permute-start.4 = (bf16[2,288,128]{2,1,0:T(8,128)(2,1)S(1)}, bf16[2,288,128]{2,1,0:T(8,128)(2,1)S(1)}, u32[]{:S(2)}, u32[]{:S(2)}) collective-permute-start(bf16[2,288,128]{2,1,0:T(8,128)(2,1)S(1)} %get-tuple-element.76), channel_id=1, source_target_pairs={{0,2},{1,3},{2,0},{3,1},{4,6},{5,7},{6,4},{7,5},{8,10},{9,11},{10,... | collective-permute-start | bytes 442376 | tf_op jit(solution)/shard_map/ppermute | solution.py:544
  13.6 2.8 %collective-permute-start.3 = (bf16[2,288,128]{2,1,0:T(8,128)(2,1)S(1)}, bf16[2,288,128]{2,1,0:T(8,128)(2,1)S(1)}, u32[]{:S(2)}, u32[]{:S(2)}) collective-permute-start(bf16[2,288,128]{2,1,0:T(8,128)(2,1)S(1)} %get-tuple-element.77), channel_id=1, source_target_pairs={{0,3},{1,2},{2,1},{3,0},{4,7},{5,6},{6,5},{7,4},{8,11},{9,10},{10,... | collective-permute-start | bytes 442376 | tf_op jit(solution)/shard_map/ppermute | solution.py:544
  16.4 0.5 %collective-permute-start.2 = (bf16[2,288,128]{2,1,0:T(8,128)(2,1)S(1)}, bf16[2,288,128]{2,1,0:T(8,128)(2,1)S(1)}, u32[]{:S(2)}, u32[]{:S(2)}) collective-permute-start(bf16[2,288,128]{2,1,0:T(8,128)(2,1)S(1)} %get-tuple-element.78), channel_id=1, source_target_pairs={{0,1},{1,0},{2,3},{3,2},{4,5},{5,4},{6,7},{7,6},{8,9},{9,8},{10,11... | collective-permute-start | bytes 442376 | tf_op jit(solution)/shard_map/ppermute | solution.py:544
  16.9 1.5 %collective-permute-start.5 = (bf16[16,512]{1,0:T(8,128)(2,1)S(1)}, bf16[16,512]{1,0:T(8,128)(2,1)S(1)}, u32[]{:S(2)}, u32[]{:S(2)}) collective-permute-start(bf16[16,512]{1,0:T(8,128)(2,1)S(1)} %get-tuple-element.59), channel_id=1, source_target_pairs={{0,1},{1,2},{2,3},{3,4},{4,5},{5,6},{6,7},{7,8},{8,9},{9,10},{10,1... | collective-permute-start | bytes 49160 | tf_op jit(solution)/shard_map/ppermute | solution.py:505
  18.4 1.3 %collective-permute-done.4 = bf16[2,288,128]{2,1,0:T(8,128)(2,1)S(1)} collective-permute-done((bf16[2,288,128]{2,1,0:T(8,128)(2,1)S(1)}, bf16[2,288,128]{2,1,0:T(8,128)(2,1)S(1)}, u32[]{:S(2)}, u32[]{:S(2)}) %collective-permute-start.4) | collective-permute-done | bytes 147488 | tf_op jit(solution)/shard_map/ppermute | solution.py:544
  19.7 1.5 %collective-permute-done.3 = bf16[2,288,128]{2,1,0:T(8,128)(2,1)S(1)} collective-permute-done((bf16[2,288,128]{2,1,0:T(8,128)(2,1)S(1)}, bf16[2,288,128]{2,1,0:T(8,128)(2,1)S(1)}, u32[]{:S(2)}, u32[]{:S(2)}) %collective-permute-start.3) | collective-permute-done | bytes 147488 | tf_op jit(solution)/shard_map/ppermute | solution.py:544
  21.1 2.2 %collective-permute-done.2 = bf16[2,288,128]{2,1,0:T(8,128)(2,1)S(1)} collective-permute-done((bf16[2,288,128]{2,1,0:T(8,128)(2,1)S(1)}, bf16[2,288,128]{2,1,0:T(8,128)(2,1)S(1)}, u32[]{:S(2)}, u32[]{:S(2)}) %collective-permute-start.2) | collective-permute-done | bytes 147488 | tf_op jit(solution)/shard_map/ppermute | solution.py:544
  23.3 0.1 fusion.5
  23.4 0.0 collective-permute-done.5.back_ref
  23.4 2.7 %collective-permute-start.6 = (bf16[288,128]{1,0:T(8,128)(2,1)S(1)}, bf16[288,128]{1,0:T(8,128)(2,1)S(1)}, u32[]{:S(2)}, u32[]{:S(2)}) collective-permute-start(bf16[288,128]{1,0:T(8,128)(2,1)S(1)} %get-tuple-element.60), channel_id=1, source_target_pairs={{0,12},{1,13},{2,14},{3,15},{4,8},{5,9},{6,10},{7,11},{8,4},{9,5},... | collective-permute-start | bytes 221192 | tf_op jit(solution)/shard_map/ppermute | solution.py:548
  26.1 0.7 %collective-permute-start.7 = (bf16[288,128]{1,0:T(8,128)(2,1)S(1)}, bf16[288,128]{1,0:T(8,128)(2,1)S(1)}, u32[]{:S(2)}, u32[]{:S(2)}) collective-permute-start(bf16[288,128]{1,0:T(8,128)(2,1)S(1)} %get-tuple-element.61), channel_id=1, source_target_pairs={{0,0},{1,1},{2,2},{3,3},{4,4},{5,5},{6,6},{7,7},{8,8},{9,9},{10,10... | collective-permute-start | bytes 221192 | tf_op jit(solution)/shard_map/ppermute | solution.py:548
  26.8 0.7 %assemble.1 = (f32[128,512]{1,0:T(8,128)}, f32[1,128]{1,0:T(1,128)}) custom-call(f32[128,512]{1,0:T(8,128)S(1)} %get-tuple-element.62.own_ref, f32[1,128]{1,0:T(1,128)S(1)} %get-tuple-element.63.scores_ref, bf16[16,512]{1,0:T(8,128)(2,1)S(1)} %collective-permute-done.5.back_ref), custom_call_target="tpu_custom_call" | custom-call | flops 65536 | bytes 524288 | tf_op jit(solution)/shard_map/assemble/pallas_call | solution.py:509
  27.5 2.5 %collective-permute-done.6 = bf16[288,128]{1,0:T(8,128)(2,1)S(1)} collective-permute-done((bf16[288,128]{1,0:T(8,128)(2,1)S(1)}, bf16[288,128]{1,0:T(8,128)(2,1)S(1)}, u32[]{:S(2)}, u32[]{:S(2)}) %collective-permute-start.6) | collective-permute-done | bytes 73760 | tf_op jit(solution)/shard_map/ppermute | solution.py:548
  30.0 0.0 collective-permute-done.7
  30.1 0.4 %collective-permute-start.8 = (bf16[288,128]{1,0:T(8,128)(2,1)S(1)}, bf16[288,128]{1,0:T(8,128)(2,1)S(1)}, u32[]{:S(2)}, u32[]{:S(2)}) collective-permute-start(bf16[288,128]{1,0:T(8,128)(2,1)S(1)} %add_convert_fusion.mine_ref), channel_id=1, source_target_pairs={{0,16},{16,0},{1,17},{17,1},{2,18},{18,2},{3,19},{19,3},{4,20},{20... | collective-permute-start | bytes 221192 | tf_op jit(solution)/shard_map/ppermute | solution.py:552
  30.5 0.9 %collective-permute-done.8.other_ref = bf16[288,128]{1,0:T(8,128)(2,1)S(1)} collective-permute-done((bf16[288,128]{1,0:T(8,128)(2,1)S(1)}, bf16[288,128]{1,0:T(8,128)(2,1)S(1)}, u32[]{:S(2)}, u32[]{:S(2)}) %collective-permute-start.8) | collective-permute-done | bytes 73760 | tf_op jit(solution)/shard_map/ppermute | solution.py:552
  31.4 0.7 %unpack.1 = (f32[4,768]{1,0:T(4,128)}, f32[20,128]{1,0:T(8,128)}, f32[40,256]{1,0:T(8,128)}, f32[80,256]{1,0:T(8,128)}, f32[1,48]{1,0:T(1,128)}) custom-call(bf16[288,128]{1,0:T(8,128)(2,1)S(1)} %add_convert_fusion.mine_ref, bf16[288,128]{1,0:T(8,128)(2,1)S(1)} %collective-permute-done.8.other_ref), custom_call_target="tpu_custom_call" | custom-call | tf_op jit(solution)/shard_map/unpack/pallas_call | solution.py:560
  (2 shorter events, 0.1 us)
Async XLA Ops:
  1.4 4.9 %collective-permute-start = (bf16[32,512]{1,0:T(8,128)(2,1)S(1)}, bf16[32,512]{1,0:T(8,128)(2,1)S(1)}, u32[]{:S(2)}, u32[]{:S(2)}) collective-permute-start(bf16[32,512]{1,0:T(8,128)(2,1)S(1)} %edge.1), channel_id=1, source_target_pairs={{0,16},{1,0},{2,1},{3,2},{4,3},{5,4},{6,5},{7,6},{8,7},{9,8},{10,9... | collective-permute-start | bytes 98312 | tf_op jit(solution)/shard_map/ppermute | solution.py:425
  9.2 2.1 %collective-permute-start.1 = (bf16[4,2,288,128]{3,2,1,0:T(8,128)(2,1)S(1)}, bf16[4,2,288,128]{3,2,1,0:T(8,128)(2,1)S(1)}, u32[]{:S(2)}, u32[]{:S(2)}) collective-permute-start(bf16[4,2,288,128]{3,2,1,0:T(8,128)(2,1)S(1)} %slice_bitcast_fusion), channel_id=1, source_target_pairs={{0,16},{16,0},{1,17},{17,1},{2,18},{18,2},{3,19},{19,3},{4,20},{20... | collective-permute-start | bytes 1769480 | tf_op jit(solution)/shard_map/ppermute | solution.py:540
  11.4 8.2 %collective-permute-start.4 = (bf16[2,288,128]{2,1,0:T(8,128)(2,1)S(1)}, bf16[2,288,128]{2,1,0:T(8,128)(2,1)S(1)}, u32[]{:S(2)}, u32[]{:S(2)}) collective-permute-start(bf16[2,288,128]{2,1,0:T(8,128)(2,1)S(1)} %get-tuple-element.76), channel_id=1, source_target_pairs={{0,2},{1,3},{2,0},{3,1},{4,6},{5,7},{6,4},{7,5},{8,10},{9,11},{10,... | collective-permute-start | bytes 442376 | tf_op jit(solution)/shard_map/ppermute | solution.py:544
  13.6 7.6 %collective-permute-start.3 = (bf16[2,288,128]{2,1,0:T(8,128)(2,1)S(1)}, bf16[2,288,128]{2,1,0:T(8,128)(2,1)S(1)}, u32[]{:S(2)}, u32[]{:S(2)}) collective-permute-start(bf16[2,288,128]{2,1,0:T(8,128)(2,1)S(1)} %get-tuple-element.77), channel_id=1, source_target_pairs={{0,3},{1,2},{2,1},{3,0},{4,7},{5,6},{6,5},{7,4},{8,11},{9,10},{10,... | collective-permute-start | bytes 442376 | tf_op jit(solution)/shard_map/ppermute | solution.py:544
  16.4 6.9 %collective-permute-start.2 = (bf16[2,288,128]{2,1,0:T(8,128)(2,1)S(1)}, bf16[2,288,128]{2,1,0:T(8,128)(2,1)S(1)}, u32[]{:S(2)}, u32[]{:S(2)}) collective-permute-start(bf16[2,288,128]{2,1,0:T(8,128)(2,1)S(1)} %get-tuple-element.78), channel_id=1, source_target_pairs={{0,1},{1,0},{2,3},{3,2},{4,5},{5,4},{6,7},{7,6},{8,9},{9,8},{10,11... | collective-permute-start | bytes 442376 | tf_op jit(solution)/shard_map/ppermute | solution.py:544
  16.9 6.5 %collective-permute-start.5 = (bf16[16,512]{1,0:T(8,128)(2,1)S(1)}, bf16[16,512]{1,0:T(8,128)(2,1)S(1)}, u32[]{:S(2)}, u32[]{:S(2)}) collective-permute-start(bf16[16,512]{1,0:T(8,128)(2,1)S(1)} %get-tuple-element.59), channel_id=1, source_target_pairs={{0,1},{1,2},{2,3},{3,4},{4,5},{5,6},{6,7},{7,8},{8,9},{9,10},{10,1... | collective-permute-start | bytes 49160 | tf_op jit(solution)/shard_map/ppermute | solution.py:505
  23.4 6.6 %collective-permute-start.6 = (bf16[288,128]{1,0:T(8,128)(2,1)S(1)}, bf16[288,128]{1,0:T(8,128)(2,1)S(1)}, u32[]{:S(2)}, u32[]{:S(2)}) collective-permute-start(bf16[288,128]{1,0:T(8,128)(2,1)S(1)} %get-tuple-element.60), channel_id=1, source_target_pairs={{0,12},{1,13},{2,14},{3,15},{4,8},{5,9},{6,10},{7,11},{8,4},{9,5},... | collective-permute-start | bytes 221192 | tf_op jit(solution)/shard_map/ppermute | solution.py:548
  26.1 3.9 %collective-permute-start.7 = (bf16[288,128]{1,0:T(8,128)(2,1)S(1)}, bf16[288,128]{1,0:T(8,128)(2,1)S(1)}, u32[]{:S(2)}, u32[]{:S(2)}) collective-permute-start(bf16[288,128]{1,0:T(8,128)(2,1)S(1)} %get-tuple-element.61), channel_id=1, source_target_pairs={{0,0},{1,1},{2,2},{3,3},{4,4},{5,5},{6,6},{7,7},{8,8},{9,9},{10,10... | collective-permute-start | bytes 221192 | tf_op jit(solution)/shard_map/ppermute | solution.py:548
  30.1 1.3 %collective-permute-start.8 = (bf16[288,128]{1,0:T(8,128)(2,1)S(1)}, bf16[288,128]{1,0:T(8,128)(2,1)S(1)}, u32[]{:S(2)}, u32[]{:S(2)}) collective-permute-start(bf16[288,128]{1,0:T(8,128)(2,1)S(1)} %add_convert_fusion.mine_ref), channel_id=1, source_target_pairs={{0,16},{16,0},{1,17},{17,1},{2,18},{18,2},{3,19},{19,3},{4,20},{20... | collective-permute-start | bytes 221192 | tf_op jit(solution)/shard_map/ppermute | solution.py:552
